TPU v7x, 32 devices: a whole 2x2x4 slice. The times are simulated.
32 devices in a mesh: grp: 1, dev: 16 (over z, y, core), section: 2 (over x), tp: 1.
Axes of the slice: x: 2, y: 2, z: 4, core: 2. Of those that a mesh axis runs over, the one named last changes fastest.
Arguments:
- prompt_pages: bfloat16 [32, 32, 16, 576], P(('grp', 'dev', 'section', 'tp')), may hold values from -6 to 6
- send_page: int32 [32, 32], P(('grp', 'dev', 'section', 'tp')), may hold values from -1 to 31, as said below
- page_table: int32 [32, 2, 16], P(('grp', 'dev', 'section', 'tp')), may hold values from -1 to 31, as said below
- context_len: int32 [32, 2], P(('grp', 'dev', 'section', 'tp')), may hold values from 1 to 256, as said below
- new_latent: bfloat16 [32, 2, 4, 576], P(('grp', 'dev', 'section', 'tp')), may hold values from -8 to 8
- queries: bfloat16 [32, 2, 4, 64, 576], P(('grp', 'dev', 'section', 'tp')), may hold values from -120 to 120
- moe_rows: bfloat16 [32, 4, 3584], P(('grp', 'dev', 'section', 'tp')), may hold values from -6 to 6
- routing: int32 [32, 4, 8], P(('grp', 'dev', 'section', 'tp')), may hold values from 0 to 15, all different within a row; in each aligned block of 4 rows (0 to 3, 4 to 7, ..., all dimensions but the last counted through in order) at most 3 rows name the same one
- gate_weights: float32 [32, 4, 8], P(('grp', 'dev', 'section', 'tp')), may hold values from 0.05 to 0.5
- expert_gate: bfloat16 [16, 3584, 1024], P('dev', None, ('section', 'tp')), may hold values from -0.09375 to 0.09375
- expert_up: bfloat16 [16, 3584, 1024], P('dev', None, ('section', 'tp')), may hold values from -0.09375 to 0.09375
- expert_down: bfloat16 [16, 1024, 3584], P('dev', ('section', 'tp')), may hold values from -0.1875 to 0.1875
Outputs:
- attended: bfloat16 [32, 2, 4, 64, 512], P(('grp', 'dev', 'section', 'tp'))
- expert_out: bfloat16 [32, 4, 3584], P(('grp', 'dev', 'section', 'tp'))
Inputs may be any that keep to these rules, and one draw needn't show every extreme that they name: context_len of some request of every rank is exactly 256. `page_table`: of a rank's entries, those with p < ceil(context_len / 16) are distinct slots, all others -1. `send_page`: an outgoing slot holds a page exactly when the receiving rank's page_table names it; the pages of one rank named are distinct. `routing`: no rank names one expert in more than 3 of its assignments.
All inputs are finite; a program needn't handle non-finite values.
Results may differ from a plain program's by a relative error of at most 0.02.
Values may be sent and summed in bfloat16 or wider, within the bound.
No kernel may reach another device: no remote copies, remote signals or barrier semaphores. Data moves between devices by JAX's collectives and lax.ppermute only.
A program may use at most 64 MiB of HBM per device.

v0:
```python
import jax
import jax.numpy as jnp
from jax import lax
from jax.sharding import PartitionSpec as P

VDIM = 512


SCALE = 192.0 ** (-0.5)


def attend(queries, new_latent, cache, lengths):
    steps = queries.shape[1]
    ctx = cache.shape[1]
    keys = jnp.concatenate([cache, new_latent], axis=1)
    scores = jnp.einsum("rshl,rkl->rshk", queries, keys, preferred_element_type=jnp.float32) * SCALE
    position = jnp.arange(ctx + steps)
    step_index = jnp.arange(steps)
    in_cache = position[None, :] < lengths[:, None]
    in_new = (position[None, :] >= ctx) & (position[None, :] - ctx <= step_index[:, None])
    allowed = in_cache[:, None, :] | in_new[None, :, :]
    scores = jnp.where(allowed[:, :, None, :], scores, -jnp.inf)
    top = jnp.max(scores, axis=-1, keepdims=True)
    weights = jnp.exp(scores - top)
    weights = (weights / jnp.sum(weights, axis=-1, keepdims=True)).astype(jnp.bfloat16)
    values = keys[:, :, :VDIM]
    return jnp.einsum("rshk,rkv->rshv", weights, values, preferred_element_type=jnp.float32).astype(
        jnp.bfloat16
    )


def partial_answer(block, w_gate, w_up, w_down):
    gate = jnp.einsum("nocd,odh->noch", block, w_gate, preferred_element_type=jnp.float32)
    up = jnp.einsum("nocd,odh->noch", block, w_up, preferred_element_type=jnp.float32)
    hidden = (jax.nn.silu(gate) * up).astype(jnp.bfloat16)
    partial_value = jnp.einsum("noch,ohd->nocd", hidden, w_down, preferred_element_type=jnp.float32)
    return partial_value.astype(jnp.bfloat16).astype(jnp.float32)


def body(
    prompt_pages,
    send_page,
    page_table,
    context_len,
    new_latent,
    queries,
    moe_rows,
    routing,
    gate_weights,
    expert_gate,
    expert_up,
    expert_down,
):
    peers = lax.axis_size("dev")
    pages = prompt_pages[0]
    outgoing_slots = send_page[0]
    page_len, width_lat = (pages.shape[1], pages.shape[2])
    capp = outgoing_slots.shape[0] // peers
    picked_pages = pages[jnp.maximum(outgoing_slots, 0)]
    picked_pages = jnp.where(
        (outgoing_slots >= 0)[:, None, None], picked_pages, jnp.zeros_like(picked_pages)
    )
    arrived = lax.all_to_all(
        picked_pages.reshape(peers, capp, page_len, width_lat),
        "dev",
        split_axis=0,
        concat_axis=0,
        tiled=True,
    )
    arrived = arrived.reshape(peers * capp, page_len, width_lat)
    table = page_table[0]
    requests, most_pages = table.shape
    cache = arrived[jnp.maximum(table, 0)].reshape(requests, most_pages * page_len, width_lat)
    attended = attend(queries[0], new_latent[0], cache, context_len[0])
    owned = expert_gate.shape[0]
    experts = peers * owned
    blocks = lax.axis_size(("section", "tp"))
    rows, topk = (routing.shape[1], routing.shape[2])
    width = moe_rows.shape[2]
    capacity = min(rows, max(2, 3 * rows * topk // (2 * experts)))
    ids = routing[0].reshape(-1)
    onehot = (ids[:, None] == jnp.arange(experts)[None, :]).astype(jnp.int32)
    earlier = jnp.cumsum(onehot, axis=0) - onehot
    slot = jnp.sum(earlier * onehot, axis=1)
    position = ids * capacity + slot
    chosen = position[None, :] == jnp.arange(experts * capacity)[:, None]
    dispatch_matrix = jnp.any(chosen.reshape(experts * capacity, rows, topk), axis=2).astype(
        jnp.bfloat16
    )
    outgoing = jnp.dot(dispatch_matrix, moe_rows[0], preferred_element_type=jnp.float32).astype(
        jnp.bfloat16
    )
    outgoing = outgoing.reshape(peers, owned * capacity, width)
    pooled = lax.all_gather(outgoing[None], ("section", "tp"), axis=0, tiled=True)
    received = lax.all_to_all(pooled, "dev", split_axis=1, concat_axis=1, tiled=True)
    partial_value = partial_answer(
        received.reshape(blocks * peers, owned, capacity, width),
        expert_gate,
        expert_up,
        expert_down,
    )
    partial_value = partial_value.astype(jnp.bfloat16).reshape(
        blocks, peers, owned * capacity, width
    )
    backward = lax.all_to_all(partial_value, "dev", split_axis=1, concat_axis=1, tiled=True)
    summed = lax.psum_scatter(
        backward.astype(jnp.float32).astype(jnp.bfloat16),
        ("section", "tp"),
        scatter_dimension=0,
        tiled=True,
    )
    flat_back = summed.reshape(experts * capacity, width)
    gathered = flat_back[position].reshape(rows, topk, width)
    mixed = jnp.sum(gathered.astype(jnp.float32) * gate_weights[0][:, :, None], axis=1)
    return (attended[None], mixed.astype(jnp.bfloat16)[None])


def solution(mesh):
    return jax.shard_map(
        body,
        mesh=mesh,
        in_specs=(
            P(("grp", "dev", "section", "tp"), None, None, None),
            P(("grp", "dev", "section", "tp"), None),
            P(("grp", "dev", "section", "tp"), None, None),
            P(("grp", "dev", "section", "tp"), None),
            P(("grp", "dev", "section", "tp"), None, None, None),
            P(("grp", "dev", "section", "tp"), None, None, None, None),
            P(("grp", "dev", "section", "tp"), None, None),
            P(("grp", "dev", "section", "tp"), None, None),
            P(("grp", "dev", "section", "tp"), None, None),
            P("dev", None, ("section", "tp")),
            P("dev", None, ("section", "tp")),
            P("dev", ("section", "tp"), None),
        ),
        out_specs=(
            P(("grp", "dev", "section", "tp"), None, None, None, None),
            P(("grp", "dev", "section", "tp"), None, None),
        ),
        check_vma=False,
    )
```

profile of v0, /device:TPU:0, one launch (start us, length us, event | category | flops | bytes accessed | tf_op | source)
XLA Modules:
  0.0 111.1 jit_solution(15071533206475971144)
XLA Ops:
  7.2 0.8 eq.29
  8.1 0.2 select_reduce_fusion
  8.3 0.1 reduce_sum.33
  8.4 0.7 bitcast_add_fusion
  9.1 0.1 fusion.45
  9.2 1.1 convolution_convert_fusion.1
  10.3 0.2 broadcast_in_dim_reshape.3
  10.6 11.8 %all_gather.3 = bf16[2,16,3,3584]{3,1,2,0:T(8,128)(2,1)S(1)} all-gather(bf16[1,16,3,3584]{3,1,2,0:T(8,128)(2,1)S(1)} %copy.24), channel_id=1, replica_groups=mesh['grp'=1,'dev'=16,'section'=2,'tp'=1] {'section','tp'}, dimensions={0}, use_global_device_ids=true | all-gather | bytes 1032192 | tf_op jit(solution)/shard_map/all_gather | solution.py:94
  22.4 0.7 copy.25
  23.1 24.6 %all_to_all.15 = bf16[2,16,3,3584]{3,0,2,1:T(2,128)(2,1)S(1)} all-to-all(bf16[2,16,3,3584]{3,0,2,1:T(2,128)(2,1)S(1)} %copy.25), channel_id=1, replica_groups=mesh['grp'=1,'dev'=16,'section'=2,'tp'=1] {'dev'}, dimensions={1} | all-to-all | bytes 1376256 | tf_op jit(solution)/shard_map/all_to_all | solution.py:95
  47.8 0.7 fusion.11
  48.5 4.6 %convolution_convert_fusion = bf16[32,3,3584]{2,0,1:T(8,128)(2,1)S(1)} fusion(bf16[1,512,3584]{2,1,0:T(8,128)(2,1)} %param.23, bf16[32,3,3584]{2,0,1:T(8,128)(2,1)S(1)} %bitcast.119, bf16[1,3584,512]{2,1,0:T(8,128)(2,1)} %param.22, f32[32,1,3,512]{3,0,2,1:T(8,128)S(1)} %fusion.11), kind=kOutput, calls=%fused_computation.4 | convolution fusion | flops 705282048 | bytes 8912896 | tf_op jit(solution)/shard_map/noch,ohd->nocd/dot_general | solution.py:36
  53.1 1.6 %copy.27 = bf16[2,16,3,3584]{3,0,2,1:T(2,128)(2,1)} copy(bf16[2,16,3,3584]{3,1,0,2:T(8,128)(2,1)S(1)} %bitcast.120) | data formatting | bytes 1376256 | tf_op jit(solution)/shard_map/reshape | solution.py:102
  54.7 3.7 %all-to-all-start.2 = ((bf16[2,16,3,3584]{3,0,2,1:T(2,128)(2,1)}), bf16[2,16,3,3584]{3,0,2,1:T(2,128)(2,1)S(1)}, u32[]{:S(2)}, u32[]{:S(2)}) async-start(bf16[2,16,3,3584]{3,0,2,1:T(2,128)(2,1)} %copy.27), calls=%async_computation.2 | async-start | bytes 1376256 | tf_op jit(solution)/shard_map/all_to_all | solution.py:105
  58.4 0.1 reshape.223
  58.5 0.1 ge.20
  58.6 0.1 mul.61
  58.8 0.7 gather_fusion
  59.5 1.0 broadcast_select_fusion
  60.5 15.0 %all-to-all-done.2 = bf16[2,16,3,3584]{3,0,2,1:T(2,128)(2,1)S(1)} async-done(((bf16[2,16,3,3584]{3,0,2,1:T(2,128)(2,1)}), bf16[2,16,3,3584]{3,0,2,1:T(2,128)(2,1)S(1)}, u32[]{:S(2)}, u32[]{:S(2)}) %all-to-all-start.2) | async-done | bytes 688160 | tf_op jit(solution)/shard_map/all_to_all | solution.py:105
  75.5 4.9 %all-to-all-start = ((bf16[16,2,16,576]{3,2,1,0:T(8,128)(2,1)}), bf16[16,2,16,576]{3,2,1,0:T(8,128)(2,1)S(1)}, u32[]{:S(2)}, u32[]{:S(2)}) async-start(bf16[16,2,16,576]{3,2,1,0:T(8,128)(2,1)} %broadcast_select_fusion), calls=%async_computation | async-start | bytes 1310720 | tf_op jit(solution)/shard_map/all_to_all | solution.py:63
  80.5 0.9 copy.28
  81.5 15.5 %all-to-all-done = bf16[16,2,16,576]{3,2,1,0:T(8,128)(2,1)S(1)} async-done(((bf16[16,2,16,576]{3,2,1,0:T(8,128)(2,1)}), bf16[16,2,16,576]{3,2,1,0:T(8,128)(2,1)S(1)}, u32[]{:S(2)}, u32[]{:S(2)}) %all-to-all-start) | async-done | bytes 589856 | tf_op jit(solution)/shard_map/all_to_all | solution.py:63
  97.0 0.7 gather_fusion.1
  97.7 0.8 fusion.60
  98.4 0.6 fusion.9
  99.0 1.9 %fusion.10 = bf16[1,2,4,64,512]{4,3,2,1,0:T(8,128)(2,1)} fusion(bf16[2,256,576]{2,1,0:T(8,128)(2,1)S(1)} %bitcast.125, bf16[2,4,576]{2,1,0:T(4,128)(2,1)S(1)} %bitcast.131, f32[2,4,64]{2,1,0:T(4,128)S(1)} %fusion.60, f32[2,4,64,260]{3,2,1,0:T(8,128)S(1)} %fusion.9), kind=kOutput, calls=%fused_computation.17 | convolution fusion | flops 138042112 | bytes 2766848 | tf_op jit(solution)/shard_map/rshk,rkv->rshv/dot_general | solution.py:27
  101.0 0.2 reduce-scatter.2.cloned.1.call-done
  101.2 1.3 %copy.29 = bf16[1,16,3,3584]{3,2,1,0:T(4,128)(2,1)S(1)} copy(bf16[1,16,3,3584]{3,1,2,0:T(8,128)(2,1)} %reduce-scatter.2.cloned.1.call-done) | data formatting | bytes 688128 | tf_op jit(solution)/shard_map/reduce_scatter | solution.py:106
  102.4 0.3 reshape.211
  102.7 0.7 gather_fusion.2
  103.4 0.8 fusion.35
  (37 shorter events, 0.6 us)
Async XLA Ops:
  7.2 51.6 %copy-start = (bf16[1,32,16,576]{3,2,1,0:T(8,128)(2,1)S(1)}, bf16[1,32,16,576]{3,2,1,0:T(8,128)(2,1)}, u32[]{:S(2)}) copy-start(bf16[1,32,16,576]{3,2,1,0:T(8,128)(2,1)} %param.12) | copy-start | bytes 1769476
  10.5 37.3 %copy-start.1 = (bf16[1,3584,512]{2,1,0:T(8,128)(2,1)S(1)}, bf16[1,3584,512]{2,1,0:T(8,128)(2,1)}, u32[]{:S(2)}) copy-start(bf16[1,3584,512]{2,1,0:T(8,128)(2,1)} %param.21) | copy-start | bytes 11010052
  48.5 9.9 %copy-start.4 = (s32[1,2,16]{2,1,0:T(2,128)S(1)}, s32[1,2,16]{2,1,0:T(2,128)}, u32[]{:S(2)}) copy-start(s32[1,2,16]{2,1,0:T(2,128)} %param.14) | copy-start | bytes 388
  48.5 10.0 %copy-start.8 = (s32[1,32]{1,0:T(1,128)S(1)}, s32[1,32]{1,0:T(1,128)}, u32[]{:S(2)}) copy-start(s32[1,32]{1,0:T(1,128)} %param.13) | copy-start | bytes 388
  48.5 10.1 %copy-start.2 = (s32[1,4,8]{2,1,0:T(4,128)S(1)}, s32[1,4,8]{2,1,0:T(4,128)}, u32[]{:S(2)}) copy-start(s32[1,4,8]{2,1,0:T(4,128)} %param.19) | copy-start | bytes 388
  54.7 26.8 %copy-start.5 = (s32[1,2]{1,0:T(1,128)S(1)}, s32[1,2]{1,0:T(1,128)}, u32[]{:S(2)}) copy-start(s32[1,2]{1,0:T(1,128)} %param.15) | copy-start | bytes 28
  54.7 20.8 %all-to-all-start.2 = ((bf16[2,16,3,3584]{3,0,2,1:T(2,128)(2,1)}), bf16[2,16,3,3584]{3,0,2,1:T(2,128)(2,1)S(1)}, u32[]{:S(2)}, u32[]{:S(2)}) async-start(bf16[2,16,3,3584]{3,0,2,1:T(2,128)(2,1)} %copy.27), calls=%async_computation.2 | async-start | bytes 1376256 | tf_op jit(solution)/shard_map/all_to_all | solution.py:105
  58.8 38.9 %copy-start.6 = (bf16[1,2,4,64,576]{4,3,2,1,0:T(8,128)(2,1)S(1)}, bf16[1,2,4,64,576]{4,3,2,1,0:T(8,128)(2,1)}, u32[]{:S(2)}) copy-start(bf16[1,2,4,64,576]{4,3,2,1,0:T(8,128)(2,1)} %param.17) | copy-start | bytes 1769476
  58.8 38.9 %copy-start.7 = (bf16[1,2,4,576]{3,2,1,0:T(4,128)(2,1)S(1)}, bf16[1,2,4,576]{3,2,1,0:T(4,128)(2,1)}, u32[]{:S(2)}) copy-start(bf16[1,2,4,576]{3,2,1,0:T(4,128)(2,1)} %param.16) | copy-start | bytes 27652
  75.5 21.5 %all-to-all-start = ((bf16[16,2,16,576]{3,2,1,0:T(8,128)(2,1)}), bf16[16,2,16,576]{3,2,1,0:T(8,128)(2,1)S(1)}, u32[]{:S(2)}, u32[]{:S(2)}) async-start(bf16[16,2,16,576]{3,2,1,0:T(8,128)(2,1)} %broadcast_select_fusion), calls=%async_computation | async-start | bytes 1310720 | tf_op jit(solution)/shard_map/all_to_all | solution.py:63
  80.4 20.8 %reduce-scatter.2.cloned.1.call-start = ((), (), s32[]{:S(2)}) async-start(), calls=%async_computation.4 | async-start | bytes 1032192 | tf_op jit(solution)/shard_map/reduce_scatter | solution.py:106
  99.0 4.4 %copy-start.3 = (f32[1,4,8]{2,1,0:T(4,128)S(1)}, f32[1,4,8]{2,1,0:T(4,128)}, u32[]{:S(2)}) copy-start(f32[1,4,8]{2,1,0:T(4,128)} %param.20) | copy-start | bytes 388
Sparse Core Ops, SparseCore 0:
  83.5 17.6 reduce-scatter.1
where the time goes:
time: 112 us; the launch traced here: 111 us
  blocking collectives  36.4 us (32%)
  waiting for transfers between devices  30.7 us (27%)
  between operations  14.3 us (13%)
  matrix products  9.6 us (9%)
  starting transfers between devices  8.67 us (8%)
  local copies, waits for them, and re-layouts  8.34 us (7%)
  other arithmetic  3.08 us (3%)
    all_to_all x1, blocking collectives, body(): lax.all_to_all(pooled, 'dev', split_axis=1, concat_axis=1, tiled=True)  24.6 us
    all_to_all x1, waiting for transfers between devices, body(): lax.all_to_all(picked_pages.reshape(peers, capp, page_len, width_lat), 'd...  15.5 us
    all_to_all x1, waiting for transfers between devices, body(): lax.all_to_all(partial_value, 'dev', split_axis=1, concat_axis=1, tiled=T...  15 us
    all_gather x1, blocking collectives, body(): lax.all_gather(outgoing[None], ('section', 'tp'), axis=0, tiled=True)  11.8 us
    all_to_all x1, starting transfers between devices, body(): lax.all_to_all(picked_pages.reshape(peers, capp, page_len, width_lat), 'd...  4.9 us
    dot_general x1, matrix products, partial_answer(): jnp.einsum('noch,ohd->nocd', hidden, w_down, preferred_element_type=jnp.f...  4.57 us
    all_to_all x1, starting transfers between devices, body(): lax.all_to_all(partial_value, 'dev', split_axis=1, concat_axis=1, tiled=T...  3.73 us
  transfers between devices with their start and end apart: 3, of which 3 were waited for; matrix products, arithmetic and copies ran while one was open for 6% of the time, Pallas kernels for 0%

commit v1 on v0

v1 whole, which is shorter than its diff:
```python
import jax
import jax.numpy as jnp
from jax import lax
from jax.sharding import PartitionSpec as P

VDIM = 512
SCALE = 192.0 ** (-0.5)
RANK = ("dev", "section", "tp")


def attend(queries, new_latent, cache, lengths):
    steps = queries.shape[1]
    ctx = cache.shape[1]
    keys = jnp.concatenate([cache, new_latent], axis=1)
    scores = jnp.einsum("rshl,rkl->rshk", queries, keys, preferred_element_type=jnp.float32) * SCALE
    position = jnp.arange(ctx + steps)
    step_index = jnp.arange(steps)
    in_cache = position[None, :] < lengths[:, None]
    in_new = (position[None, :] >= ctx) & (position[None, :] - ctx <= step_index[:, None])
    allowed = in_cache[:, None, :] | in_new[None, :, :]
    scores = jnp.where(allowed[:, :, None, :], scores, -jnp.inf)
    top = jnp.max(scores, axis=-1, keepdims=True)
    weights = jnp.exp(scores - top)
    weights = (weights / jnp.sum(weights, axis=-1, keepdims=True)).astype(jnp.bfloat16)
    values = keys[:, :, :VDIM]
    return jnp.einsum("rshk,rkv->rshv", weights, values, preferred_element_type=jnp.float32).astype(
        jnp.bfloat16
    )


def body(
    prompt_pages,
    send_page,
    page_table,
    context_len,
    new_latent,
    queries,
    moe_rows,
    routing,
    gate_weights,
    expert_gate,
    expert_up,
    expert_down,
):
    peers = lax.axis_size("dev")
    pages = prompt_pages[0]
    outgoing_slots = send_page[0]
    page_len, width_lat = (pages.shape[1], pages.shape[2])
    capp = outgoing_slots.shape[0] // peers
    picked_pages = pages[jnp.maximum(outgoing_slots, 0)]
    arrived = lax.all_to_all(
        picked_pages.reshape(peers, capp, page_len, width_lat),
        "dev",
        split_axis=0,
        concat_axis=0,
        tiled=True,
    )
    arrived = arrived.reshape(peers * capp, page_len, width_lat)

    owned = expert_gate.shape[0]
    experts = peers * owned
    rows = routing.shape[1]
    width = moe_rows.shape[2]
    named = routing[0][:, :, None] == jnp.arange(experts)[None, None, :]
    dense = jnp.sum(jnp.where(named, gate_weights[0][:, :, None], 0.0), axis=1)
    high = dense.astype(jnp.bfloat16)
    low = (dense - high.astype(jnp.float32)).astype(jnp.bfloat16)
    extra = jnp.concatenate([high, low], axis=1)
    pad = -extra.shape[1] % 128
    packed = jnp.concatenate([moe_rows[0], jnp.pad(extra, ((0, 0), (0, pad)))], axis=1)
    pooled = lax.all_gather(packed, RANK, axis=0, tiled=True)
    every = pooled[:, :width]
    first = lax.axis_index("dev") * owned
    total = None
    for own in range(owned):
        column = width + first + own
        weight = lax.dynamic_slice_in_dim(pooled, column, 1, 1).astype(jnp.float32) + lax.dynamic_slice_in_dim(
            pooled, column + experts, 1, 1
        ).astype(jnp.float32)
        gate = jnp.dot(every, expert_gate[own], preferred_element_type=jnp.float32)
        up = jnp.dot(every, expert_up[own], preferred_element_type=jnp.float32)
        hidden = (jax.nn.silu(gate) * up).astype(jnp.bfloat16)
        term = jnp.dot(hidden, expert_down[own], preferred_element_type=jnp.float32) * weight
        total = term if total is None else total + term
    mixed = lax.psum_scatter(total.astype(jnp.bfloat16), RANK, scatter_dimension=0, tiled=True)

    table = page_table[0]
    requests, most_pages = table.shape
    cache = arrived[jnp.maximum(table, 0)].reshape(requests, most_pages * page_len, width_lat)
    attended = attend(queries[0], new_latent[0], cache, context_len[0])
    return (attended[None], mixed[None])


def solution(mesh):
    rank = ("grp",) + RANK
    return jax.shard_map(
        body,
        mesh=mesh,
        in_specs=(
            P(rank, None, None, None),
            P(rank, None),
            P(rank, None, None),
            P(rank, None),
            P(rank, None, None, None),
            P(rank, None, None, None, None),
            P(rank, None, None),
            P(rank, None, None),
            P(rank, None, None),
            P("dev", None, ("section", "tp")),
            P("dev", None, ("section", "tp")),
            P("dev", ("section", "tp"), None),
        ),
        out_specs=(
            P(rank, None, None, None, None),
            P(rank, None, None),
        ),
        check_vma=False,
    )
```

time: 112 us -> 238 us (2.12)
  waiting for transfers between devices: 30.7 us -> 125 us
  blocking collectives: 36.4 us -> 75.4 us
  starting transfers between devices: 8.67 us -> 3.63 us
  local copies, waits for them, and re-layouts: 8.34 us -> 4.18 us
  matrix products: 9.6 us -> 13.6 us
    unnamed x1 -> x2, waiting for transfers between devices: 0.02 us -> 125 us
    all_gather x1, blocking collectives: 11.8 us -> 75.4 us  [body(): pooled = lax.all_gather(packed, RANK, axis=0, tiled=True)]
    all_to_all x1 -> x0, blocking collectives: 24.6 us -> none  [body(): lax.all_to_all(pooled, 'dev', split_axis=1, concat_axis=1, tiled=True)]
    all_to_all x1, waiting for transfers between devices: 15.5 us -> 0.01 us  [body(): lax.all_to_all(picked_pages.reshape(peers, capp, page_len, width_lat), 'd...]
    all_to_all x1 -> x0, waiting for transfers between devices: 15 us -> none  [body(): lax.all_to_all(partial_value, 'dev', split_axis=1, concat_axis=1, tiled=T...]
    all_to_all x1 -> x0, starting transfers between devices: 3.73 us -> none  [body(): lax.all_to_all(partial_value, 'dev', split_axis=1, concat_axis=1, tiled=T...]
    dot_general x3 -> x2, matrix products: 6.34 us -> 8.09 us  [the longest x1 5.38 us: body(): jnp.dot(hidden, expert_down[own], preferred_element_type=jnp.float32)]
  transfers between devices with their start and end apart: 3 -> 2, of which waited for: 3 -> 1; matrix products, arithmetic and copies ran while one was open for 6% -> 1% of each run, Pallas kernels for 0% -> 0%
where the time goes in v1:
time: 238 us
  waiting for transfers between devices  125 us (53%)
  blocking collectives  75.4 us (32%)
  between operations  14.2 us (6%)
  matrix products  13.6 us (6%)
  local copies, waits for them, and re-layouts  4.18 us (2%)
  starting transfers between devices  3.63 us (2%)
    unnamed x2, waiting for transfers between devices  125 us
    all_gather x1, blocking collectives, body(): pooled = lax.all_gather(packed, RANK, axis=0, tiled=True)  75.4 us
    dot_general x1, matrix products, body(): jnp.dot(hidden, expert_down[own], preferred_element_type=jnp.float32)  5.38 us
  transfers between devices with their start and end apart: 2, of which 1 were waited for; matrix products, arithmetic and copies ran while one was open for 1% of the time, Pallas kernels for 0%

profile of v1, /device:TPU:0, one launch (start us, length us, event | category | flops | bytes accessed | tf_op | source)
XLA Modules:
  0.0 238.0 jit_solution(472562673525085344)
XLA Ops:
  7.2 0.0 copy-start
  7.2 0.0 all-reduce.4.cloned.1.call-start
  7.2 0.8 select_reduce_fusion
  8.1 0.1 fusion.44
  8.2 0.8 maximum_bitcast_fusion
  8.9 75.4 %all-gather = bf16[32,4,3712]{2,1,0:T(4,128)(2,1)S(1)} all-gather(bf16[1,4,3712]{2,1,0:T(4,128)(2,1)S(1)} %maximum_bitcast_fusion), channel_id=1, replica_groups=mesh['grp'=1,'dev'=16,'section'=2,'tp'=1] {'dev','section','tp'}, dimensions={0}, use_global_device_ids=true | all-gather | bytes 979968 | tf_op jit(solution)/shard_map/all_gather | solution.py:71
  84.3 0.2 reshape.131
  84.6 0.1 constant_dynamic-slice_fusion.1
  84.7 0.1 copy.22
  84.7 0.1 copy.23
  84.8 2.7 %fusion.5 = f32[128,512]{1,0:T(8,128)S(1)} fusion(bf16[1,3584,512]{2,1,0:T(8,128)(2,1)} %param.21, bf16[128,3712]{1,0:T(8,128)(2,1)S(1)} %reshape.131), kind=kOutput, calls=%fused_computation.8 | convolution fusion | flops 469762048 | bytes 4849664 | tf_op jit(solution)/shard_map/dot_general | solution.py:80
  87.6 0.0 copy-start.5
  87.6 0.0 copy-start.1
  87.6 0.0 copy-start.2
  87.6 5.4 %fusion.1 = bf16[128,3584]{1,0:T(8,128)(2,1)} fusion(bf16[1,512,3584]{2,1,0:T(8,128)(2,1)} %param.23, f32[128]{0:T(128)S(1)} %add_bitcast_fusion, bf16[1,3584,512]{2,1,0:T(8,128)(2,1)} %param.22, bf16[128,3712]{1,0:T(8,128)(2,1)S(1)} %reshape.131, f32[128,512]{1,0:T(8,128)S(1)} %fusion.5), kind=kOutput, calls=%fused_computation.4 | convolution fusion | flops 940834816 | bytes 9437696 | tf_op jit(solution)/shard_map/dot_general | solution.py:83
  93.0 0.0 all-reduce.4.cloned.1.call-update
  93.0 0.0 copy-done.5
  93.0 0.0 copy-done
  93.0 1.5 gather_fusion
  94.5 3.6 %all-to-all-start = ((bf16[16,2,16,576]{3,2,1,0:T(8,128)(2,1)}), bf16[16,2,16,576]{3,2,1,0:T(8,128)(2,1)S(1)}, u32[]{:S(2)}, u32[]{:S(2)}) async-start(bf16[16,2,16,576]{3,2,1,0:T(8,128)(2,1)} %bitcast.3), calls=%async_computation | async-start | bytes 1310720 | tf_op jit(solution)/shard_map/all_to_all | solution.py:51
  98.1 0.0 copy-done.1
  98.1 0.1 reshape.120
  98.2 0.1 iota_compare_fusion.2
  98.4 125.2 %all-reduce.4.cloned.1.call-done = bf16[128,3584]{1,0:T(8,128)(2,1)} async-done(((bf16[128,3584]{1,0:T(8,128)(2,1)}), bf16[128,3584]{1,0:T(8,128)(2,1)}) %all-reduce.4.cloned.1.call-update) | async-done | bytes 917520
  223.5 1.4 dynamic-slice_bitcast_fusion
  225.0 0.0 all-to-all-done
  225.0 0.7 gather_fusion.1
  225.6 0.0 copy-done.3
  225.7 0.0 copy-done.4
  225.7 1.4 fusion.10
  227.1 0.7 fusion.53
  227.8 3.3 %fusion.11 = bf16[1,2,4,64,512]{4,3,2,1,0:T(8,128)(2,1)} fusion(bf16[2,256,576]{2,1,0:T(8,128)(2,1)S(1)} %bitcast.68, bf16[2,4,576]{2,1,0:T(4,128)(2,1)S(1)} %bitcast.75, f32[2,4,64]{2,1,0:T(4,128)S(1)} %fusion.53, f32[2,4,64,260]{3,2,1,0:T(8,128)} %fusion.10), kind=kOutput, calls=%fused_computation.16 | convolution fusion | flops 138042112 | bytes 2698240 | tf_op jit(solution)/shard_map/rshk,rkv->rshv/dot_general | solution.py:26
  (13 shorter events, 0.1 us)
Async XLA Ops:
  7.2 85.9 %copy-start = (bf16[1,32,16,576]{3,2,1,0:T(8,128)(2,1)S(1)}, bf16[1,32,16,576]{3,2,1,0:T(8,128)(2,1)}, u32[]{:S(2)}) copy-start(bf16[1,32,16,576]{3,2,1,0:T(8,128)(2,1)} %param.12) | copy-start | bytes 1769476
  7.2 216.3 %all-reduce.4.cloned.1.call-start = ((), (), s32[]{:S(2)}) async-start(), calls=%async_computation.1 | async-start | bytes 1835008
  87.6 5.4 %copy-start.5 = (s32[1,32]{1,0:T(1,128)S(1)}, s32[1,32]{1,0:T(1,128)}, u32[]{:S(2)}) copy-start(s32[1,32]{1,0:T(1,128)} %param.13) | copy-start | bytes 388
  87.6 10.6 %copy-start.1 = (s32[1,2,16]{2,1,0:T(2,128)S(1)}, s32[1,2,16]{2,1,0:T(2,128)}, u32[]{:S(2)}) copy-start(s32[1,2,16]{2,1,0:T(2,128)} %param.14) | copy-start | bytes 388
  87.6 10.7 %copy-start.2 = (s32[1,2]{1,0:T(1,128)S(1)}, s32[1,2]{1,0:T(1,128)}, u32[]{:S(2)}) copy-start(s32[1,2]{1,0:T(1,128)} %param.15) | copy-start | bytes 28
  93.0 132.7 %copy-start.3 = (bf16[1,2,4,64,576]{4,3,2,1,0:T(8,128)(2,1)S(1)}, bf16[1,2,4,64,576]{4,3,2,1,0:T(8,128)(2,1)}, u32[]{:S(2)}) copy-start(bf16[1,2,4,64,576]{4,3,2,1,0:T(8,128)(2,1)} %param.17) | copy-start | bytes 1769476
  93.0 132.7 %copy-start.4 = (bf16[1,2,4,576]{3,2,1,0:T(4,128)(2,1)S(1)}, bf16[1,2,4,576]{3,2,1,0:T(4,128)(2,1)}, u32[]{:S(2)}) copy-start(bf16[1,2,4,576]{3,2,1,0:T(4,128)(2,1)} %param.16) | copy-start | bytes 27652
  94.5 130.4 %all-to-all-start = ((bf16[16,2,16,576]{3,2,1,0:T(8,128)(2,1)}), bf16[16,2,16,576]{3,2,1,0:T(8,128)(2,1)S(1)}, u32[]{:S(2)}, u32[]{:S(2)}) async-start(bf16[16,2,16,576]{3,2,1,0:T(8,128)(2,1)} %bitcast.3), calls=%async_computation | async-start | bytes 1310720 | tf_op jit(solution)/shard_map/all_to_all | solution.py:51
Sparse Core Ops, SparseCore 0:
  93.1 130.3 all-reduce.3

commit v2 on v1

--- a/solution.py
+++ b/solution.py
@@ -6,6 +6,30 @@
 VDIM = 512
 SCALE = 192.0 ** (-0.5)
 RANK = ("dev", "section", "tp")
+
+
+def gather_stages(peers, blocks):
+    low = blocks.bit_length() - 1
+    bits = peers.bit_length() - 1
+    far = [low + bit for bit in range(2, bits)]
+    near = list(range(low)) + [low + bit for bit in range(1, min(bits, 2))]
+    last = [low + bit for bit in range(min(bits, 1))]
+    stages = []
+    for group in (far, near, last):
+        stages += [group[at : at + 2] for at in range(0, len(group), 2)]
+    return stages
+
+
+def masks_of(stage):
+    masks = [0]
+    for bit in stage:
+        masks += [mask | (1 << bit) for mask in masks]
+    return masks
+
+
+def exchange(value, mask):
+    count = lax.axis_size(RANK)
+    return lax.ppermute(value, RANK, [(at, at ^ mask) for at in range(count)])
 
 
 def attend(queries, new_latent, cache, lengths):
@@ -68,7 +92,12 @@
     extra = jnp.concatenate([high, low], axis=1)
     pad = -extra.shape[1] % 128
     packed = jnp.concatenate([moe_rows[0], jnp.pad(extra, ((0, 0), (0, pad)))], axis=1)
-    pooled = lax.all_gather(packed, RANK, axis=0, tiled=True)
+    stages = gather_stages(peers, lax.axis_size(("section", "tp")))
+    pooled = packed
+    for stage in stages:
+        pooled = jnp.concatenate(
+            [pooled] + [exchange(pooled, mask) for mask in masks_of(stage)[1:]], axis=0
+        )
     every = pooled[:, :width]
     first = lax.axis_index("dev") * owned
     total = None
@@ -82,7 +111,15 @@
         hidden = (jax.nn.silu(gate) * up).astype(jnp.bfloat16)
         term = jnp.dot(hidden, expert_down[own], preferred_element_type=jnp.float32) * weight
         total = term if total is None else total + term
-    mixed = lax.psum_scatter(total.astype(jnp.bfloat16), RANK, scatter_dimension=0, tiled=True)
+    mixed = total.astype(jnp.bfloat16)
+    for stage in stages[::-1]:
+        masks = masks_of(stage)
+        count = mixed.shape[0] // len(masks)
+        kept = mixed[:count].astype(jnp.float32)
+        for turn in range(1, len(masks)):
+            sent = mixed[turn * count : (turn + 1) * count]
+            kept = kept + exchange(sent, masks[turn]).astype(jnp.float32)
+        mixed = kept.astype(jnp.bfloat16)
 
     table = page_table[0]
     requests, most_pages = table.shape

time: 238 us -> 57.5 us (0.24)
  waiting for transfers between devices: 125 us -> 13.2 us
  blocking collectives: 75.4 us -> 0 us
  starting transfers between devices: 3.63 us -> 21.5 us
  between operations: 14.2 us -> 0.83 us
  other arithmetic: 1.81 us -> 4.29 us
    unnamed x2 -> x0, waiting for transfers between devices: 125 us -> none
    all_gather x1 -> x0, blocking collectives: 75.4 us -> none  [body(): pooled = lax.all_gather(packed, RANK, axis=0, tiled=True)]
    ppermute x0 -> x14, starting transfers between devices: none -> 17.9 us  [exchange(): return lax.ppermute(value, RANK, [(at, at ^ mask) for at in range(count)])]
    ppermute x0 -> x14, waiting for transfers between devices: none -> 13.2 us  [exchange(): return lax.ppermute(value, RANK, [(at, at ^ mask) for at in range(count)])]
  transfers between devices with their start and end apart: 2 -> 15, of which waited for: 1 -> 7; matrix products, arithmetic and copies ran while one was open for 1% -> 32% of each run, Pallas kernels for 0% -> 0%
where the time goes in v2:
time: 57.5 us; the launch traced here: 57 us
  starting transfers between devices  21.5 us (37%)
  waiting for transfers between devices  13.2 us (23%)
  matrix products  12.5 us (22%)
  local copies, waits for them, and re-layouts  4.6 us (8%)
  other arithmetic  4.29 us (7%)
  between operations  0.83 us (1%)
    ppermute x14, starting transfers between devices, exchange(): return lax.ppermute(value, RANK, [(at, at ^ mask) for at in range(count)])  17.9 us
    ppermute x14, waiting for transfers between devices, exchange(): return lax.ppermute(value, RANK, [(at, at ^ mask) for at in range(count)])  13.2 us
    dot_general x1, matrix products, body(): jnp.dot(hidden, expert_down[own], preferred_element_type=jnp.float32)  4.46 us
    all_to_all x1, starting transfers between devices, body(): lax.all_to_all(picked_pages.reshape(peers, capp, page_len, width_lat), 'd...  3.59 us
    dot_general x1, matrix products, body(): up = jnp.dot(every, expert_up[own], preferred_element_type=jnp.float32)  2.68 us
    concatenate x2, local copies, waits for them, and re-layouts, body(): jnp.concatenate([pooled] + [exchange(pooled, mask) for mask in masks_of(s...  2.26 us
    dot_general x1, matrix products, attend(): jnp.einsum('rshk,rkv->rshv', weights, values, preferred_element_type=jnp....  1.93 us
    sub x1, matrix products, attend(): weights = jnp.exp(scores - top)  1.83 us
  transfers between devices with their start and end apart: 15, of which 7 were waited for; matrix products, arithmetic and copies ran while one was open for 32% of the time, Pallas kernels for 0%

profile of v2, /device:TPU:0, one launch (start us, length us, event | category | flops | bytes accessed | tf_op | source)
XLA Modules:
  0.0 57.0 jit_solution(10531884183918563096)
XLA Ops:
  0.7 0.8 %select_reduce_fusion = f32[4,16]{1,0:T(4,128)S(1)} fusion(f32[4,8]{1,0:T(4,128)} %bitcast.65, s32[4,8]{1,0:T(4,128)} %bitcast.66), kind=kLoop, calls=%fused_computation.38 | loop fusion | flops 1472 | bytes 512 | tf_op jit(solution)/shard_map/reduce_sum | solution.py:89
  1.6 0.8 %pad_maximum_fusion.2 = bf16[4,3712]{1,0:T(4,128)(2,1)S(1)} fusion(bf16[4,128]{1,0:T(4,128)(2,1)S(1)} %fusion.39, bf16[4,3584]{1,0:T(4,128)(2,1)} %bitcast.63), kind=kLoop, calls=%fused_computation.36 | loop fusion | flops 59392 | bytes 59392 | tf_op jit(solution)/shard_map/concatenate | solution.py:94
  2.4 3.1 %collective-permute-start = (bf16[4,3712]{1,0:T(4,128)(2,1)S(1)}, bf16[4,3712]{1,0:T(4,128)(2,1)S(1)}, u32[]{:S(2)}, u32[]{:S(2)}) collective-permute-start(bf16[4,3712]{1,0:T(4,128)(2,1)S(1)} %pad_maximum_fusion.2), channel_id=1, source_target_pairs={{0,8},{1,9},{2,10},{3,11},{4,12},{5,13},{6,14},{7,15},{8,0},{9,1},... | collective-permute-start | bytes 89096 | tf_op jit(solution)/shard_map/ppermute | solution.py:32
  5.5 2.6 %collective-permute-start.1 = (bf16[4,3712]{1,0:T(4,128)(2,1)S(1)}, bf16[4,3712]{1,0:T(4,128)(2,1)S(1)}, u32[]{:S(2)}, u32[]{:S(2)}) collective-permute-start(bf16[4,3712]{1,0:T(4,128)(2,1)S(1)} %pad_maximum_fusion.2), channel_id=1, source_target_pairs={{0,16},{1,17},{2,18},{3,19},{4,20},{5,21},{6,22},{7,23},{8,24},{9,... | collective-permute-start | bytes 89096 | tf_op jit(solution)/shard_map/ppermute | solution.py:32
  8.1 2.7 %collective-permute-done.1 = bf16[4,3712]{1,0:T(4,128)(2,1)S(1)} collective-permute-done((bf16[4,3712]{1,0:T(4,128)(2,1)S(1)}, bf16[4,3712]{1,0:T(4,128)(2,1)S(1)}, u32[]{:S(2)}, u32[]{:S(2)}) %collective-permute-start.1) | collective-permute-done | bytes 29728 | tf_op jit(solution)/shard_map/ppermute | solution.py:32
  10.7 3.0 %collective-permute-done.2 = bf16[4,3712]{1,0:T(4,128)(2,1)S(1)} collective-permute-done((bf16[4,3712]{1,0:T(4,128)(2,1)S(1)}, bf16[4,3712]{1,0:T(4,128)(2,1)S(1)}, u32[]{:S(2)}, u32[]{:S(2)}) %collective-permute-start.2) | collective-permute-done | bytes 29728 | tf_op jit(solution)/shard_map/ppermute | solution.py:32
  13.7 0.8 %pad_maximum_fusion.1 = bf16[16,3712]{1,0:T(8,128)(2,1)S(1)} fusion(bf16[4,3712]{1,0:T(4,128)(2,1)S(1)} %collective-permute-done.2, bf16[4,3712]{1,0:T(4,128)(2,1)S(1)} %collective-permute-done.1, bf16[4,3712]{1,0:T(4,128)(2,1)S(1)} %collective-permute-done, bf16[4,128]{1,0:T(4,128)(2,1)S(1)} %fusion.39, bf16[4,3584]{1,0:T(4,128)(2,1)} %bitcast.64), kind=kLoop, calls=%fused_computation.33 | loop fusion | flops 593920 | bytes 237568 | tf_op jit(solution)/shard_map/concatenate | solution.py:98
  14.6 1.6 %collective-permute-start.3 = (bf16[16,3712]{1,0:T(8,128)(2,1)S(1)}, bf16[16,3712]{1,0:T(8,128)(2,1)S(1)}, u32[]{:S(2)}, u32[]{:S(2)}) collective-permute-start(bf16[16,3712]{1,0:T(8,128)(2,1)S(1)} %pad_maximum_fusion.1), channel_id=1, source_target_pairs={{0,1},{1,0},{2,3},{3,2},{4,5},{5,4},{6,7},{7,6},{8,9},{9,8},{10,11... | collective-permute-start | bytes 356360 | tf_op jit(solution)/shard_map/ppermute | solution.py:32
  16.1 1.5 %collective-permute-start.4 = (bf16[16,3712]{1,0:T(8,128)(2,1)S(1)}, bf16[16,3712]{1,0:T(8,128)(2,1)S(1)}, u32[]{:S(2)}, u32[]{:S(2)}) collective-permute-start(bf16[16,3712]{1,0:T(8,128)(2,1)S(1)} %pad_maximum_fusion.1), channel_id=1, source_target_pairs={{0,4},{1,5},{2,6},{3,7},{4,0},{5,1},{6,2},{7,3},{8,12},{9,13},{10,... | collective-permute-start | bytes 356360 | tf_op jit(solution)/shard_map/ppermute | solution.py:32
  17.6 0.5 collective-permute-start.5
  18.1 0.7 %maximum_bitcast_fusion = s32[32]{0:T(128)S(1)} fusion(s32[1,32]{1,0:T(1,128)} %param.13), kind=kLoop, calls=%fused_computation.54 | loop fusion | flops 32 | bytes 256 | tf_op jit(solution)/shard_map/max | solution.py:74
  18.8 1.5 %gather_fusion = bf16[32,16,576]{2,1,0:T(8,128)(2,1)} fusion(bf16[32,16,576]{2,1,0:T(8,128)(2,1)S(1)} %bitcast.58, s32[1024]{0:T(1024)S(1)} %pad_clamp_fusion.1), kind=kCustom, calls=%fused_computation | custom fusion | bytes 1179776 | tf_op jit(solution)/shard_map/gather | solution.py:74
  20.2 3.6 %all-to-all-start = ((bf16[16,2,16,576]{3,2,1,0:T(8,128)(2,1)}), bf16[16,2,16,576]{3,2,1,0:T(8,128)(2,1)S(1)}, u32[]{:S(2)}, u32[]{:S(2)}) async-start(bf16[16,2,16,576]{3,2,1,0:T(8,128)(2,1)} %bitcast.3), calls=%async_computation | async-start | bytes 1310720 | tf_op jit(solution)/shard_map/all_to_all | solution.py:75
  24.1 0.4 collective-permute-start.6
  24.6 1.5 %collective-permute-done.6 = bf16[64,3712]{1,0:T(8,128)(2,1)} collective-permute-done((bf16[64,3712]{1,0:T(8,128)(2,1)S(1)}, bf16[64,3712]{1,0:T(8,128)(2,1)}, u32[]{:S(2)}, u32[]{:S(2)}) %collective-permute-start.6) | collective-permute-done | bytes 475168 | tf_op jit(solution)/shard_map/ppermute | solution.py:32
  26.1 2.1 %concatenate.25 = bf16[128,3712]{1,0:T(8,128)(2,1)S(1)} concatenate(bf16[4,3712]{1,0:T(4,128)(2,1)S(1)} %pad_maximum_fusion.2, bf16[4,3712]{1,0:T(4,128)(2,1)S(1)} %collective-permute-done, bf16[4,3712]{1,0:T(4,128)(2,1)S(1)} %collective-permute-done.1, bf16[4,3712]{1,0:T(4,128)(2,1)S(1)} %collective-permute-done.2, bf16[16,3712]{1,0:T(8,128)(2,1)S(1)} %collective-permute-done.3, ...), dimensions={0} | concatenate | bytes 1900544 | tf_op jit(solution)/shard_map/concatenate | solution.py:98
  28.2 2.7 %fusion.3 = f32[128,512]{1,0:T(8,128)S(1)} fusion(bf16[1,3584,512]{2,1,0:T(8,128)(2,1)} %param.22, bf16[128,3712]{1,0:T(8,128)(2,1)S(1)} %concatenate.25), kind=kOutput, calls=%fused_computation.6 | convolution fusion | flops 469762048 | bytes 4849664 | tf_op jit(solution)/shard_map/dot_general | solution.py:110
  31.1 4.5 %fusion.1 = bf16[128,3584]{1,0:T(8,128)(2,1)S(1)} fusion(bf16[1,512,3584]{2,1,0:T(8,128)(2,1)} %param.23, f32[128]{0:T(128)S(1)} %add_reduce_fusion, f32[128,512]{1,0:T(8,128)S(1)} %fusion.3, bf16[1,3584,512]{2,1,0:T(8,128)(2,1)} %param.21, bf16[128,3712]{1,0:T(8,128)(2,1)S(1)} %concatenate.25), kind=kOutput, calls=%fused_computation.4 | convolution fusion | flops 940834816 | bytes 9437696 | tf_op jit(solution)/shard_map/dot_general | solution.py:112
  35.6 0.4 collective-permute-start.7
  36.0 1.5 %collective-permute-done.7 = bf16[64,3584]{1,0:T(8,128)(2,1)S(1)} collective-permute-done((bf16[64,3584]{1,0:T(8,128)(2,1)S(1)}, bf16[64,3584]{1,0:T(8,128)(2,1)S(1)}, u32[]{:S(2)}, u32[]{:S(2)}) %collective-permute-start.7) | collective-permute-done | bytes 458784 | tf_op jit(solution)/shard_map/ppermute | solution.py:32
  37.6 2.8 %collective-permute-start.10 = (bf16[16,3584]{1,0:T(8,128)(2,1)S(1)}, bf16[16,3584]{1,0:T(8,128)(2,1)S(1)}, u32[]{:S(2)}, u32[]{:S(2)}) collective-permute-start(bf16[16,3584]{1,0:T(8,128)(2,1)S(1)} %get-tuple-element.5), channel_id=1, source_target_pairs={{0,5},{1,4},{2,7},{3,6},{4,1},{5,0},{6,3},{7,2},{8,13},{9,12},{10,... | collective-permute-start | bytes 344072 | tf_op jit(solution)/shard_map/ppermute | solution.py:32
  40.4 0.5 collective-permute-start.8
  41.2 0.7 %gather_fusion.1 = bf16[32,16,576]{2,1,0:T(8,128)(2,1)S(1)} fusion(bf16[32,16,576]{2,1,0:T(8,128)(2,1)S(1)} %bitcast.59, s32[1024]{0:T(1024)S(1)} %pad_clamp_fusion), kind=kCustom, calls=%fused_computation.1 | custom fusion | bytes 1179776 | tf_op jit(solution)/shard_map/gather | solution.py:126
  41.8 1.6 %fusion.10 = f32[2,4,64,260]{3,2,1,0:T(8,128)S(1)} fusion(bf16[2,4,576]{2,1,0:T(4,128)(2,1)S(1)} %bitcast.68, bf16[1,2,4,64,576]{4,3,2,1,0:T(8,128)(2,1)} %param.17, bf16[2,256,576]{2,1,0:T(8,128)(2,1)S(1)} %bitcast.60, pred[2,4,260]{2,1,0:T(4,128)(4,1)S(1)} %broadcast_or_fusion), kind=kOutput, calls=%fused_computation.15 | convolution fusion | flops 154818560 | bytes 1723424 | tf_op jit(solution)/shard_map/rshl,rkl->rshk/dot_general | solution.py:39
  43.5 1.8 %fusion.50 = f32[2,4,64]{2,1,0:T(4,128)S(1)} fusion(bf16[2,4,576]{2,1,0:T(4,128)(2,1)S(1)} %bitcast.69, bf16[1,2,4,64,576]{4,3,2,1,0:T(8,128)(2,1)} %param.17, bf16[2,256,576]{2,1,0:T(8,128)(2,1)S(1)} %bitcast.61, pred[2,4,260]{2,1,0:T(4,128)(4,1)S(1)} %broadcast_or_fusion), kind=kOutput, calls=%fused_computation.64 | convolution fusion | flops 155085056 | bytes 1192992 | tf_op jit(solution)/shard_map/sub | solution.py:47
  45.3 1.2 %collective-permute-done.8 = bf16[16,3584]{1,0:T(8,128)(2,1)S(1)} collective-permute-done((bf16[16,3584]{1,0:T(8,128)(2,1)S(1)}, bf16[16,3584]{1,0:T(8,128)(2,1)S(1)}, u32[]{:S(2)}, u32[]{:S(2)}) %collective-permute-start.8) | collective-permute-done | bytes 114720 | tf_op jit(solution)/shard_map/ppermute | solution.py:32
  46.7 1.6 %collective-permute-start.11 = (bf16[4,3584]{1,0:T(4,128)(2,1)S(1)}, bf16[4,3584]{1,0:T(4,128)(2,1)S(1)}, u32[]{:S(2)}, u32[]{:S(2)}) collective-permute-start(bf16[4,3584]{1,0:T(4,128)(2,1)S(1)} %get-tuple-element.7), channel_id=1, source_target_pairs={{0,8},{1,9},{2,10},{3,11},{4,12},{5,13},{6,14},{7,15},{8,0},{9,1},... | collective-permute-start | bytes 86024 | tf_op jit(solution)/shard_map/ppermute | solution.py:32
  48.2 2.4 %collective-permute-start.12 = (bf16[4,3584]{1,0:T(4,128)(2,1)S(1)}, bf16[4,3584]{1,0:T(4,128)(2,1)S(1)}, u32[]{:S(2)}, u32[]{:S(2)}) collective-permute-start(bf16[4,3584]{1,0:T(4,128)(2,1)S(1)} %get-tuple-element.9), channel_id=1, source_target_pairs={{0,16},{1,17},{2,18},{3,19},{4,20},{5,21},{6,22},{7,23},{8,24},{9,... | collective-permute-start | bytes 86024 | tf_op jit(solution)/shard_map/ppermute | solution.py:32
  50.7 0.5 collective-permute-start.13
  51.1 1.9 %fusion.11 = bf16[1,2,4,64,512]{4,3,2,1,0:T(8,128)(2,1)} fusion(bf16[2,256,576]{2,1,0:T(8,128)(2,1)S(1)} %bitcast.62, bf16[2,4,576]{2,1,0:T(4,128)(2,1)S(1)} %bitcast.70, f32[2,4,64]{2,1,0:T(4,128)S(1)} %fusion.50, f32[2,4,64,260]{3,2,1,0:T(8,128)S(1)} %fusion.10), kind=kOutput, calls=%fused_computation.16 | convolution fusion | flops 138042112 | bytes 2766848 | tf_op jit(solution)/shard_map/rshk,rkv->rshv/dot_general | solution.py:50
  53.3 3.0 %collective-permute-done.13 = bf16[4,3584]{1,0:T(4,128)(2,1)S(1)} collective-permute-done((bf16[4,3584]{1,0:T(4,128)(2,1)S(1)}, bf16[4,3584]{1,0:T(4,128)(2,1)S(1)}, u32[]{:S(2)}, u32[]{:S(2)}) %collective-permute-start.13) | collective-permute-done | bytes 28704 | tf_op jit(solution)/shard_map/ppermute | solution.py:32
  56.3 0.6 %fusion.31 = bf16[1,4,3584]{2,1,0:T(4,128)(2,1)} fusion(bf16[4,3584]{1,0:T(4,128)(2,1)S(1)} %collective-permute-done.13, bf16[4,3584]{1,0:T(4,128)(2,1)S(1)} %collective-permute-done.12, bf16[4,3584]{1,0:T(4,128)(2,1)S(1)} %collective-permute-done.11, bf16[16,3584]{1,0:T(8,128)(2,1)S(1)} %add_convert_fusion.1), kind=kLoop, calls=%fused_computation.37 | loop fusion | flops 114688 | bytes 143360 | tf_op jit(solution)/shard_map/broadcast_in_dim | solution.py:128
  (37 shorter events, 1.4 us)
Async XLA Ops:
  0.6 18.1 %copy-start = (bf16[1,32,16,576]{3,2,1,0:T(8,128)(2,1)S(1)}, bf16[1,32,16,576]{3,2,1,0:T(8,128)(2,1)}, u32[]{:S(2)}) copy-start(bf16[1,32,16,576]{3,2,1,0:T(8,128)(2,1)} %param.12) | copy-start | bytes 1769476
  0.6 23.8 %copy-start.1 = (s32[1,2,16]{2,1,0:T(2,128)S(1)}, s32[1,2,16]{2,1,0:T(2,128)}, u32[]{:S(2)}) copy-start(s32[1,2,16]{2,1,0:T(2,128)} %param.14) | copy-start | bytes 388
  0.7 23.8 %copy-start.2 = (s32[1,2]{1,0:T(1,128)S(1)}, s32[1,2]{1,0:T(1,128)}, u32[]{:S(2)}) copy-start(s32[1,2]{1,0:T(1,128)} %param.15) | copy-start | bytes 28
  2.4 5.7 %collective-permute-start = (bf16[4,3712]{1,0:T(4,128)(2,1)S(1)}, bf16[4,3712]{1,0:T(4,128)(2,1)S(1)}, u32[]{:S(2)}, u32[]{:S(2)}) collective-permute-start(bf16[4,3712]{1,0:T(4,128)(2,1)S(1)} %pad_maximum_fusion.2), channel_id=1, source_target_pairs={{0,8},{1,9},{2,10},{3,11},{4,12},{5,13},{6,14},{7,15},{8,0},{9,1},... | collective-permute-start | bytes 89096 | tf_op jit(solution)/shard_map/ppermute | solution.py:32
  5.5 5.3 %collective-permute-start.1 = (bf16[4,3712]{1,0:T(4,128)(2,1)S(1)}, bf16[4,3712]{1,0:T(4,128)(2,1)S(1)}, u32[]{:S(2)}, u32[]{:S(2)}) collective-permute-start(bf16[4,3712]{1,0:T(4,128)(2,1)S(1)} %pad_maximum_fusion.2), channel_id=1, source_target_pairs={{0,16},{1,17},{2,18},{3,19},{4,20},{5,21},{6,22},{7,23},{8,24},{9,... | collective-permute-start | bytes 89096 | tf_op jit(solution)/shard_map/ppermute | solution.py:32
  8.0 5.7 %collective-permute-start.2 = (bf16[4,3712]{1,0:T(4,128)(2,1)S(1)}, bf16[4,3712]{1,0:T(4,128)(2,1)S(1)}, u32[]{:S(2)}, u32[]{:S(2)}) collective-permute-start(bf16[4,3712]{1,0:T(4,128)(2,1)S(1)} %pad_maximum_fusion.2), channel_id=1, source_target_pairs={{0,24},{1,25},{2,26},{3,27},{4,28},{5,29},{6,30},{7,31},{8,16},{9,... | collective-permute-start | bytes 89096 | tf_op jit(solution)/shard_map/ppermute | solution.py:32
  14.6 9.3 %collective-permute-start.3 = (bf16[16,3712]{1,0:T(8,128)(2,1)S(1)}, bf16[16,3712]{1,0:T(8,128)(2,1)S(1)}, u32[]{:S(2)}, u32[]{:S(2)}) collective-permute-start(bf16[16,3712]{1,0:T(8,128)(2,1)S(1)} %pad_maximum_fusion.1), channel_id=1, source_target_pairs={{0,1},{1,0},{2,3},{3,2},{4,5},{5,4},{6,7},{7,6},{8,9},{9,8},{10,11... | collective-permute-start | bytes 356360 | tf_op jit(solution)/shard_map/ppermute | solution.py:32
  16.1 7.7 %collective-permute-start.4 = (bf16[16,3712]{1,0:T(8,128)(2,1)S(1)}, bf16[16,3712]{1,0:T(8,128)(2,1)S(1)}, u32[]{:S(2)}, u32[]{:S(2)}) collective-permute-start(bf16[16,3712]{1,0:T(8,128)(2,1)S(1)} %pad_maximum_fusion.1), channel_id=1, source_target_pairs={{0,4},{1,5},{2,6},{3,7},{4,0},{5,1},{6,2},{7,3},{8,12},{9,13},{10,... | collective-permute-start | bytes 356360 | tf_op jit(solution)/shard_map/ppermute | solution.py:32
  17.6 6.2 %collective-permute-start.5 = (bf16[16,3712]{1,0:T(8,128)(2,1)S(1)}, bf16[16,3712]{1,0:T(8,128)(2,1)S(1)}, u32[]{:S(2)}, u32[]{:S(2)}) collective-permute-start(bf16[16,3712]{1,0:T(8,128)(2,1)S(1)} %pad_maximum_fusion.1), channel_id=1, source_target_pairs={{0,5},{1,4},{2,7},{3,6},{4,1},{5,0},{6,3},{7,2},{8,13},{9,12},{10,... | collective-permute-start | bytes 356360 | tf_op jit(solution)/shard_map/ppermute | solution.py:32
  20.2 20.9 %all-to-all-start = ((bf16[16,2,16,576]{3,2,1,0:T(8,128)(2,1)}), bf16[16,2,16,576]{3,2,1,0:T(8,128)(2,1)S(1)}, u32[]{:S(2)}, u32[]{:S(2)}) async-start(bf16[16,2,16,576]{3,2,1,0:T(8,128)(2,1)} %bitcast.3), calls=%async_computation | async-start | bytes 1310720 | tf_op jit(solution)/shard_map/all_to_all | solution.py:75
  24.1 2.0 %collective-permute-start.6 = (bf16[64,3712]{1,0:T(8,128)(2,1)S(1)}, bf16[64,3712]{1,0:T(8,128)(2,1)}, u32[]{:S(2)}, u32[]{:S(2)}) collective-permute-start(bf16[64,3712]{1,0:T(8,128)(2,1)S(1)} %concatenate.24), channel_id=1, source_target_pairs={{0,2},{1,3},{2,0},{3,1},{4,6},{5,7},{6,4},{7,5},{8,10},{9,11},{10,... | collective-permute-start | bytes 1425416 | tf_op jit(solution)/shard_map/ppermute | solution.py:32
  35.5 6.3 %copy-start.3 = (bf16[1,2,4,576]{3,2,1,0:T(4,128)(2,1)S(1)}, bf16[1,2,4,576]{3,2,1,0:T(4,128)(2,1)}, u32[]{:S(2)}) copy-start(bf16[1,2,4,576]{3,2,1,0:T(4,128)(2,1)} %param.16) | copy-start | bytes 27652
  35.6 1.9 %collective-permute-start.7 = (bf16[64,3584]{1,0:T(8,128)(2,1)S(1)}, bf16[64,3584]{1,0:T(8,128)(2,1)S(1)}, u32[]{:S(2)}, u32[]{:S(2)}) collective-permute-start(bf16[64,3584]{1,0:T(8,128)(2,1)S(1)} %slice.56), channel_id=1, source_target_pairs={{0,2},{1,3},{2,0},{3,1},{4,6},{5,7},{6,4},{7,5},{8,10},{9,11},{10,... | collective-permute-start | bytes 1376264 | tf_op jit(solution)/shard_map/ppermute | solution.py:32
  37.6 7.7 %collective-permute-start.10 = (bf16[16,3584]{1,0:T(8,128)(2,1)S(1)}, bf16[16,3584]{1,0:T(8,128)(2,1)S(1)}, u32[]{:S(2)}, u32[]{:S(2)}) collective-permute-start(bf16[16,3584]{1,0:T(8,128)(2,1)S(1)} %get-tuple-element.5), channel_id=1, source_target_pairs={{0,5},{1,4},{2,7},{3,6},{4,1},{5,0},{6,3},{7,2},{8,13},{9,12},{10,... | collective-permute-start | bytes 344072 | tf_op jit(solution)/shard_map/ppermute | solution.py:32
  40.4 6.2 %collective-permute-start.8 = (bf16[16,3584]{1,0:T(8,128)(2,1)S(1)}, bf16[16,3584]{1,0:T(8,128)(2,1)S(1)}, u32[]{:S(2)}, u32[]{:S(2)}) collective-permute-start(bf16[16,3584]{1,0:T(8,128)(2,1)S(1)} %get-tuple-element.4), channel_id=1, source_target_pairs={{0,1},{1,0},{2,3},{3,2},{4,5},{5,4},{6,7},{7,6},{8,9},{9,8},{10,11... | collective-permute-start | bytes 344072 | tf_op jit(solution)/shard_map/ppermute | solution.py:32
  40.9 5.6 %collective-permute-start.9 = (bf16[16,3584]{1,0:T(8,128)(2,1)S(1)}, bf16[16,3584]{1,0:T(8,128)(2,1)S(1)}, u32[]{:S(2)}, u32[]{:S(2)}) collective-permute-start(bf16[16,3584]{1,0:T(8,128)(2,1)S(1)} %get-tuple-element.6), channel_id=1, source_target_pairs={{0,4},{1,5},{2,6},{3,7},{4,0},{5,1},{6,2},{7,3},{8,12},{9,13},{10,... | collective-permute-start | bytes 344072 | tf_op jit(solution)/shard_map/ppermute | solution.py:32
  46.7 6.4 %collective-permute-start.11 = (bf16[4,3584]{1,0:T(4,128)(2,1)S(1)}, bf16[4,3584]{1,0:T(4,128)(2,1)S(1)}, u32[]{:S(2)}, u32[]{:S(2)}) collective-permute-start(bf16[4,3584]{1,0:T(4,128)(2,1)S(1)} %get-tuple-element.7), channel_id=1, source_target_pairs={{0,8},{1,9},{2,10},{3,11},{4,12},{5,13},{6,14},{7,15},{8,0},{9,1},... | collective-permute-start | bytes 86024 | tf_op jit(solution)/shard_map/ppermute | solution.py:32
  48.2 5.0 %collective-permute-start.12 = (bf16[4,3584]{1,0:T(4,128)(2,1)S(1)}, bf16[4,3584]{1,0:T(4,128)(2,1)S(1)}, u32[]{:S(2)}, u32[]{:S(2)}) collective-permute-start(bf16[4,3584]{1,0:T(4,128)(2,1)S(1)} %get-tuple-element.9), channel_id=1, source_target_pairs={{0,16},{1,17},{2,18},{3,19},{4,20},{5,21},{6,22},{7,23},{8,24},{9,... | collective-permute-start | bytes 86024 | tf_op jit(solution)/shard_map/ppermute | solution.py:32
  50.7 5.7 %collective-permute-start.13 = (bf16[4,3584]{1,0:T(4,128)(2,1)S(1)}, bf16[4,3584]{1,0:T(4,128)(2,1)S(1)}, u32[]{:S(2)}, u32[]{:S(2)}) collective-permute-start(bf16[4,3584]{1,0:T(4,128)(2,1)S(1)} %get-tuple-element.8), channel_id=1, source_target_pairs={{0,24},{1,25},{2,26},{3,27},{4,28},{5,29},{6,30},{7,31},{8,16},{9,... | collective-permute-start | bytes 86024 | tf_op jit(solution)/shard_map/ppermute | solution.py:32

commit v3 on v1

--- a/solution.py
+++ b/solution.py
@@ -6,6 +6,30 @@
 VDIM = 512
 SCALE = 192.0 ** (-0.5)
 RANK = ("dev", "section", "tp")
+
+
+def steps_of(peers, blocks):
+    low = blocks.bit_length() - 1
+    bits = peers.bit_length() - 1
+    far = [low + bit for bit in range(2, bits)]
+    near = list(range(low)) + [low + bit for bit in range(1, min(bits, 2))]
+    last = [low + bit for bit in range(min(bits, 1))]
+    return far, near, last
+
+
+def exchange(value, bit):
+    count = lax.axis_size(RANK)
+    return lax.ppermute(value, RANK, [(at, at ^ (1 << bit)) for at in range(count)])
+
+
+def spread(value, bit):
+    return lax.optimization_barrier(jnp.concatenate([value, exchange(value, bit)], axis=0))
+
+
+def collect(value, bit):
+    half = value.shape[0] // 2
+    kept = value[:half].astype(jnp.float32) + exchange(value[half:], bit).astype(jnp.float32)
+    return kept.astype(jnp.bfloat16)
 
 
 def attend(queries, new_latent, cache, lengths):
@@ -48,15 +72,6 @@
     page_len, width_lat = (pages.shape[1], pages.shape[2])
     capp = outgoing_slots.shape[0] // peers
     picked_pages = pages[jnp.maximum(outgoing_slots, 0)]
-    arrived = lax.all_to_all(
-        picked_pages.reshape(peers, capp, page_len, width_lat),
-        "dev",
-        split_axis=0,
-        concat_axis=0,
-        tiled=True,
-    )
-    arrived = arrived.reshape(peers * capp, page_len, width_lat)
-
     owned = expert_gate.shape[0]
     experts = peers * owned
     rows = routing.shape[1]
@@ -68,7 +83,28 @@
     extra = jnp.concatenate([high, low], axis=1)
     pad = -extra.shape[1] % 128
     packed = jnp.concatenate([moe_rows[0], jnp.pad(extra, ((0, 0), (0, pad)))], axis=1)
-    pooled = lax.all_gather(packed, RANK, axis=0, tiled=True)
+    far, near, last = steps_of(peers, lax.axis_size(("section", "tp")))
+    pooled = packed[None]
+    for bit in far:
+        pooled = spread(pooled, bit)
+    half = pooled.shape[0] // 2
+    one, two = pooled[:half], pooled[half:]
+    for turn, (bit, other) in enumerate(zip(near, near[::-1])):
+        if turn == len(near) - 1:
+            one, two, picked_pages = lax.optimization_barrier((one, two, picked_pages))
+        one, two = spread(one, bit), spread(two, other)
+    arrived = lax.all_to_all(
+        picked_pages.reshape(peers, capp, page_len, width_lat),
+        "dev",
+        split_axis=0,
+        concat_axis=0,
+        tiled=True,
+    )
+    arrived = arrived.reshape(peers * capp, page_len, width_lat)
+    pooled = jnp.concatenate([one, two], axis=0)
+    for bit in last:
+        pooled = spread(pooled, bit)
+    pooled = pooled.reshape(-1, pooled.shape[-1])
     every = pooled[:, :width]
     first = lax.axis_index("dev") * owned
     total = None
@@ -82,7 +118,17 @@
         hidden = (jax.nn.silu(gate) * up).astype(jnp.bfloat16)
         term = jnp.dot(hidden, expert_down[own], preferred_element_type=jnp.float32) * weight
         total = term if total is None else total + term
-    mixed = lax.psum_scatter(total.astype(jnp.bfloat16), RANK, scatter_dimension=0, tiled=True)
+    mixed = total.astype(jnp.bfloat16).reshape(-1, rows, width)
+    for bit in last[::-1]:
+        mixed = collect(mixed, bit)
+    half = mixed.shape[0] // 2
+    one, two = mixed[:half], mixed[half:]
+    for bit, other in zip(near[::-1], near):
+        one, two = collect(one, bit), collect(two, other)
+    mixed = jnp.concatenate([one, two], axis=0)
+    for bit in far[::-1]:
+        mixed = collect(mixed, bit)
+    mixed = mixed[0]
 
     table = page_table[0]
     requests, most_pages = table.shape

time: 238 us -> 79.3 us (0.33)
  waiting for transfers between devices: 125 us -> 24.8 us
  blocking collectives: 75.4 us -> 0 us
  starting transfers between devices: 3.63 us -> 29.1 us
  between operations: 14.2 us -> 0.93 us
  other arithmetic: 1.81 us -> 6.23 us
    unnamed x2 -> x0, waiting for transfers between devices: 125 us -> none
    all_gather x1 -> x0, blocking collectives: 75.4 us -> none  [body(): pooled = lax.all_gather(packed, RANK, axis=0, tiled=True)]
    ppermute x0 -> x14, starting transfers between devices: none -> 22.7 us  [exchange(): lax.ppermute(value, RANK, [(at, at ^ 1 << bit) for at in range(count)])]
    ppermute x0 -> x14, waiting for transfers between devices: none -> 13.7 us  [exchange(): lax.ppermute(value, RANK, [(at, at ^ 1 << bit) for at in range(count)])]
    all_to_all x1, waiting for transfers between devices: 0.01 us -> 11 us  [body(): lax.all_to_all(picked_pages.reshape(peers, capp, page_len, width_lat), 'd...]
    all_to_all x1, starting transfers between devices: 3.59 us -> 6.49 us  [body(): lax.all_to_all(picked_pages.reshape(peers, capp, page_len, width_lat), 'd...]
  transfers between devices with their start and end apart: 2 -> 15, of which waited for: 1 -> 7; matrix products, arithmetic and copies ran while one was open for 1% -> 15% of each run, Pallas kernels for 0% -> 0%
where the time goes in v3:
time: 79.3 us; the launch traced here: 78.8 us
  starting transfers between devices  29.1 us (37%)
  waiting for transfers between devices  24.8 us (31%)
  matrix products  13.7 us (17%)
  other arithmetic  6.23 us (8%)
  local copies, waits for them, and re-layouts  4.06 us (5%)
  between operations  0.93 us (1%)
    ppermute x14, starting transfers between devices, exchange(): lax.ppermute(value, RANK, [(at, at ^ 1 << bit) for at in range(count)])  22.7 us
    ppermute x14, waiting for transfers between devices, exchange(): lax.ppermute(value, RANK, [(at, at ^ 1 << bit) for at in range(count)])  13.7 us
    all_to_all x1, waiting for transfers between devices, body(): lax.all_to_all(picked_pages.reshape(peers, capp, page_len, width_lat), 'd...  11 us
    all_to_all x1, starting transfers between devices, body(): lax.all_to_all(picked_pages.reshape(peers, capp, page_len, width_lat), 'd...  6.49 us
    dot_general x1, matrix products, body(): jnp.dot(hidden, expert_down[own], preferred_element_type=jnp.float32)  4.4 us
    dot_general x1, matrix products, attend(): jnp.einsum('rshk,rkv->rshv', weights, values, preferred_element_type=jnp....  3.3 us
    dot_general x1, matrix products, body(): gate = jnp.dot(every, expert_gate[own], preferred_element_type=jnp.float32)  2.7 us
    dot_general x1, matrix products, attend(): jnp.einsum('rshl,rkl->rshk', queries, keys, preferred_element_type=jnp.fl...  2.55 us
  transfers between devices with their start and end apart: 15, of which 7 were waited for; matrix products, arithmetic and copies ran while one was open for 15% of the time, Pallas kernels for 0%

profile of v3, /device:TPU:0, one launch (start us, length us, event | category | flops | bytes accessed | tf_op | source)
XLA Modules:
  0.0 78.8 jit_solution(12560192062989701447)
XLA Ops:
  0.7 0.8 %select_reduce_fusion = f32[4,16]{1,0:T(4,128)S(1)} fusion(f32[4,8]{1,0:T(4,128)} %bitcast.68, s32[4,8]{1,0:T(4,128)} %bitcast.69), kind=kLoop, calls=%fused_computation.54 | loop fusion | flops 1472 | bytes 512 | tf_op jit(solution)/shard_map/reduce_sum | solution.py:80
  1.6 0.8 maximum_bitcast_fusion
  2.4 3.1 %collective-permute-start = (bf16[1,4,3712]{2,1,0:T(4,128)(2,1)S(1)}, bf16[1,4,3712]{2,1,0:T(4,128)(2,1)S(1)}, u32[]{:S(2)}, u32[]{:S(2)}) collective-permute-start(bf16[1,4,3712]{2,1,0:T(4,128)(2,1)S(1)} %maximum_bitcast_fusion), channel_id=1, source_target_pairs={{0,8},{1,9},{2,10},{3,11},{4,12},{5,13},{6,14},{7,15},{8,0},{9,1},... | collective-permute-start | bytes 89096 | tf_op jit(solution)/shard_map/ppermute | solution.py:22
  5.4 1.9 %collective-permute-done = bf16[1,4,3712]{2,1,0:T(4,128)(2,1)S(1)} collective-permute-done((bf16[1,4,3712]{2,1,0:T(4,128)(2,1)S(1)}, bf16[1,4,3712]{2,1,0:T(4,128)(2,1)S(1)}, u32[]{:S(2)}, u32[]{:S(2)}) %collective-permute-start) | collective-permute-done | bytes 29728 | tf_op jit(solution)/shard_map/ppermute | solution.py:22
  7.4 3.1 %collective-permute-start.1 = (bf16[2,4,3712]{2,1,0:T(4,128)(2,1)S(1)}, bf16[2,4,3712]{2,1,0:T(4,128)(2,1)S(1)}, u32[]{:S(2)}, u32[]{:S(2)}) collective-permute-start(bf16[2,4,3712]{2,1,0:T(4,128)(2,1)S(1)} %pad_maximum_fusion.8), channel_id=1, source_target_pairs={{0,16},{1,17},{2,18},{3,19},{4,20},{5,21},{6,22},{7,23},{8,24},{9,... | collective-permute-start | bytes 178184 | tf_op jit(solution)/shard_map/ppermute | solution.py:22
  10.5 0.7 maximum_bitcast_fusion.1
  11.1 1.5 %collective-permute-done.1 = bf16[2,4,3712]{2,1,0:T(4,128)(2,1)S(1)} collective-permute-done((bf16[2,4,3712]{2,1,0:T(4,128)(2,1)S(1)}, bf16[2,4,3712]{2,1,0:T(4,128)(2,1)S(1)}, u32[]{:S(2)}, u32[]{:S(2)}) %collective-permute-start.1) | collective-permute-done | bytes 59424 | tf_op jit(solution)/shard_map/ppermute | solution.py:22
  12.8 1.9 %collective-permute-start.2 = (bf16[2,4,3712]{2,1,0:T(4,128)(2,1)S(1)}, bf16[2,4,3712]{2,1,0:T(4,128)(2,1)S(1)}, u32[]{:S(2)}, u32[]{:S(2)}) collective-permute-start(bf16[2,4,3712]{2,1,0:T(4,128)(2,1)S(1)} %get-tuple-element.19), channel_id=1, source_target_pairs={{0,1},{1,0},{2,3},{3,2},{4,5},{5,4},{6,7},{7,6},{8,9},{9,8},{10,11... | collective-permute-start | bytes 178184 | tf_op jit(solution)/shard_map/ppermute | solution.py:22
  14.7 1.5 %gather_fusion = bf16[32,16,576]{2,1,0:T(8,128)(2,1)} fusion(bf16[32,16,576]{2,1,0:T(8,128)(2,1)S(1)} %bitcast.62, s32[1024]{0:T(1024)S(1)} %pad_clamp_fusion.1), kind=kCustom, calls=%fused_computation | custom fusion | bytes 1179776 | tf_op jit(solution)/shard_map/gather | solution.py:74
  16.1 1.5 %collective-permute-start.3 = (bf16[2,4,3712]{2,1,0:T(4,128)(2,1)S(1)}, bf16[2,4,3712]{2,1,0:T(4,128)(2,1)S(1)}, u32[]{:S(2)}, u32[]{:S(2)}) collective-permute-start(bf16[2,4,3712]{2,1,0:T(4,128)(2,1)S(1)} %get-tuple-element.18), channel_id=1, source_target_pairs={{0,4},{1,5},{2,6},{3,7},{4,0},{5,1},{6,2},{7,3},{8,12},{9,13},{10,... | collective-permute-start | bytes 178184 | tf_op jit(solution)/shard_map/ppermute | solution.py:22
  17.8 3.2 %collective-permute-done.3 = bf16[2,4,3712]{2,1,0:T(4,128)(2,1)S(1)} collective-permute-done((bf16[2,4,3712]{2,1,0:T(4,128)(2,1)S(1)}, bf16[2,4,3712]{2,1,0:T(4,128)(2,1)S(1)}, u32[]{:S(2)}, u32[]{:S(2)}) %collective-permute-start.3) | collective-permute-done | bytes 59424 | tf_op jit(solution)/shard_map/ppermute | solution.py:22
  21.1 1.6 %collective-permute-start.4 = (bf16[4,4,3712]{2,1,0:T(4,128)(2,1)S(1)}, bf16[4,4,3712]{2,1,0:T(4,128)(2,1)S(1)}, u32[]{:S(2)}, u32[]{:S(2)}) collective-permute-start(bf16[4,4,3712]{2,1,0:T(4,128)(2,1)S(1)} %pad_maximum_fusion.6), channel_id=1, source_target_pairs={{0,4},{1,5},{2,6},{3,7},{4,0},{5,1},{6,2},{7,3},{8,12},{9,13},{10,... | collective-permute-start | bytes 356360 | tf_op jit(solution)/shard_map/ppermute | solution.py:22
  22.7 3.2 %collective-permute-done.5 = bf16[4,4,3712]{2,1,0:T(4,128)(2,1)S(1)} collective-permute-done((bf16[4,4,3712]{2,1,0:T(4,128)(2,1)S(1)}, bf16[4,4,3712]{2,1,0:T(4,128)(2,1)S(1)}, u32[]{:S(2)}, u32[]{:S(2)}) %collective-permute-start.5) | collective-permute-done | bytes 118816 | tf_op jit(solution)/shard_map/ppermute | solution.py:22
  26.8 1.7 %collective-permute-done.6 = bf16[16,4,3712]{2,1,0:T(4,128)(2,1)S(1)} collective-permute-done((bf16[16,4,3712]{2,1,0:T(4,128)(2,1)S(1)}, bf16[16,4,3712]{2,1,0:T(4,128)(2,1)S(1)}, u32[]{:S(2)}, u32[]{:S(2)}) %collective-permute-start.6) | collective-permute-done | bytes 475168 | tf_op jit(solution)/shard_map/ppermute | solution.py:22
  28.5 0.6 pad_maximum_fusion
  29.7 2.7 %fusion.5 = f32[128,512]{1,0:T(8,128)S(1)} fusion(bf16[1,3584,512]{2,1,0:T(8,128)(2,1)} %param.21, bf16[128,3712]{1,0:T(8,128)(2,1)S(1)} %reshape.118), kind=kOutput, calls=%fused_computation.8 | convolution fusion | flops 469762048 | bytes 4849664 | tf_op jit(solution)/shard_map/dot_general | solution.py:116
  32.4 4.4 %fusion.1 = bf16[128,3584]{1,0:T(8,128)(2,1)S(1)} fusion(bf16[1,512,3584]{2,1,0:T(8,128)(2,1)} %param.23, f32[128]{0:T(128)S(1)} %add_bitcast_fusion, bf16[1,3584,512]{2,1,0:T(8,128)(2,1)} %param.22, bf16[128,3712]{1,0:T(8,128)(2,1)S(1)} %reshape.118, f32[128,512]{1,0:T(8,128)S(1)} %fusion.5), kind=kOutput, calls=%fused_computation.4 | convolution fusion | flops 940834816 | bytes 9437696 | tf_op jit(solution)/shard_map/dot_general | solution.py:119
  36.9 0.9 %slice.64 = bf16[16,4,3584]{2,1,0:T(4,128)(2,1)} reshape(bf16[64,3584]{1,0:T(8,128)(2,1)S(1)} %get-tuple-element.12) | data formatting | bytes 917504 | tf_op jit(solution)/shard_map/slice | solution.py:31
  38.0 6.5 %all-to-all-start = ((bf16[16,2,16,576]{3,2,1,0:T(8,128)(2,1)}), bf16[16,2,16,576]{3,2,1,0:T(8,128)(2,1)S(1)}, u32[]{:S(2)}, u32[]{:S(2)}) async-start(bf16[16,2,16,576]{3,2,1,0:T(8,128)(2,1)} %bitcast.7), calls=%async_computation | async-start | bytes 1310720 | tf_op jit(solution)/shard_map/all_to_all | solution.py:96
  44.8 1.3 %add_convert_fusion = bf16[16,4,3584]{2,1,0:T(4,128)(2,1)S(1)} fusion(f32[16,4,3584]{2,1,0:T(4,128)S(1)} %reshape.119, bf16[16,4,3584]{2,1,0:T(4,128)(2,1)} %collective-permute-done.7), kind=kLoop, calls=%fused_computation.22 | loop fusion | flops 688128 | bytes 1835008 | tf_op jit(solution)/shard_map/convert_element_type | solution.py:32
  46.1 2.0 %collective-permute-start.8 = (bf16[4,4,3584]{2,1,0:T(4,128)(2,1)S(1)}, bf16[4,4,3584]{2,1,0:T(4,128)(2,1)S(1)}, u32[]{:S(2)}, u32[]{:S(2)}) collective-permute-start(bf16[4,4,3584]{2,1,0:T(4,128)(2,1)S(1)} %get-tuple-element.16), channel_id=1, source_target_pairs={{0,4},{1,5},{2,6},{3,7},{4,0},{5,1},{6,2},{7,3},{8,12},{9,13},{10,... | collective-permute-start | bytes 344072 | tf_op jit(solution)/shard_map/ppermute | solution.py:22
  48.1 1.8 %collective-permute-start.10 = (bf16[4,4,3584]{2,1,0:T(4,128)(2,1)S(1)}, bf16[4,4,3584]{2,1,0:T(4,128)(2,1)S(1)}, u32[]{:S(2)}, u32[]{:S(2)}) collective-permute-start(bf16[4,4,3584]{2,1,0:T(4,128)(2,1)S(1)} %get-tuple-element.17), channel_id=1, source_target_pairs={{0,1},{1,0},{2,3},{3,2},{4,5},{5,4},{6,7},{7,6},{8,9},{9,8},{10,11... | collective-permute-start | bytes 344072 | tf_op jit(solution)/shard_map/ppermute | solution.py:22
  50.0 11.0 %all-to-all-done = bf16[16,2,16,576]{3,2,1,0:T(8,128)(2,1)S(1)} async-done(((bf16[16,2,16,576]{3,2,1,0:T(8,128)(2,1)}), bf16[16,2,16,576]{3,2,1,0:T(8,128)(2,1)S(1)}, u32[]{:S(2)}, u32[]{:S(2)}) %all-to-all-start) | async-done | bytes 589856 | tf_op jit(solution)/shard_map/all_to_all | solution.py:96
  61.1 0.7 gather_fusion.1
  61.9 0.8 %collective-permute-start.11 = (bf16[2,4,3584]{2,1,0:T(4,128)(2,1)S(1)}, bf16[2,4,3584]{2,1,0:T(4,128)(2,1)S(1)}, u32[]{:S(2)}, u32[]{:S(2)}) collective-permute-start(bf16[2,4,3584]{2,1,0:T(4,128)(2,1)S(1)} %slice.93), channel_id=1, source_target_pairs={{0,4},{1,5},{2,6},{3,7},{4,0},{5,1},{6,2},{7,3},{8,12},{9,13},{10,... | collective-permute-start | bytes 172040 | tf_op jit(solution)/shard_map/ppermute | solution.py:22
  62.8 2.5 %fusion.10 = f32[2,4,64,260]{3,2,1,0:T(8,128)} fusion(bf16[2,4,576]{2,1,0:T(4,128)(2,1)S(1)} %bitcast.71, bf16[1,2,4,64,576]{4,3,2,1,0:T(8,128)(2,1)} %param.17, bf16[2,256,576]{2,1,0:T(8,128)(2,1)S(1)} %bitcast.64, pred[2,4,260]{2,1,0:T(4,128)(4,1)S(1)} %broadcast_or_fusion), kind=kOutput, calls=%fused_computation.15 | convolution fusion | flops 154818560 | bytes 1723424 | tf_op jit(solution)/shard_map/rshl,rkl->rshk/dot_general | solution.py:39
  65.3 1.9 %collective-permute-start.9 = (bf16[2,4,3584]{2,1,0:T(4,128)(2,1)S(1)}, bf16[2,4,3584]{2,1,0:T(4,128)(2,1)S(1)}, u32[]{:S(2)}, u32[]{:S(2)}) collective-permute-start(bf16[2,4,3584]{2,1,0:T(4,128)(2,1)S(1)} %slice.89), channel_id=1, source_target_pairs={{0,1},{1,0},{2,3},{3,2},{4,5},{5,4},{6,7},{7,6},{8,9},{9,8},{10,11... | collective-permute-start | bytes 172040 | tf_op jit(solution)/shard_map/ppermute | solution.py:22
  67.3 2.3 %collective-permute-start.12 = (bf16[2,4,3584]{2,1,0:T(4,128)(2,1)S(1)}, bf16[2,4,3584]{2,1,0:T(4,128)(2,1)S(1)}, u32[]{:S(2)}, u32[]{:S(2)}) collective-permute-start(bf16[2,4,3584]{2,1,0:T(4,128)(2,1)S(1)} %add_convert_fusion.4), channel_id=1, source_target_pairs={{0,16},{1,17},{2,18},{3,19},{4,20},{5,21},{6,22},{7,23},{8,24},{9,... | collective-permute-start | bytes 172040 | tf_op jit(solution)/shard_map/ppermute | solution.py:22
  69.6 0.7 fusion.56
  70.3 2.1 %collective-permute-done.12 = bf16[2,4,3584]{2,1,0:T(4,128)(2,1)S(1)} collective-permute-done((bf16[2,4,3584]{2,1,0:T(4,128)(2,1)S(1)}, bf16[2,4,3584]{2,1,0:T(4,128)(2,1)S(1)}, u32[]{:S(2)}, u32[]{:S(2)}) %collective-permute-start.12) | collective-permute-done | bytes 57376 | tf_op jit(solution)/shard_map/ppermute | solution.py:22
  72.5 2.4 %collective-permute-start.13 = (bf16[1,4,3584]{2,1,0:T(4,128)(2,1)S(1)}, bf16[1,4,3584]{2,1,0:T(4,128)(2,1)S(1)}, u32[]{:S(2)}, u32[]{:S(2)}) collective-permute-start(bf16[1,4,3584]{2,1,0:T(4,128)(2,1)S(1)} %slice.95), channel_id=1, source_target_pairs={{0,8},{1,9},{2,10},{3,11},{4,12},{5,13},{6,14},{7,15},{8,0},{9,1},... | collective-permute-start | bytes 86024 | tf_op jit(solution)/shard_map/ppermute | solution.py:22
  74.9 3.3 %fusion.11 = bf16[1,2,4,64,512]{4,3,2,1,0:T(8,128)(2,1)} fusion(bf16[2,256,576]{2,1,0:T(8,128)(2,1)S(1)} %bitcast.66, bf16[2,4,576]{2,1,0:T(4,128)(2,1)S(1)} %bitcast.73, f32[2,4,64]{2,1,0:T(4,128)S(1)} %fusion.56, f32[2,4,64,260]{3,2,1,0:T(8,128)} %fusion.10), kind=kOutput, calls=%fused_computation.16 | convolution fusion | flops 138042112 | bytes 2698240 | tf_op jit(solution)/shard_map/rshk,rkv->rshv/dot_general | solution.py:50
  (55 shorter events, 3.4 us)
Async XLA Ops:
  0.6 14.0 %copy-start = (bf16[1,32,16,576]{3,2,1,0:T(8,128)(2,1)S(1)}, bf16[1,32,16,576]{3,2,1,0:T(8,128)(2,1)}, u32[]{:S(2)}) copy-start(bf16[1,32,16,576]{3,2,1,0:T(8,128)(2,1)} %param.12) | copy-start | bytes 1769476
  0.6 26.1 %copy-start.2 = (s32[1,2]{1,0:T(1,128)S(1)}, s32[1,2]{1,0:T(1,128)}, u32[]{:S(2)}) copy-start(s32[1,2]{1,0:T(1,128)} %param.15) | copy-start | bytes 28
  2.4 5.0 %collective-permute-start = (bf16[1,4,3712]{2,1,0:T(4,128)(2,1)S(1)}, bf16[1,4,3712]{2,1,0:T(4,128)(2,1)S(1)}, u32[]{:S(2)}, u32[]{:S(2)}) collective-permute-start(bf16[1,4,3712]{2,1,0:T(4,128)(2,1)S(1)} %maximum_bitcast_fusion), channel_id=1, source_target_pairs={{0,8},{1,9},{2,10},{3,11},{4,12},{5,13},{6,14},{7,15},{8,0},{9,1},... | collective-permute-start | bytes 89096 | tf_op jit(solution)/shard_map/ppermute | solution.py:22
  7.4 5.3 %collective-permute-start.1 = (bf16[2,4,3712]{2,1,0:T(4,128)(2,1)S(1)}, bf16[2,4,3712]{2,1,0:T(4,128)(2,1)S(1)}, u32[]{:S(2)}, u32[]{:S(2)}) collective-permute-start(bf16[2,4,3712]{2,1,0:T(4,128)(2,1)S(1)} %pad_maximum_fusion.8), channel_id=1, source_target_pairs={{0,16},{1,17},{2,18},{3,19},{4,20},{5,21},{6,22},{7,23},{8,24},{9,... | collective-permute-start | bytes 178184 | tf_op jit(solution)/shard_map/ppermute | solution.py:22
  12.8 4.9 %collective-permute-start.2 = (bf16[2,4,3712]{2,1,0:T(4,128)(2,1)S(1)}, bf16[2,4,3712]{2,1,0:T(4,128)(2,1)S(1)}, u32[]{:S(2)}, u32[]{:S(2)}) collective-permute-start(bf16[2,4,3712]{2,1,0:T(4,128)(2,1)S(1)} %get-tuple-element.19), channel_id=1, source_target_pairs={{0,1},{1,0},{2,3},{3,2},{4,5},{5,4},{6,7},{7,6},{8,9},{9,8},{10,11... | collective-permute-start | bytes 178184 | tf_op jit(solution)/shard_map/ppermute | solution.py:22
  16.1 4.8 %collective-permute-start.3 = (bf16[2,4,3712]{2,1,0:T(4,128)(2,1)S(1)}, bf16[2,4,3712]{2,1,0:T(4,128)(2,1)S(1)}, u32[]{:S(2)}, u32[]{:S(2)}) collective-permute-start(bf16[2,4,3712]{2,1,0:T(4,128)(2,1)S(1)} %get-tuple-element.18), channel_id=1, source_target_pairs={{0,4},{1,5},{2,6},{3,7},{4,0},{5,1},{6,2},{7,3},{8,12},{9,13},{10,... | collective-permute-start | bytes 178184 | tf_op jit(solution)/shard_map/ppermute | solution.py:22
  21.1 4.9 %collective-permute-start.5 = (bf16[4,4,3712]{2,1,0:T(4,128)(2,1)S(1)}, bf16[4,4,3712]{2,1,0:T(4,128)(2,1)S(1)}, u32[]{:S(2)}, u32[]{:S(2)}) collective-permute-start(bf16[4,4,3712]{2,1,0:T(4,128)(2,1)S(1)} %pad_maximum_fusion.7), channel_id=1, source_target_pairs={{0,1},{1,0},{2,3},{3,2},{4,5},{5,4},{6,7},{7,6},{8,9},{9,8},{10,11... | collective-permute-start | bytes 356360 | tf_op jit(solution)/shard_map/ppermute | solution.py:22
  21.1 5.0 %collective-permute-start.4 = (bf16[4,4,3712]{2,1,0:T(4,128)(2,1)S(1)}, bf16[4,4,3712]{2,1,0:T(4,128)(2,1)S(1)}, u32[]{:S(2)}, u32[]{:S(2)}) collective-permute-start(bf16[4,4,3712]{2,1,0:T(4,128)(2,1)S(1)} %pad_maximum_fusion.6), channel_id=1, source_target_pairs={{0,4},{1,5},{2,6},{3,7},{4,0},{5,1},{6,2},{7,3},{8,12},{9,13},{10,... | collective-permute-start | bytes 356360 | tf_op jit(solution)/shard_map/ppermute | solution.py:22
  26.6 1.9 %collective-permute-start.6 = (bf16[16,4,3712]{2,1,0:T(4,128)(2,1)S(1)}, bf16[16,4,3712]{2,1,0:T(4,128)(2,1)S(1)}, u32[]{:S(2)}, u32[]{:S(2)}) collective-permute-start(bf16[16,4,3712]{2,1,0:T(4,128)(2,1)S(1)} %pad_maximum_fusion.2), channel_id=1, source_target_pairs={{0,2},{1,3},{2,0},{3,1},{4,6},{5,7},{6,4},{7,5},{8,10},{9,11},{10,... | collective-permute-start | bytes 1425416 | tf_op jit(solution)/shard_map/ppermute | solution.py:22
  36.9 13.0 %copy-start.1 = (s32[1,2,16]{2,1,0:T(2,128)S(1)}, s32[1,2,16]{2,1,0:T(2,128)}, u32[]{:S(2)}) copy-start(s32[1,2,16]{2,1,0:T(2,128)} %param.14) | copy-start | bytes 388
  37.8 7.0 %collective-permute-start.7 = (bf16[16,4,3584]{2,1,0:T(4,128)(2,1)}, bf16[16,4,3584]{2,1,0:T(4,128)(2,1)}, u32[]{:S(2)}, u32[]{:S(2)}) collective-permute-start(bf16[16,4,3584]{2,1,0:T(4,128)(2,1)} %slice.64), channel_id=1, source_target_pairs={{0,2},{1,3},{2,0},{3,1},{4,6},{5,7},{6,4},{7,5},{8,10},{9,11},{10,... | collective-permute-start | bytes 1376264 | tf_op jit(solution)/shard_map/ppermute | solution.py:22
  38.0 24.8 %copy-start.4 = (bf16[1,2,4,576]{3,2,1,0:T(4,128)(2,1)S(1)}, bf16[1,2,4,576]{3,2,1,0:T(4,128)(2,1)}, u32[]{:S(2)}) copy-start(bf16[1,2,4,576]{3,2,1,0:T(4,128)(2,1)} %param.16) | copy-start | bytes 27652
  38.0 23.1 %all-to-all-start = ((bf16[16,2,16,576]{3,2,1,0:T(8,128)(2,1)}), bf16[16,2,16,576]{3,2,1,0:T(8,128)(2,1)S(1)}, u32[]{:S(2)}, u32[]{:S(2)}) async-start(bf16[16,2,16,576]{3,2,1,0:T(8,128)(2,1)} %bitcast.7), calls=%async_computation | async-start | bytes 1310720 | tf_op jit(solution)/shard_map/all_to_all | solution.py:96
  46.1 15.7 %collective-permute-start.8 = (bf16[4,4,3584]{2,1,0:T(4,128)(2,1)S(1)}, bf16[4,4,3584]{2,1,0:T(4,128)(2,1)S(1)}, u32[]{:S(2)}, u32[]{:S(2)}) collective-permute-start(bf16[4,4,3584]{2,1,0:T(4,128)(2,1)S(1)} %get-tuple-element.16), channel_id=1, source_target_pairs={{0,4},{1,5},{2,6},{3,7},{4,0},{5,1},{6,2},{7,3},{8,12},{9,13},{10,... | collective-permute-start | bytes 344072 | tf_op jit(solution)/shard_map/ppermute | solution.py:22
  48.1 13.7 %collective-permute-start.10 = (bf16[4,4,3584]{2,1,0:T(4,128)(2,1)S(1)}, bf16[4,4,3584]{2,1,0:T(4,128)(2,1)S(1)}, u32[]{:S(2)}, u32[]{:S(2)}) collective-permute-start(bf16[4,4,3584]{2,1,0:T(4,128)(2,1)S(1)} %get-tuple-element.17), channel_id=1, source_target_pairs={{0,1},{1,0},{2,3},{3,2},{4,5},{5,4},{6,7},{7,6},{8,9},{9,8},{10,11... | collective-permute-start | bytes 344072 | tf_op jit(solution)/shard_map/ppermute | solution.py:22
  61.7 7.8 %copy-start.3 = (bf16[1,2,4,64,576]{4,3,2,1,0:T(8,128)(2,1)S(1)}, bf16[1,2,4,64,576]{4,3,2,1,0:T(8,128)(2,1)}, u32[]{:S(2)}) copy-start(bf16[1,2,4,64,576]{4,3,2,1,0:T(8,128)(2,1)} %param.17) | copy-start | bytes 1769476
  61.9 5.3 %collective-permute-start.11 = (bf16[2,4,3584]{2,1,0:T(4,128)(2,1)S(1)}, bf16[2,4,3584]{2,1,0:T(4,128)(2,1)S(1)}, u32[]{:S(2)}, u32[]{:S(2)}) collective-permute-start(bf16[2,4,3584]{2,1,0:T(4,128)(2,1)S(1)} %slice.93), channel_id=1, source_target_pairs={{0,4},{1,5},{2,6},{3,7},{4,0},{5,1},{6,2},{7,3},{8,12},{9,13},{10,... | collective-permute-start | bytes 172040 | tf_op jit(solution)/shard_map/ppermute | solution.py:22
  65.3 5.0 %collective-permute-start.9 = (bf16[2,4,3584]{2,1,0:T(4,128)(2,1)S(1)}, bf16[2,4,3584]{2,1,0:T(4,128)(2,1)S(1)}, u32[]{:S(2)}, u32[]{:S(2)}) collective-permute-start(bf16[2,4,3584]{2,1,0:T(4,128)(2,1)S(1)} %slice.89), channel_id=1, source_target_pairs={{0,1},{1,0},{2,3},{3,2},{4,5},{5,4},{6,7},{7,6},{8,9},{9,8},{10,11... | collective-permute-start | bytes 172040 | tf_op jit(solution)/shard_map/ppermute | solution.py:22
  67.3 5.2 %collective-permute-start.12 = (bf16[2,4,3584]{2,1,0:T(4,128)(2,1)S(1)}, bf16[2,4,3584]{2,1,0:T(4,128)(2,1)S(1)}, u32[]{:S(2)}, u32[]{:S(2)}) collective-permute-start(bf16[2,4,3584]{2,1,0:T(4,128)(2,1)S(1)} %add_convert_fusion.4), channel_id=1, source_target_pairs={{0,16},{1,17},{2,18},{3,19},{4,20},{5,21},{6,22},{7,23},{8,24},{9,... | collective-permute-start | bytes 172040 | tf_op jit(solution)/shard_map/ppermute | solution.py:22
  72.5 5.7 %collective-permute-start.13 = (bf16[1,4,3584]{2,1,0:T(4,128)(2,1)S(1)}, bf16[1,4,3584]{2,1,0:T(4,128)(2,1)S(1)}, u32[]{:S(2)}, u32[]{:S(2)}) collective-permute-start(bf16[1,4,3584]{2,1,0:T(4,128)(2,1)S(1)} %slice.95), channel_id=1, source_target_pairs={{0,8},{1,9},{2,10},{3,11},{4,12},{5,13},{6,14},{7,15},{8,0},{9,1},... | collective-permute-start | bytes 86024 | tf_op jit(solution)/shard_map/ppermute | solution.py:22

commit v4 on v2

--- a/solution.py
+++ b/solution.py
@@ -93,8 +93,12 @@
     pad = -extra.shape[1] % 128
     packed = jnp.concatenate([moe_rows[0], jnp.pad(extra, ((0, 0), (0, pad)))], axis=1)
     stages = gather_stages(peers, lax.axis_size(("section", "tp")))
-    pooled = packed
-    for stage in stages:
+    pooled = packed[None]
+    for turn, stage in enumerate(stages):
+        if turn == 1:
+            pooled = pooled.reshape(-1, packed.shape[1])
+        if turn == len(stages) - 1:
+            pooled = lax.optimization_barrier(pooled)
         pooled = jnp.concatenate(
             [pooled] + [exchange(pooled, mask) for mask in masks_of(stage)[1:]], axis=0
         )

time: 57.5 us -> 54.9 us (0.955)
  local copies, waits for them, and re-layouts: 4.6 us -> 2.38 us
  matrix products: 12.5 us -> 13.8 us
  waiting for transfers between devices: 13.2 us -> 12.3 us
  other arithmetic: 4.29 us -> 3.64 us
    ppermute x14, waiting for transfers between devices: 13.2 us -> 9.8 us  [exchange(): return lax.ppermute(value, RANK, [(at, at ^ mask) for at in range(count)])]
    all_to_all x1, waiting for transfers between devices: 0.01 us -> 2.55 us  [body(): lax.all_to_all(picked_pages.reshape(peers, capp, page_len, width_lat), 'd...]
    concatenate x2 -> x0, local copies, waits for them, and re-layouts: 2.26 us -> none  [body(): jnp.concatenate([pooled] + [exchange(pooled, mask) for mask in masks_of(s...]
    dot_general x1, matrix products: 1.93 us -> 3.3 us  [attend(): jnp.einsum('rshk,rkv->rshv', weights, values, preferred_element_type=jnp....]
    sub x1, matrix products: 1.83 us -> 0.75 us  [attend(): weights = jnp.exp(scores - top)]
    dot_general x1, matrix products: 1.64 us -> 2.59 us  [attend(): jnp.einsum('rshl,rkl->rshk', queries, keys, preferred_element_type=jnp.fl...]
    broadcast_in_dim x0 -> x1, other arithmetic: none -> 0.76 us  [body(): pooled = packed[None]]
    concatenate x1 -> x0, other arithmetic: 0.76 us -> none  [body(): jnp.concatenate([moe_rows[0], jnp.pad(extra, ((0, 0), (0, pad)))], axis=1)]
  transfers between devices with their start and end apart: 15 -> 15, of which waited for: 7 -> 6; matrix products, arithmetic and copies ran while one was open for 32% -> 32% of each run, Pallas kernels for 0% -> 0%
where the time goes in v4:
time: 54.9 us; the launch traced here: 54.5 us
  starting transfers between devices  21.5 us (39%)
  matrix products  13.8 us (25%)
  waiting for transfers between devices  12.3 us (22%)
  other arithmetic  3.64 us (7%)
  local copies, waits for them, and re-layouts  2.38 us (4%)
  between operations  0.83 us (2%)
    ppermute x14, starting transfers between devices, exchange(): return lax.ppermute(value, RANK, [(at, at ^ mask) for at in range(count)])  17.9 us
    ppermute x14, waiting for transfers between devices, exchange(): return lax.ppermute(value, RANK, [(at, at ^ mask) for at in range(count)])  9.8 us
    dot_general x1, matrix products, body(): jnp.dot(hidden, expert_down[own], preferred_element_type=jnp.float32)  4.46 us
    all_to_all x1, starting transfers between devices, body(): lax.all_to_all(picked_pages.reshape(peers, capp, page_len, width_lat), 'd...  3.59 us
    dot_general x1, matrix products, attend(): jnp.einsum('rshk,rkv->rshv', weights, values, preferred_element_type=jnp....  3.3 us
    dot_general x1, matrix products, body(): up = jnp.dot(every, expert_up[own], preferred_element_type=jnp.float32)  2.67 us
    dot_general x1, matrix products, attend(): jnp.einsum('rshl,rkl->rshk', queries, keys, preferred_element_type=jnp.fl...  2.59 us
    all_to_all x1, waiting for transfers between devices, body(): lax.all_to_all(picked_pages.reshape(peers, capp, page_len, width_lat), 'd...  2.55 us
  transfers between devices with their start and end apart: 15, of which 6 were waited for; matrix products, arithmetic and copies ran while one was open for 32% of the time, Pallas kernels for 0%

profile of v4, /device:TPU:0, one launch (start us, length us, event | category | flops | bytes accessed | tf_op | source)
XLA Modules:
  0.0 54.5 jit_solution(14122975932724718746)
XLA Ops:
  0.6 0.8 %select_reduce_fusion = f32[4,16]{1,0:T(4,128)S(1)} fusion(f32[4,8]{1,0:T(4,128)} %bitcast.66, s32[4,8]{1,0:T(4,128)} %bitcast.67), kind=kLoop, calls=%fused_computation.46 | loop fusion | flops 1472 | bytes 512 | tf_op jit(solution)/shard_map/reduce_sum | solution.py:89
  1.6 0.8 %maximum_bitcast_fusion = bf16[1,4,3712]{2,1,0:T(4,128)(2,1)S(1)} fusion(bf16[4,128]{1,0:T(4,128)(2,1)S(1)} %fusion.36, bf16[4,3584]{1,0:T(4,128)(2,1)} %bitcast.65), kind=kLoop, calls=%fused_computation.44 | loop fusion | flops 59392 | bytes 59392 | tf_op jit(solution)/shard_map/broadcast_in_dim | solution.py:96
  2.4 3.1 %collective-permute-start = (bf16[1,4,3712]{2,1,0:T(4,128)(2,1)S(1)}, bf16[1,4,3712]{2,1,0:T(4,128)(2,1)S(1)}, u32[]{:S(2)}, u32[]{:S(2)}) collective-permute-start(bf16[1,4,3712]{2,1,0:T(4,128)(2,1)S(1)} %maximum_bitcast_fusion), channel_id=1, source_target_pairs={{0,8},{1,9},{2,10},{3,11},{4,12},{5,13},{6,14},{7,15},{8,0},{9,1},... | collective-permute-start | bytes 89096 | tf_op jit(solution)/shard_map/ppermute | solution.py:32
  5.4 2.6 %collective-permute-start.1 = (bf16[1,4,3712]{2,1,0:T(4,128)(2,1)S(1)}, bf16[1,4,3712]{2,1,0:T(4,128)(2,1)S(1)}, u32[]{:S(2)}, u32[]{:S(2)}) collective-permute-start(bf16[1,4,3712]{2,1,0:T(4,128)(2,1)S(1)} %maximum_bitcast_fusion), channel_id=1, source_target_pairs={{0,16},{1,17},{2,18},{3,19},{4,20},{5,21},{6,22},{7,23},{8,24},{9,... | collective-permute-start | bytes 89096 | tf_op jit(solution)/shard_map/ppermute | solution.py:32
  8.0 2.7 %collective-permute-done.1 = bf16[1,4,3712]{2,1,0:T(4,128)(2,1)S(1)} collective-permute-done((bf16[1,4,3712]{2,1,0:T(4,128)(2,1)S(1)}, bf16[1,4,3712]{2,1,0:T(4,128)(2,1)S(1)}, u32[]{:S(2)}, u32[]{:S(2)}) %collective-permute-start.1) | collective-permute-done | bytes 29728 | tf_op jit(solution)/shard_map/ppermute | solution.py:32
  10.7 3.0 %collective-permute-done.2 = bf16[1,4,3712]{2,1,0:T(4,128)(2,1)S(1)} collective-permute-done((bf16[1,4,3712]{2,1,0:T(4,128)(2,1)S(1)}, bf16[1,4,3712]{2,1,0:T(4,128)(2,1)S(1)}, u32[]{:S(2)}, u32[]{:S(2)}) %collective-permute-start.2) | collective-permute-done | bytes 29728 | tf_op jit(solution)/shard_map/ppermute | solution.py:32
  13.9 1.6 %collective-permute-start.3 = (bf16[16,3712]{1,0:T(8,128)(2,1)S(1)}, bf16[16,3712]{1,0:T(8,128)(2,1)S(1)}, u32[]{:S(2)}, u32[]{:S(2)}) collective-permute-start(bf16[16,3712]{1,0:T(8,128)(2,1)S(1)} %reshape.113), channel_id=1, source_target_pairs={{0,1},{1,0},{2,3},{3,2},{4,5},{5,4},{6,7},{7,6},{8,9},{9,8},{10,11... | collective-permute-start | bytes 356360 | tf_op jit(solution)/shard_map/ppermute | solution.py:32
  15.4 1.5 %collective-permute-start.4 = (bf16[16,3712]{1,0:T(8,128)(2,1)S(1)}, bf16[16,3712]{1,0:T(8,128)(2,1)S(1)}, u32[]{:S(2)}, u32[]{:S(2)}) collective-permute-start(bf16[16,3712]{1,0:T(8,128)(2,1)S(1)} %reshape.113), channel_id=1, source_target_pairs={{0,4},{1,5},{2,6},{3,7},{4,0},{5,1},{6,2},{7,3},{8,12},{9,13},{10,... | collective-permute-start | bytes 356360 | tf_op jit(solution)/shard_map/ppermute | solution.py:32
  17.0 0.5 collective-permute-start.5
  17.4 0.7 %maximum_bitcast_fusion.1 = s32[32]{0:T(128)S(1)} fusion(s32[1,32]{1,0:T(1,128)} %param.13), kind=kLoop, calls=%fused_computation.62 | loop fusion | flops 32 | bytes 256 | tf_op jit(solution)/shard_map/max | solution.py:74
  18.1 1.5 %gather_fusion = bf16[32,16,576]{2,1,0:T(8,128)(2,1)} fusion(bf16[32,16,576]{2,1,0:T(8,128)(2,1)S(1)} %bitcast.60, s32[1024]{0:T(1024)S(1)} %pad_clamp_fusion.1), kind=kCustom, calls=%fused_computation | custom fusion | bytes 1179776 | tf_op jit(solution)/shard_map/gather | solution.py:74
  19.6 3.6 %all-to-all-start = ((bf16[16,2,16,576]{3,2,1,0:T(8,128)(2,1)}), bf16[16,2,16,576]{3,2,1,0:T(8,128)(2,1)S(1)}, u32[]{:S(2)}, u32[]{:S(2)}) async-start(bf16[16,2,16,576]{3,2,1,0:T(8,128)(2,1)} %bitcast.3), calls=%async_computation | async-start | bytes 1310720 | tf_op jit(solution)/shard_map/all_to_all | solution.py:75
  23.2 0.4 collective-permute-start.6
  23.8 1.4 %collective-permute-done.6 = bf16[64,3712]{1,0:T(8,128)(2,1)S(1)} collective-permute-done((bf16[64,3712]{1,0:T(8,128)(2,1)S(1)}, bf16[64,3712]{1,0:T(8,128)(2,1)S(1)}, u32[]{:S(2)}, u32[]{:S(2)}) %collective-permute-start.6) | collective-permute-done | bytes 475168 | tf_op jit(solution)/shard_map/ppermute | solution.py:32
  25.1 2.7 %fusion.3 = f32[128,512]{1,0:T(8,128)S(1)} fusion(bf16[1,3584,512]{2,1,0:T(8,128)(2,1)} %param.22, bf16[64,3712]{1,0:T(8,128)(2,1)S(1)} %pad_maximum_fusion.1, bf16[64,3712]{1,0:T(8,128)(2,1)S(1)} %collective-permute-done.6), kind=kOutput, calls=%fused_computation.6 | convolution fusion | flops 471597056 | bytes 4882432 | tf_op jit(solution)/shard_map/dot_general | solution.py:114
  27.8 0.2 add_reduce_fusion
  28.0 4.5 %fusion.1 = bf16[128,3584]{1,0:T(8,128)(2,1)S(1)} fusion(bf16[1,512,3584]{2,1,0:T(8,128)(2,1)} %param.23, f32[128]{0:T(128)S(1)} %add_reduce_fusion, f32[128,512]{1,0:T(8,128)S(1)} %fusion.3, bf16[1,3584,512]{2,1,0:T(8,128)(2,1)} %param.21, bf16[64,3712]{1,0:T(8,128)(2,1)S(1)} %pad_maximum_fusion.1, bf16[64,3712]{1,0:T(8,128)(2,1)S(1)} %collective-permute-done.6), kind=kOutput, calls=%fused_computation.4 | convolution fusion | flops 942669824 | bytes 9470464 | tf_op jit(solution)/shard_map/dot_general | solution.py:116
  32.5 0.4 collective-permute-start.7
  32.9 1.5 %collective-permute-done.7 = bf16[64,3584]{1,0:T(8,128)(2,1)S(1)} collective-permute-done((bf16[64,3584]{1,0:T(8,128)(2,1)S(1)}, bf16[64,3584]{1,0:T(8,128)(2,1)S(1)}, u32[]{:S(2)}, u32[]{:S(2)}) %collective-permute-start.7) | collective-permute-done | bytes 458784 | tf_op jit(solution)/shard_map/ppermute | solution.py:32
  34.6 2.8 %collective-permute-start.10 = (bf16[16,3584]{1,0:T(8,128)(2,1)S(1)}, bf16[16,3584]{1,0:T(8,128)(2,1)S(1)}, u32[]{:S(2)}, u32[]{:S(2)}) collective-permute-start(bf16[16,3584]{1,0:T(8,128)(2,1)S(1)} %get-tuple-element.5), channel_id=1, source_target_pairs={{0,5},{1,4},{2,7},{3,6},{4,1},{5,0},{6,3},{7,2},{8,13},{9,12},{10,... | collective-permute-start | bytes 344072 | tf_op jit(solution)/shard_map/ppermute | solution.py:32
  37.4 0.6 %collective-permute-start.8 = (bf16[16,3584]{1,0:T(8,128)(2,1)S(1)}, bf16[16,3584]{1,0:T(8,128)(2,1)S(1)}, u32[]{:S(2)}, u32[]{:S(2)}) collective-permute-start(bf16[16,3584]{1,0:T(8,128)(2,1)S(1)} %get-tuple-element.4), channel_id=1, source_target_pairs={{0,1},{1,0},{2,3},{3,2},{4,5},{5,4},{6,7},{7,6},{8,9},{9,8},{10,11... | collective-permute-start | bytes 344072 | tf_op jit(solution)/shard_map/ppermute | solution.py:32
  37.9 0.2 collective-permute-start.9
  38.1 2.5 %all-to-all-done = bf16[16,2,16,576]{3,2,1,0:T(8,128)(2,1)S(1)} async-done(((bf16[16,2,16,576]{3,2,1,0:T(8,128)(2,1)}), bf16[16,2,16,576]{3,2,1,0:T(8,128)(2,1)S(1)}, u32[]{:S(2)}, u32[]{:S(2)}) %all-to-all-start) | async-done | bytes 589856 | tf_op jit(solution)/shard_map/all_to_all | solution.py:75
  40.7 0.7 %gather_fusion.1 = bf16[32,16,576]{2,1,0:T(8,128)(2,1)S(1)} fusion(bf16[32,16,576]{2,1,0:T(8,128)(2,1)S(1)} %bitcast.61, s32[1024]{0:T(1024)S(1)} %pad_clamp_fusion), kind=kCustom, calls=%fused_computation.1 | custom fusion | bytes 1179776 | tf_op jit(solution)/shard_map/gather | solution.py:130
  41.4 2.6 %fusion.10 = f32[2,4,64,260]{3,2,1,0:T(8,128)} fusion(bf16[2,4,576]{2,1,0:T(4,128)(2,1)S(1)} %bitcast.69, bf16[1,2,4,64,576]{4,3,2,1,0:T(8,128)(2,1)} %param.17, bf16[2,256,576]{2,1,0:T(8,128)(2,1)S(1)} %bitcast.62, pred[2,4,260]{2,1,0:T(4,128)(4,1)S(1)} %broadcast_or_fusion), kind=kOutput, calls=%fused_computation.15 | convolution fusion | flops 154818560 | bytes 1723424 | tf_op jit(solution)/shard_map/rshl,rkl->rshk/dot_general | solution.py:39
  44.0 0.8 %fusion.50 = f32[2,4,64]{2,1,0:T(4,128)S(1)} fusion(bf16[2,4,576]{2,1,0:T(4,128)(2,1)S(1)} %bitcast.70, bf16[1,2,4,64,576]{4,3,2,1,0:T(8,128)(2,1)S(1)} %copy-done.3, bf16[2,256,576]{2,1,0:T(8,128)(2,1)S(1)} %bitcast.63, pred[2,4,260]{2,1,0:T(4,128)(4,1)S(1)} %broadcast_or_fusion), kind=kOutput, calls=%fused_computation.72 | convolution fusion | flops 155085056 | bytes 1192992 | tf_op jit(solution)/shard_map/sub | solution.py:47
  44.9 1.2 %collective-permute-start.11 = (bf16[4,3584]{1,0:T(4,128)(2,1)S(1)}, bf16[4,3584]{1,0:T(4,128)(2,1)S(1)}, u32[]{:S(2)}, u32[]{:S(2)}) collective-permute-start(bf16[4,3584]{1,0:T(4,128)(2,1)S(1)} %get-tuple-element.7), channel_id=1, source_target_pairs={{0,8},{1,9},{2,10},{3,11},{4,12},{5,13},{6,14},{7,15},{8,0},{9,1},... | collective-permute-start | bytes 86024 | tf_op jit(solution)/shard_map/ppermute | solution.py:32
  46.1 2.1 %collective-permute-start.12 = (bf16[4,3584]{1,0:T(4,128)(2,1)S(1)}, bf16[4,3584]{1,0:T(4,128)(2,1)S(1)}, u32[]{:S(2)}, u32[]{:S(2)}) collective-permute-start(bf16[4,3584]{1,0:T(4,128)(2,1)S(1)} %get-tuple-element.9), channel_id=1, source_target_pairs={{0,16},{1,17},{2,18},{3,19},{4,20},{5,21},{6,22},{7,23},{8,24},{9,... | collective-permute-start | bytes 86024 | tf_op jit(solution)/shard_map/ppermute | solution.py:32
  48.2 1.1 %collective-permute-start.13 = (bf16[4,3584]{1,0:T(4,128)(2,1)S(1)}, bf16[4,3584]{1,0:T(4,128)(2,1)S(1)}, u32[]{:S(2)}, u32[]{:S(2)}) collective-permute-start(bf16[4,3584]{1,0:T(4,128)(2,1)S(1)} %get-tuple-element.8), channel_id=1, source_target_pairs={{0,24},{1,25},{2,26},{3,27},{4,28},{5,29},{6,30},{7,31},{8,16},{9,... | collective-permute-start | bytes 86024 | tf_op jit(solution)/shard_map/ppermute | solution.py:32
  49.3 3.3 %fusion.11 = bf16[1,2,4,64,512]{4,3,2,1,0:T(8,128)(2,1)} fusion(bf16[2,256,576]{2,1,0:T(8,128)(2,1)S(1)} %bitcast.64, bf16[2,4,576]{2,1,0:T(4,128)(2,1)S(1)} %bitcast.71, f32[2,4,64]{2,1,0:T(4,128)S(1)} %fusion.50, f32[2,4,64,260]{3,2,1,0:T(8,128)} %fusion.10), kind=kOutput, calls=%fused_computation.16 | convolution fusion | flops 138042112 | bytes 2698240 | tf_op jit(solution)/shard_map/rshk,rkv->rshv/dot_general | solution.py:50
  52.6 1.2 %collective-permute-done.13 = bf16[4,3584]{1,0:T(4,128)(2,1)S(1)} collective-permute-done((bf16[4,3584]{1,0:T(4,128)(2,1)S(1)}, bf16[4,3584]{1,0:T(4,128)(2,1)S(1)}, u32[]{:S(2)}, u32[]{:S(2)}) %collective-permute-start.13) | collective-permute-done | bytes 28704 | tf_op jit(solution)/shard_map/ppermute | solution.py:32
  53.9 0.6 %fusion.28 = bf16[1,4,3584]{2,1,0:T(4,128)(2,1)} fusion(bf16[4,3584]{1,0:T(4,128)(2,1)S(1)} %collective-permute-done.13, bf16[4,3584]{1,0:T(4,128)(2,1)S(1)} %collective-permute-done.12, bf16[4,3584]{1,0:T(4,128)(2,1)S(1)} %collective-permute-done.11, bf16[16,3584]{1,0:T(8,128)(2,1)S(1)} %add_convert_fusion.1), kind=kLoop, calls=%fused_computation.45 | loop fusion | flops 114688 | bytes 143360 | tf_op jit(solution)/shard_map/broadcast_in_dim | solution.py:132
  (39 shorter events, 0.8 us)
Async XLA Ops:
  0.6 17.5 %copy-start = (bf16[1,32,16,576]{3,2,1,0:T(8,128)(2,1)S(1)}, bf16[1,32,16,576]{3,2,1,0:T(8,128)(2,1)}, u32[]{:S(2)}) copy-start(bf16[1,32,16,576]{3,2,1,0:T(8,128)(2,1)} %param.12) | copy-start | bytes 1769476
  2.4 5.7 %collective-permute-start = (bf16[1,4,3712]{2,1,0:T(4,128)(2,1)S(1)}, bf16[1,4,3712]{2,1,0:T(4,128)(2,1)S(1)}, u32[]{:S(2)}, u32[]{:S(2)}) collective-permute-start(bf16[1,4,3712]{2,1,0:T(4,128)(2,1)S(1)} %maximum_bitcast_fusion), channel_id=1, source_target_pairs={{0,8},{1,9},{2,10},{3,11},{4,12},{5,13},{6,14},{7,15},{8,0},{9,1},... | collective-permute-start | bytes 89096 | tf_op jit(solution)/shard_map/ppermute | solution.py:32
  5.4 5.3 %collective-permute-start.1 = (bf16[1,4,3712]{2,1,0:T(4,128)(2,1)S(1)}, bf16[1,4,3712]{2,1,0:T(4,128)(2,1)S(1)}, u32[]{:S(2)}, u32[]{:S(2)}) collective-permute-start(bf16[1,4,3712]{2,1,0:T(4,128)(2,1)S(1)} %maximum_bitcast_fusion), channel_id=1, source_target_pairs={{0,16},{1,17},{2,18},{3,19},{4,20},{5,21},{6,22},{7,23},{8,24},{9,... | collective-permute-start | bytes 89096 | tf_op jit(solution)/shard_map/ppermute | solution.py:32
  8.0 5.7 %collective-permute-start.2 = (bf16[1,4,3712]{2,1,0:T(4,128)(2,1)S(1)}, bf16[1,4,3712]{2,1,0:T(4,128)(2,1)S(1)}, u32[]{:S(2)}, u32[]{:S(2)}) collective-permute-start(bf16[1,4,3712]{2,1,0:T(4,128)(2,1)S(1)} %maximum_bitcast_fusion), channel_id=1, source_target_pairs={{0,24},{1,25},{2,26},{3,27},{4,28},{5,29},{6,30},{7,31},{8,16},{9,... | collective-permute-start | bytes 89096 | tf_op jit(solution)/shard_map/ppermute | solution.py:32
  13.9 9.7 %copy-start.1 = (s32[1,2,16]{2,1,0:T(2,128)S(1)}, s32[1,2,16]{2,1,0:T(2,128)}, u32[]{:S(2)}) copy-start(s32[1,2,16]{2,1,0:T(2,128)} %param.14) | copy-start | bytes 388
  13.9 9.8 %copy-start.2 = (s32[1,2]{1,0:T(1,128)S(1)}, s32[1,2]{1,0:T(1,128)}, u32[]{:S(2)}) copy-start(s32[1,2]{1,0:T(1,128)} %param.15) | copy-start | bytes 28
  13.9 9.3 %collective-permute-start.3 = (bf16[16,3712]{1,0:T(8,128)(2,1)S(1)}, bf16[16,3712]{1,0:T(8,128)(2,1)S(1)}, u32[]{:S(2)}, u32[]{:S(2)}) collective-permute-start(bf16[16,3712]{1,0:T(8,128)(2,1)S(1)} %reshape.113), channel_id=1, source_target_pairs={{0,1},{1,0},{2,3},{3,2},{4,5},{5,4},{6,7},{7,6},{8,9},{9,8},{10,11... | collective-permute-start | bytes 356360 | tf_op jit(solution)/shard_map/ppermute | solution.py:32
  15.4 7.7 %collective-permute-start.4 = (bf16[16,3712]{1,0:T(8,128)(2,1)S(1)}, bf16[16,3712]{1,0:T(8,128)(2,1)S(1)}, u32[]{:S(2)}, u32[]{:S(2)}) collective-permute-start(bf16[16,3712]{1,0:T(8,128)(2,1)S(1)} %reshape.113), channel_id=1, source_target_pairs={{0,4},{1,5},{2,6},{3,7},{4,0},{5,1},{6,2},{7,3},{8,12},{9,13},{10,... | collective-permute-start | bytes 356360 | tf_op jit(solution)/shard_map/ppermute | solution.py:32
  17.0 6.2 %collective-permute-start.5 = (bf16[16,3712]{1,0:T(8,128)(2,1)S(1)}, bf16[16,3712]{1,0:T(8,128)(2,1)S(1)}, u32[]{:S(2)}, u32[]{:S(2)}) collective-permute-start(bf16[16,3712]{1,0:T(8,128)(2,1)S(1)} %reshape.113), channel_id=1, source_target_pairs={{0,5},{1,4},{2,7},{3,6},{4,1},{5,0},{6,3},{7,2},{8,13},{9,12},{10,... | collective-permute-start | bytes 356360 | tf_op jit(solution)/shard_map/ppermute | solution.py:32
  19.6 21.1 %all-to-all-start = ((bf16[16,2,16,576]{3,2,1,0:T(8,128)(2,1)}), bf16[16,2,16,576]{3,2,1,0:T(8,128)(2,1)S(1)}, u32[]{:S(2)}, u32[]{:S(2)}) async-start(bf16[16,2,16,576]{3,2,1,0:T(8,128)(2,1)} %bitcast.3), calls=%async_computation | async-start | bytes 1310720 | tf_op jit(solution)/shard_map/all_to_all | solution.py:75
  23.2 1.9 %collective-permute-start.6 = (bf16[64,3712]{1,0:T(8,128)(2,1)S(1)}, bf16[64,3712]{1,0:T(8,128)(2,1)S(1)}, u32[]{:S(2)}, u32[]{:S(2)}) collective-permute-start(bf16[64,3712]{1,0:T(8,128)(2,1)S(1)} %pad_maximum_fusion.1), channel_id=1, source_target_pairs={{0,2},{1,3},{2,0},{3,1},{4,6},{5,7},{6,4},{7,5},{8,10},{9,11},{10,... | collective-permute-start | bytes 1425416 | tf_op jit(solution)/shard_map/ppermute | solution.py:32
  32.5 8.8 %copy-start.4 = (bf16[1,2,4,576]{3,2,1,0:T(4,128)(2,1)S(1)}, bf16[1,2,4,576]{3,2,1,0:T(4,128)(2,1)}, u32[]{:S(2)}) copy-start(bf16[1,2,4,576]{3,2,1,0:T(4,128)(2,1)} %param.16) | copy-start | bytes 27652
  32.5 1.9 %collective-permute-start.7 = (bf16[64,3584]{1,0:T(8,128)(2,1)S(1)}, bf16[64,3584]{1,0:T(8,128)(2,1)S(1)}, u32[]{:S(2)}, u32[]{:S(2)}) collective-permute-start(bf16[64,3584]{1,0:T(8,128)(2,1)S(1)} %slice.57), channel_id=1, source_target_pairs={{0,2},{1,3},{2,0},{3,1},{4,6},{5,7},{6,4},{7,5},{8,10},{9,11},{10,... | collective-permute-start | bytes 1376264 | tf_op jit(solution)/shard_map/ppermute | solution.py:32
  34.6 10.1 %collective-permute-start.10 = (bf16[16,3584]{1,0:T(8,128)(2,1)S(1)}, bf16[16,3584]{1,0:T(8,128)(2,1)S(1)}, u32[]{:S(2)}, u32[]{:S(2)}) collective-permute-start(bf16[16,3584]{1,0:T(8,128)(2,1)S(1)} %get-tuple-element.5), channel_id=1, source_target_pairs={{0,5},{1,4},{2,7},{3,6},{4,1},{5,0},{6,3},{7,2},{8,13},{9,12},{10,... | collective-permute-start | bytes 344072 | tf_op jit(solution)/shard_map/ppermute | solution.py:32
  37.4 7.4 %collective-permute-start.8 = (bf16[16,3584]{1,0:T(8,128)(2,1)S(1)}, bf16[16,3584]{1,0:T(8,128)(2,1)S(1)}, u32[]{:S(2)}, u32[]{:S(2)}) collective-permute-start(bf16[16,3584]{1,0:T(8,128)(2,1)S(1)} %get-tuple-element.4), channel_id=1, source_target_pairs={{0,1},{1,0},{2,3},{3,2},{4,5},{5,4},{6,7},{7,6},{8,9},{9,8},{10,11... | collective-permute-start | bytes 344072 | tf_op jit(solution)/shard_map/ppermute | solution.py:32
  37.9 6.8 %collective-permute-start.9 = (bf16[16,3584]{1,0:T(8,128)(2,1)S(1)}, bf16[16,3584]{1,0:T(8,128)(2,1)S(1)}, u32[]{:S(2)}, u32[]{:S(2)}) collective-permute-start(bf16[16,3584]{1,0:T(8,128)(2,1)S(1)} %get-tuple-element.6), channel_id=1, source_target_pairs={{0,4},{1,5},{2,6},{3,7},{4,0},{5,1},{6,2},{7,3},{8,12},{9,13},{10,... | collective-permute-start | bytes 344072 | tf_op jit(solution)/shard_map/ppermute | solution.py:32
  41.4 2.6 %copy-start.3 = (bf16[1,2,4,64,576]{4,3,2,1,0:T(8,128)(2,1)S(1)}, bf16[1,2,4,64,576]{4,3,2,1,0:T(8,128)(2,1)}, u32[]{:S(2)}) copy-start(bf16[1,2,4,64,576]{4,3,2,1,0:T(8,128)(2,1)} %param.17) | copy-start | bytes 1769476
  44.9 7.8 %collective-permute-start.11 = (bf16[4,3584]{1,0:T(4,128)(2,1)S(1)}, bf16[4,3584]{1,0:T(4,128)(2,1)S(1)}, u32[]{:S(2)}, u32[]{:S(2)}) collective-permute-start(bf16[4,3584]{1,0:T(4,128)(2,1)S(1)} %get-tuple-element.7), channel_id=1, source_target_pairs={{0,8},{1,9},{2,10},{3,11},{4,12},{5,13},{6,14},{7,15},{8,0},{9,1},... | collective-permute-start | bytes 86024 | tf_op jit(solution)/shard_map/ppermute | solution.py:32
  46.1 6.5 %collective-permute-start.12 = (bf16[4,3584]{1,0:T(4,128)(2,1)S(1)}, bf16[4,3584]{1,0:T(4,128)(2,1)S(1)}, u32[]{:S(2)}, u32[]{:S(2)}) collective-permute-start(bf16[4,3584]{1,0:T(4,128)(2,1)S(1)} %get-tuple-element.9), channel_id=1, source_target_pairs={{0,16},{1,17},{2,18},{3,19},{4,20},{5,21},{6,22},{7,23},{8,24},{9,... | collective-permute-start | bytes 86024 | tf_op jit(solution)/shard_map/ppermute | solution.py:32
  48.2 5.7 %collective-permute-start.13 = (bf16[4,3584]{1,0:T(4,128)(2,1)S(1)}, bf16[4,3584]{1,0:T(4,128)(2,1)S(1)}, u32[]{:S(2)}, u32[]{:S(2)}) collective-permute-start(bf16[4,3584]{1,0:T(4,128)(2,1)S(1)} %get-tuple-element.8), channel_id=1, source_target_pairs={{0,24},{1,25},{2,26},{3,27},{4,28},{5,29},{6,30},{7,31},{8,16},{9,... | collective-permute-start | bytes 86024 | tf_op jit(solution)/shard_map/ppermute | solution.py:32

commit v5 on v4

--- a/solution.py
+++ b/solution.py
@@ -1,6 +1,10 @@
+import functools
+
 import jax
 import jax.numpy as jnp
 from jax import lax
+from jax.experimental import pallas as pl
+from jax.experimental.pallas import tpu as pltpu
 from jax.sharding import PartitionSpec as P
 
 VDIM = 512
@@ -30,6 +34,32 @@
 def exchange(value, mask):
     count = lax.axis_size(RANK)
     return lax.ppermute(value, RANK, [(at, at ^ mask) for at in range(count)])
+
+
+def pack_kernel(experts, rows_ref, routing_ref, weights_ref, out_ref):
+    rows, width = rows_ref.shape
+    lanes = out_ref.shape[1] - width
+    out_ref[:, :width] = rows_ref[...]
+    lane = lax.broadcasted_iota(jnp.int32, (rows, lanes), 1)
+    expert = jnp.where(lane < experts, lane, lane - experts)
+    dense = jnp.zeros((rows, lanes), jnp.float32)
+    for turn in range(routing_ref.shape[1]):
+        named = routing_ref[:, turn : turn + 1] == expert
+        dense = dense + jnp.where(named, weights_ref[:, turn : turn + 1], 0.0)
+    high = dense.astype(jnp.bfloat16).astype(jnp.float32)
+    out_ref[:, width:] = jnp.where(lane < experts, high, dense - high).astype(jnp.bfloat16)
+
+
+def pack(rows, routing, weights, experts):
+    lanes = -(-2 * experts // 128) * 128
+    vmem = pl.BlockSpec(memory_space=pltpu.VMEM)
+    return pl.pallas_call(
+        functools.partial(pack_kernel, experts),
+        out_shape=jax.ShapeDtypeStruct((rows.shape[0], rows.shape[1] + lanes), rows.dtype),
+        in_specs=[vmem, vmem, vmem],
+        out_specs=vmem,
+        name="pack",
+    )(rows, routing, weights)
 
 
 def attend(queries, new_latent, cache, lengths):
@@ -85,13 +115,7 @@
     experts = peers * owned
     rows = routing.shape[1]
     width = moe_rows.shape[2]
-    named = routing[0][:, :, None] == jnp.arange(experts)[None, None, :]
-    dense = jnp.sum(jnp.where(named, gate_weights[0][:, :, None], 0.0), axis=1)
-    high = dense.astype(jnp.bfloat16)
-    low = (dense - high.astype(jnp.float32)).astype(jnp.bfloat16)
-    extra = jnp.concatenate([high, low], axis=1)
-    pad = -extra.shape[1] % 128
-    packed = jnp.concatenate([moe_rows[0], jnp.pad(extra, ((0, 0), (0, pad)))], axis=1)
+    packed = pack(moe_rows[0], routing[0], gate_weights[0], experts)
     stages = gather_stages(peers, lax.axis_size(("section", "tp")))
     pooled = packed[None]
     for turn, stage in enumerate(stages):

time: 54.9 us -> 55.6 us (1.013)
  Pallas kernels: 0 us -> 1.54 us
  other arithmetic: 3.64 us -> 2.69 us
    pallas_call x0 -> x1, Pallas kernels: none -> 1.54 us  [pack(): pl.pallas_call(functools.partial(pack_kernel, experts), out_shape=jax.Sha...]
    reduce_sum x1 -> x0, other arithmetic: 0.85 us -> none  [body(): dense = jnp.sum(jnp.where(named, gate_weights[0][:, :, None], 0.0), axis=1)]
    broadcast_in_dim x1 -> x0, other arithmetic: 0.76 us -> none  [body(): pooled = packed[None]]
    concatenate x2, other arithmetic: 0.14 us -> 0.9 us  [body(): jnp.concatenate([pooled] + [exchange(pooled, mask) for mask in masks_of(s...]
  transfers between devices with their start and end apart: 15 -> 15, of which waited for: 6 -> 6; matrix products, arithmetic and copies ran while one was open for 32% -> 31% of each run, Pallas kernels for 0% -> 0%
where the time goes in v5:
time: 55.6 us; the launch traced here: 55.2 us
  starting transfers between devices  21.5 us (39%)
  matrix products  13.8 us (25%)
  waiting for transfers between devices  12.6 us (23%)
  other arithmetic  2.69 us (5%)
  local copies, waits for them, and re-layouts  2.38 us (4%)
  Pallas kernels  1.54 us (3%)
  between operations  0.83 us (1%)
    ppermute x14, starting transfers between devices, exchange(): return lax.ppermute(value, RANK, [(at, at ^ mask) for at in range(count)])  17.9 us
    ppermute x14, waiting for transfers between devices, exchange(): return lax.ppermute(value, RANK, [(at, at ^ mask) for at in range(count)])  10 us
    dot_general x1, matrix products, body(): jnp.dot(hidden, expert_down[own], preferred_element_type=jnp.float32)  4.46 us
    all_to_all x1, starting transfers between devices, body(): lax.all_to_all(picked_pages.reshape(peers, capp, page_len, width_lat), 'd...  3.59 us
    dot_general x1, matrix products, attend(): jnp.einsum('rshk,rkv->rshv', weights, values, preferred_element_type=jnp....  3.3 us
    dot_general x1, matrix products, body(): up = jnp.dot(every, expert_up[own], preferred_element_type=jnp.float32)  2.67 us
    dot_general x1, matrix products, attend(): jnp.einsum('rshl,rkl->rshk', queries, keys, preferred_element_type=jnp.fl...  2.6 us
    all_to_all x1, waiting for transfers between devices, body(): lax.all_to_all(picked_pages.reshape(peers, capp, page_len, width_lat), 'd...  2.55 us
  transfers between devices with their start and end apart: 15, of which 6 were waited for; matrix products, arithmetic and copies ran while one was open for 31% of the time, Pallas kernels for 0%

profile of v5, /device:TPU:0, one launch (start us, length us, event | category | flops | bytes accessed | tf_op | source)
XLA Modules:
  0.0 55.2 jit_solution(10320580799400444951)
XLA Ops:
  0.6 1.5 %pack.1 = bf16[4,3712]{1,0:T(4,128)(2,1)} custom-call(bf16[4,3584]{1,0:T(4,128)(2,1)} %bitcast.68, s32[4,8]{1,0:T(4,128)} %bitcast.69, f32[4,8]{1,0:T(4,128)} %bitcast.70), custom_call_target="tpu_custom_call" | custom-call | tf_op jit(solution)/shard_map/pack/pallas_call | solution.py:56
  2.2 3.0 %collective-permute-start = (bf16[1,4,3712]{2,1,0:T(4,128)(2,1)}, bf16[1,4,3712]{2,1,0:T(4,128)(2,1)S(1)}, u32[]{:S(2)}, u32[]{:S(2)}) collective-permute-start(bf16[1,4,3712]{2,1,0:T(4,128)(2,1)} %bitcast.64), channel_id=1, source_target_pairs={{0,8},{1,9},{2,10},{3,11},{4,12},{5,13},{6,14},{7,15},{8,0},{9,1},... | collective-permute-start | bytes 89096 | tf_op jit(solution)/shard_map/ppermute | solution.py:36
  5.2 2.6 %collective-permute-start.1 = (bf16[1,4,3712]{2,1,0:T(4,128)(2,1)}, bf16[1,4,3712]{2,1,0:T(4,128)(2,1)S(1)}, u32[]{:S(2)}, u32[]{:S(2)}) collective-permute-start(bf16[1,4,3712]{2,1,0:T(4,128)(2,1)} %bitcast.65), channel_id=1, source_target_pairs={{0,16},{1,17},{2,18},{3,19},{4,20},{5,21},{6,22},{7,23},{8,24},{9,... | collective-permute-start | bytes 89096 | tf_op jit(solution)/shard_map/ppermute | solution.py:36
  7.8 2.9 %collective-permute-done.1 = bf16[1,4,3712]{2,1,0:T(4,128)(2,1)S(1)} collective-permute-done((bf16[1,4,3712]{2,1,0:T(4,128)(2,1)}, bf16[1,4,3712]{2,1,0:T(4,128)(2,1)S(1)}, u32[]{:S(2)}, u32[]{:S(2)}) %collective-permute-start.1) | collective-permute-done | bytes 29728 | tf_op jit(solution)/shard_map/ppermute | solution.py:36
  10.7 3.0 %collective-permute-done.2 = bf16[1,4,3712]{2,1,0:T(4,128)(2,1)S(1)} collective-permute-done((bf16[1,4,3712]{2,1,0:T(4,128)(2,1)}, bf16[1,4,3712]{2,1,0:T(4,128)(2,1)S(1)}, u32[]{:S(2)}, u32[]{:S(2)}) %collective-permute-start.2) | collective-permute-done | bytes 29728 | tf_op jit(solution)/shard_map/ppermute | solution.py:36
  13.7 0.9 %pad_maximum_fusion.2 = bf16[4,4,3712]{2,1,0:T(4,128)(2,1)S(1)} fusion(bf16[1,4,3712]{2,1,0:T(4,128)(2,1)S(1)} %collective-permute-done.2, bf16[1,4,3712]{2,1,0:T(4,128)(2,1)S(1)} %collective-permute-done.1, bf16[1,4,3712]{2,1,0:T(4,128)(2,1)S(1)} %collective-permute-done, bf16[1,4,3712]{2,1,0:T(4,128)(2,1)} %bitcast.67), kind=kLoop, calls=%fused_computation.39 | loop fusion | flops 178176 | bytes 237568 | tf_op jit(solution)/shard_map/concatenate | solution.py:126
  14.6 1.6 %collective-permute-start.3 = (bf16[16,3712]{1,0:T(8,128)(2,1)S(1)}, bf16[16,3712]{1,0:T(8,128)(2,1)S(1)}, u32[]{:S(2)}, u32[]{:S(2)}) collective-permute-start(bf16[16,3712]{1,0:T(8,128)(2,1)S(1)} %reshape.111), channel_id=1, source_target_pairs={{0,1},{1,0},{2,3},{3,2},{4,5},{5,4},{6,7},{7,6},{8,9},{9,8},{10,11... | collective-permute-start | bytes 356360 | tf_op jit(solution)/shard_map/ppermute | solution.py:36
  16.2 1.5 %collective-permute-start.4 = (bf16[16,3712]{1,0:T(8,128)(2,1)S(1)}, bf16[16,3712]{1,0:T(8,128)(2,1)S(1)}, u32[]{:S(2)}, u32[]{:S(2)}) collective-permute-start(bf16[16,3712]{1,0:T(8,128)(2,1)S(1)} %reshape.111), channel_id=1, source_target_pairs={{0,4},{1,5},{2,6},{3,7},{4,0},{5,1},{6,2},{7,3},{8,12},{9,13},{10,... | collective-permute-start | bytes 356360 | tf_op jit(solution)/shard_map/ppermute | solution.py:36
  17.7 0.5 collective-permute-start.5
  18.2 0.7 %maximum_bitcast_fusion = s32[32]{0:T(128)S(1)} fusion(s32[1,32]{1,0:T(1,128)} %param.13), kind=kLoop, calls=%fused_computation.54 | loop fusion | flops 32 | bytes 256 | tf_op jit(solution)/shard_map/max | solution.py:104
  18.8 1.5 %gather_fusion = bf16[32,16,576]{2,1,0:T(8,128)(2,1)} fusion(bf16[32,16,576]{2,1,0:T(8,128)(2,1)S(1)} %bitcast.59, s32[1024]{0:T(1024)S(1)} %pad_clamp_fusion.1), kind=kCustom, calls=%fused_computation | custom fusion | bytes 1179776 | tf_op jit(solution)/shard_map/gather | solution.py:104
  20.3 3.6 %all-to-all-start = ((bf16[16,2,16,576]{3,2,1,0:T(8,128)(2,1)}), bf16[16,2,16,576]{3,2,1,0:T(8,128)(2,1)S(1)}, u32[]{:S(2)}, u32[]{:S(2)}) async-start(bf16[16,2,16,576]{3,2,1,0:T(8,128)(2,1)} %bitcast.3), calls=%async_computation | async-start | bytes 1310720 | tf_op jit(solution)/shard_map/all_to_all | solution.py:105
  24.0 0.4 collective-permute-start.6
  24.5 1.4 %collective-permute-done.6 = bf16[64,3712]{1,0:T(8,128)(2,1)S(1)} collective-permute-done((bf16[64,3712]{1,0:T(8,128)(2,1)S(1)}, bf16[64,3712]{1,0:T(8,128)(2,1)S(1)}, u32[]{:S(2)}, u32[]{:S(2)}) %collective-permute-start.6) | collective-permute-done | bytes 475168 | tf_op jit(solution)/shard_map/ppermute | solution.py:36
  25.9 2.7 %fusion.3 = f32[128,512]{1,0:T(8,128)S(1)} fusion(bf16[1,3584,512]{2,1,0:T(8,128)(2,1)} %param.22, bf16[64,3712]{1,0:T(8,128)(2,1)S(1)} %pad_maximum_fusion.1, bf16[64,3712]{1,0:T(8,128)(2,1)S(1)} %collective-permute-done.6), kind=kOutput, calls=%fused_computation.6 | convolution fusion | flops 471597056 | bytes 4882432 | tf_op jit(solution)/shard_map/dot_general | solution.py:138
  28.6 0.2 add_reduce_fusion
  28.8 4.5 %fusion.1 = bf16[128,3584]{1,0:T(8,128)(2,1)S(1)} fusion(bf16[1,512,3584]{2,1,0:T(8,128)(2,1)} %param.23, f32[128]{0:T(128)S(1)} %add_reduce_fusion, f32[128,512]{1,0:T(8,128)S(1)} %fusion.3, bf16[1,3584,512]{2,1,0:T(8,128)(2,1)} %param.21, bf16[64,3712]{1,0:T(8,128)(2,1)S(1)} %pad_maximum_fusion.1, bf16[64,3712]{1,0:T(8,128)(2,1)S(1)} %collective-permute-done.6), kind=kOutput, calls=%fused_computation.4 | convolution fusion | flops 942669824 | bytes 9470464 | tf_op jit(solution)/shard_map/dot_general | solution.py:140
  33.3 0.4 collective-permute-start.7
  33.7 1.5 %collective-permute-done.7 = bf16[64,3584]{1,0:T(8,128)(2,1)S(1)} collective-permute-done((bf16[64,3584]{1,0:T(8,128)(2,1)S(1)}, bf16[64,3584]{1,0:T(8,128)(2,1)S(1)}, u32[]{:S(2)}, u32[]{:S(2)}) %collective-permute-start.7) | collective-permute-done | bytes 458784 | tf_op jit(solution)/shard_map/ppermute | solution.py:36
  35.3 2.8 %collective-permute-start.10 = (bf16[16,3584]{1,0:T(8,128)(2,1)S(1)}, bf16[16,3584]{1,0:T(8,128)(2,1)S(1)}, u32[]{:S(2)}, u32[]{:S(2)}) collective-permute-start(bf16[16,3584]{1,0:T(8,128)(2,1)S(1)} %get-tuple-element.3), channel_id=1, source_target_pairs={{0,5},{1,4},{2,7},{3,6},{4,1},{5,0},{6,3},{7,2},{8,13},{9,12},{10,... | collective-permute-start | bytes 344072 | tf_op jit(solution)/shard_map/ppermute | solution.py:36
  38.1 0.5 collective-permute-start.8
  38.7 0.2 collective-permute-start.9
  38.9 2.6 %all-to-all-done = bf16[16,2,16,576]{3,2,1,0:T(8,128)(2,1)S(1)} async-done(((bf16[16,2,16,576]{3,2,1,0:T(8,128)(2,1)}), bf16[16,2,16,576]{3,2,1,0:T(8,128)(2,1)S(1)}, u32[]{:S(2)}, u32[]{:S(2)}) %all-to-all-start) | async-done | bytes 589856 | tf_op jit(solution)/shard_map/all_to_all | solution.py:105
  41.4 0.7 %gather_fusion.1 = bf16[32,16,576]{2,1,0:T(8,128)(2,1)S(1)} fusion(bf16[32,16,576]{2,1,0:T(8,128)(2,1)S(1)} %bitcast.60, s32[1024]{0:T(1024)S(1)} %pad_clamp_fusion), kind=kCustom, calls=%fused_computation.1 | custom fusion | bytes 1179776 | tf_op jit(solution)/shard_map/gather | solution.py:154
  42.1 2.6 %fusion.10 = f32[2,4,64,260]{3,2,1,0:T(8,128)} fusion(bf16[2,4,576]{2,1,0:T(4,128)(2,1)S(1)} %bitcast.72, bf16[1,2,4,64,576]{4,3,2,1,0:T(8,128)(2,1)} %param.17, bf16[2,256,576]{2,1,0:T(8,128)(2,1)S(1)} %bitcast.61, pred[2,4,260]{2,1,0:T(4,128)(4,1)S(1)} %broadcast_or_fusion), kind=kOutput, calls=%fused_computation.15 | convolution fusion | flops 154818560 | bytes 1723424 | tf_op jit(solution)/shard_map/rshl,rkl->rshk/dot_general | solution.py:69
  44.7 0.8 %fusion.47 = f32[2,4,64]{2,1,0:T(4,128)S(1)} fusion(bf16[2,4,576]{2,1,0:T(4,128)(2,1)S(1)} %bitcast.73, bf16[1,2,4,64,576]{4,3,2,1,0:T(8,128)(2,1)S(1)} %copy-done.3, bf16[2,256,576]{2,1,0:T(8,128)(2,1)S(1)} %bitcast.62, pred[2,4,260]{2,1,0:T(4,128)(4,1)S(1)} %broadcast_or_fusion), kind=kOutput, calls=%fused_computation.64 | convolution fusion | flops 155085056 | bytes 1192992 | tf_op jit(solution)/shard_map/sub | solution.py:77
  45.6 1.2 %collective-permute-start.11 = (bf16[4,3584]{1,0:T(4,128)(2,1)S(1)}, bf16[4,3584]{1,0:T(4,128)(2,1)S(1)}, u32[]{:S(2)}, u32[]{:S(2)}) collective-permute-start(bf16[4,3584]{1,0:T(4,128)(2,1)S(1)} %get-tuple-element.5), channel_id=1, source_target_pairs={{0,8},{1,9},{2,10},{3,11},{4,12},{5,13},{6,14},{7,15},{8,0},{9,1},... | collective-permute-start | bytes 86024 | tf_op jit(solution)/shard_map/ppermute | solution.py:36
  46.8 2.1 %collective-permute-start.12 = (bf16[4,3584]{1,0:T(4,128)(2,1)S(1)}, bf16[4,3584]{1,0:T(4,128)(2,1)S(1)}, u32[]{:S(2)}, u32[]{:S(2)}) collective-permute-start(bf16[4,3584]{1,0:T(4,128)(2,1)S(1)} %get-tuple-element.7), channel_id=1, source_target_pairs={{0,16},{1,17},{2,18},{3,19},{4,20},{5,21},{6,22},{7,23},{8,24},{9,... | collective-permute-start | bytes 86024 | tf_op jit(solution)/shard_map/ppermute | solution.py:36
  48.9 1.1 %collective-permute-start.13 = (bf16[4,3584]{1,0:T(4,128)(2,1)S(1)}, bf16[4,3584]{1,0:T(4,128)(2,1)S(1)}, u32[]{:S(2)}, u32[]{:S(2)}) collective-permute-start(bf16[4,3584]{1,0:T(4,128)(2,1)S(1)} %get-tuple-element.6), channel_id=1, source_target_pairs={{0,24},{1,25},{2,26},{3,27},{4,28},{5,29},{6,30},{7,31},{8,16},{9,... | collective-permute-start | bytes 86024 | tf_op jit(solution)/shard_map/ppermute | solution.py:36
  50.1 3.3 %fusion.11 = bf16[1,2,4,64,512]{4,3,2,1,0:T(8,128)(2,1)} fusion(bf16[2,256,576]{2,1,0:T(8,128)(2,1)S(1)} %bitcast.63, bf16[2,4,576]{2,1,0:T(4,128)(2,1)S(1)} %bitcast.74, f32[2,4,64]{2,1,0:T(4,128)S(1)} %fusion.47, f32[2,4,64,260]{3,2,1,0:T(8,128)} %fusion.10), kind=kOutput, calls=%fused_computation.16 | convolution fusion | flops 138042112 | bytes 2698240 | tf_op jit(solution)/shard_map/rshk,rkv->rshv/dot_general | solution.py:80
  53.4 1.2 %collective-permute-done.13 = bf16[4,3584]{1,0:T(4,128)(2,1)S(1)} collective-permute-done((bf16[4,3584]{1,0:T(4,128)(2,1)S(1)}, bf16[4,3584]{1,0:T(4,128)(2,1)S(1)}, u32[]{:S(2)}, u32[]{:S(2)}) %collective-permute-start.13) | collective-permute-done | bytes 28704 | tf_op jit(solution)/shard_map/ppermute | solution.py:36
  54.6 0.6 %fusion.28 = bf16[1,4,3584]{2,1,0:T(4,128)(2,1)} fusion(bf16[4,3584]{1,0:T(4,128)(2,1)S(1)} %collective-permute-done.13, bf16[4,3584]{1,0:T(4,128)(2,1)S(1)} %collective-permute-done.12, bf16[4,3584]{1,0:T(4,128)(2,1)S(1)} %collective-permute-done.11, bf16[16,3584]{1,0:T(8,128)(2,1)S(1)} %add_convert_fusion.1), kind=kLoop, calls=%fused_computation.44 | loop fusion | flops 114688 | bytes 143360 | tf_op jit(solution)/shard_map/broadcast_in_dim | solution.py:156
  (36 shorter events, 0.6 us)
Async XLA Ops:
  0.6 18.2 %copy-start = (bf16[1,32,16,576]{3,2,1,0:T(8,128)(2,1)S(1)}, bf16[1,32,16,576]{3,2,1,0:T(8,128)(2,1)}, u32[]{:S(2)}) copy-start(bf16[1,32,16,576]{3,2,1,0:T(8,128)(2,1)} %param.12) | copy-start | bytes 1769476
  2.2 5.6 %collective-permute-start = (bf16[1,4,3712]{2,1,0:T(4,128)(2,1)}, bf16[1,4,3712]{2,1,0:T(4,128)(2,1)S(1)}, u32[]{:S(2)}, u32[]{:S(2)}) collective-permute-start(bf16[1,4,3712]{2,1,0:T(4,128)(2,1)} %bitcast.64), channel_id=1, source_target_pairs={{0,8},{1,9},{2,10},{3,11},{4,12},{5,13},{6,14},{7,15},{8,0},{9,1},... | collective-permute-start | bytes 89096 | tf_op jit(solution)/shard_map/ppermute | solution.py:36
  5.2 5.5 %collective-permute-start.1 = (bf16[1,4,3712]{2,1,0:T(4,128)(2,1)}, bf16[1,4,3712]{2,1,0:T(4,128)(2,1)S(1)}, u32[]{:S(2)}, u32[]{:S(2)}) collective-permute-start(bf16[1,4,3712]{2,1,0:T(4,128)(2,1)} %bitcast.65), channel_id=1, source_target_pairs={{0,16},{1,17},{2,18},{3,19},{4,20},{5,21},{6,22},{7,23},{8,24},{9,... | collective-permute-start | bytes 89096 | tf_op jit(solution)/shard_map/ppermute | solution.py:36
  7.8 5.9 %collective-permute-start.2 = (bf16[1,4,3712]{2,1,0:T(4,128)(2,1)}, bf16[1,4,3712]{2,1,0:T(4,128)(2,1)S(1)}, u32[]{:S(2)}, u32[]{:S(2)}) collective-permute-start(bf16[1,4,3712]{2,1,0:T(4,128)(2,1)} %bitcast.66), channel_id=1, source_target_pairs={{0,24},{1,25},{2,26},{3,27},{4,28},{5,29},{6,30},{7,31},{8,16},{9,... | collective-permute-start | bytes 89096 | tf_op jit(solution)/shard_map/ppermute | solution.py:36
  14.6 9.7 %copy-start.1 = (s32[1,2,16]{2,1,0:T(2,128)S(1)}, s32[1,2,16]{2,1,0:T(2,128)}, u32[]{:S(2)}) copy-start(s32[1,2,16]{2,1,0:T(2,128)} %param.14) | copy-start | bytes 388
  14.6 9.8 %copy-start.2 = (s32[1,2]{1,0:T(1,128)S(1)}, s32[1,2]{1,0:T(1,128)}, u32[]{:S(2)}) copy-start(s32[1,2]{1,0:T(1,128)} %param.15) | copy-start | bytes 28
  14.6 9.3 %collective-permute-start.3 = (bf16[16,3712]{1,0:T(8,128)(2,1)S(1)}, bf16[16,3712]{1,0:T(8,128)(2,1)S(1)}, u32[]{:S(2)}, u32[]{:S(2)}) collective-permute-start(bf16[16,3712]{1,0:T(8,128)(2,1)S(1)} %reshape.111), channel_id=1, source_target_pairs={{0,1},{1,0},{2,3},{3,2},{4,5},{5,4},{6,7},{7,6},{8,9},{9,8},{10,11... | collective-permute-start | bytes 356360 | tf_op jit(solution)/shard_map/ppermute | solution.py:36
  16.2 7.8 %collective-permute-start.4 = (bf16[16,3712]{1,0:T(8,128)(2,1)S(1)}, bf16[16,3712]{1,0:T(8,128)(2,1)S(1)}, u32[]{:S(2)}, u32[]{:S(2)}) collective-permute-start(bf16[16,3712]{1,0:T(8,128)(2,1)S(1)} %reshape.111), channel_id=1, source_target_pairs={{0,4},{1,5},{2,6},{3,7},{4,0},{5,1},{6,2},{7,3},{8,12},{9,13},{10,... | collective-permute-start | bytes 356360 | tf_op jit(solution)/shard_map/ppermute | solution.py:36
  17.7 6.2 %collective-permute-start.5 = (bf16[16,3712]{1,0:T(8,128)(2,1)S(1)}, bf16[16,3712]{1,0:T(8,128)(2,1)S(1)}, u32[]{:S(2)}, u32[]{:S(2)}) collective-permute-start(bf16[16,3712]{1,0:T(8,128)(2,1)S(1)} %reshape.111), channel_id=1, source_target_pairs={{0,5},{1,4},{2,7},{3,6},{4,1},{5,0},{6,3},{7,2},{8,13},{9,12},{10,... | collective-permute-start | bytes 356360 | tf_op jit(solution)/shard_map/ppermute | solution.py:36
  20.3 21.1 %all-to-all-start = ((bf16[16,2,16,576]{3,2,1,0:T(8,128)(2,1)}), bf16[16,2,16,576]{3,2,1,0:T(8,128)(2,1)S(1)}, u32[]{:S(2)}, u32[]{:S(2)}) async-start(bf16[16,2,16,576]{3,2,1,0:T(8,128)(2,1)} %bitcast.3), calls=%async_computation | async-start | bytes 1310720 | tf_op jit(solution)/shard_map/all_to_all | solution.py:105
  24.0 1.9 %collective-permute-start.6 = (bf16[64,3712]{1,0:T(8,128)(2,1)S(1)}, bf16[64,3712]{1,0:T(8,128)(2,1)S(1)}, u32[]{:S(2)}, u32[]{:S(2)}) collective-permute-start(bf16[64,3712]{1,0:T(8,128)(2,1)S(1)} %pad_maximum_fusion.1), channel_id=1, source_target_pairs={{0,2},{1,3},{2,0},{3,1},{4,6},{5,7},{6,4},{7,5},{8,10},{9,11},{10,... | collective-permute-start | bytes 1425416 | tf_op jit(solution)/shard_map/ppermute | solution.py:36
  33.3 8.8 %copy-start.4 = (bf16[1,2,4,576]{3,2,1,0:T(4,128)(2,1)S(1)}, bf16[1,2,4,576]{3,2,1,0:T(4,128)(2,1)}, u32[]{:S(2)}) copy-start(bf16[1,2,4,576]{3,2,1,0:T(4,128)(2,1)} %param.16) | copy-start | bytes 27652
  33.3 1.9 %collective-permute-start.7 = (bf16[64,3584]{1,0:T(8,128)(2,1)S(1)}, bf16[64,3584]{1,0:T(8,128)(2,1)S(1)}, u32[]{:S(2)}, u32[]{:S(2)}) collective-permute-start(bf16[64,3584]{1,0:T(8,128)(2,1)S(1)} %slice.57), channel_id=1, source_target_pairs={{0,2},{1,3},{2,0},{3,1},{4,6},{5,7},{6,4},{7,5},{8,10},{9,11},{10,... | collective-permute-start | bytes 1376264 | tf_op jit(solution)/shard_map/ppermute | solution.py:36
  35.3 10.2 %collective-permute-start.10 = (bf16[16,3584]{1,0:T(8,128)(2,1)S(1)}, bf16[16,3584]{1,0:T(8,128)(2,1)S(1)}, u32[]{:S(2)}, u32[]{:S(2)}) collective-permute-start(bf16[16,3584]{1,0:T(8,128)(2,1)S(1)} %get-tuple-element.3), channel_id=1, source_target_pairs={{0,5},{1,4},{2,7},{3,6},{4,1},{5,0},{6,3},{7,2},{8,13},{9,12},{10,... | collective-permute-start | bytes 344072 | tf_op jit(solution)/shard_map/ppermute | solution.py:36
  38.1 7.4 %collective-permute-start.8 = (bf16[16,3584]{1,0:T(8,128)(2,1)S(1)}, bf16[16,3584]{1,0:T(8,128)(2,1)S(1)}, u32[]{:S(2)}, u32[]{:S(2)}) collective-permute-start(bf16[16,3584]{1,0:T(8,128)(2,1)S(1)} %get-tuple-element.2), channel_id=1, source_target_pairs={{0,1},{1,0},{2,3},{3,2},{4,5},{5,4},{6,7},{7,6},{8,9},{9,8},{10,11... | collective-permute-start | bytes 344072 | tf_op jit(solution)/shard_map/ppermute | solution.py:36
  38.7 6.8 %collective-permute-start.9 = (bf16[16,3584]{1,0:T(8,128)(2,1)S(1)}, bf16[16,3584]{1,0:T(8,128)(2,1)S(1)}, u32[]{:S(2)}, u32[]{:S(2)}) collective-permute-start(bf16[16,3584]{1,0:T(8,128)(2,1)S(1)} %get-tuple-element.4), channel_id=1, source_target_pairs={{0,4},{1,5},{2,6},{3,7},{4,0},{5,1},{6,2},{7,3},{8,12},{9,13},{10,... | collective-permute-start | bytes 344072 | tf_op jit(solution)/shard_map/ppermute | solution.py:36
  42.1 2.6 %copy-start.3 = (bf16[1,2,4,64,576]{4,3,2,1,0:T(8,128)(2,1)S(1)}, bf16[1,2,4,64,576]{4,3,2,1,0:T(8,128)(2,1)}, u32[]{:S(2)}) copy-start(bf16[1,2,4,64,576]{4,3,2,1,0:T(8,128)(2,1)} %param.17) | copy-start | bytes 1769476
  45.6 7.8 %collective-permute-start.11 = (bf16[4,3584]{1,0:T(4,128)(2,1)S(1)}, bf16[4,3584]{1,0:T(4,128)(2,1)S(1)}, u32[]{:S(2)}, u32[]{:S(2)}) collective-permute-start(bf16[4,3584]{1,0:T(4,128)(2,1)S(1)} %get-tuple-element.5), channel_id=1, source_target_pairs={{0,8},{1,9},{2,10},{3,11},{4,12},{5,13},{6,14},{7,15},{8,0},{9,1},... | collective-permute-start | bytes 86024 | tf_op jit(solution)/shard_map/ppermute | solution.py:36
  46.8 6.6 %collective-permute-start.12 = (bf16[4,3584]{1,0:T(4,128)(2,1)S(1)}, bf16[4,3584]{1,0:T(4,128)(2,1)S(1)}, u32[]{:S(2)}, u32[]{:S(2)}) collective-permute-start(bf16[4,3584]{1,0:T(4,128)(2,1)S(1)} %get-tuple-element.7), channel_id=1, source_target_pairs={{0,16},{1,17},{2,18},{3,19},{4,20},{5,21},{6,22},{7,23},{8,24},{9,... | collective-permute-start | bytes 86024 | tf_op jit(solution)/shard_map/ppermute | solution.py:36
  48.9 5.7 %collective-permute-start.13 = (bf16[4,3584]{1,0:T(4,128)(2,1)S(1)}, bf16[4,3584]{1,0:T(4,128)(2,1)S(1)}, u32[]{:S(2)}, u32[]{:S(2)}) collective-permute-start(bf16[4,3584]{1,0:T(4,128)(2,1)S(1)} %get-tuple-element.6), channel_id=1, source_target_pairs={{0,24},{1,25},{2,26},{3,27},{4,28},{5,29},{6,30},{7,31},{8,16},{9,... | collective-permute-start | bytes 86024 | tf_op jit(solution)/shard_map/ppermute | solution.py:36

commit v6 on v4

--- a/solution.py
+++ b/solution.py
@@ -44,6 +44,7 @@
     allowed = in_cache[:, None, :] | in_new[None, :, :]
     scores = jnp.where(allowed[:, :, None, :], scores, -jnp.inf)
     top = jnp.max(scores, axis=-1, keepdims=True)
+    scores, top = lax.optimization_barrier((scores, top))
     weights = jnp.exp(scores - top)
     weights = (weights / jnp.sum(weights, axis=-1, keepdims=True)).astype(jnp.bfloat16)
     values = keys[:, :, :VDIM]

time: 54.9 us -> 54.9 us (level)
  matrix products: 13.8 us -> 10.2 us
  waiting for transfers between devices: 12.3 us -> 15.7 us
    ppermute x14, waiting for transfers between devices: 9.8 us -> 13.1 us  [exchange(): return lax.ppermute(value, RANK, [(at, at ^ mask) for at in range(count)])]
    dot_general x1, matrix products: 3.3 us -> 1.29 us  [attend(): jnp.einsum('rshk,rkv->rshv', weights, values, preferred_element_type=jnp....]
    dot_general x1, matrix products: 2.59 us -> 1.74 us  [attend(): jnp.einsum('rshl,rkl->rshk', queries, keys, preferred_element_type=jnp.fl...]
    sub x1 -> x0, matrix products: 0.75 us -> none  [attend(): weights = jnp.exp(scores - top)]
  transfers between devices with their start and end apart: 15 -> 15, of which waited for: 6 -> 9; matrix products, arithmetic and copies ran while one was open for 32% -> 25% of each run, Pallas kernels for 0% -> 0%
where the time goes in v6:
time: 54.9 us; the launch traced here: 54.5 us
  starting transfers between devices  21.5 us (39%)
  waiting for transfers between devices  15.7 us (29%)
  matrix products  10.2 us (19%)
  other arithmetic  3.94 us (7%)
  local copies, waits for them, and re-layouts  2.38 us (4%)
  between operations  0.81 us (1%)
    ppermute x14, starting transfers between devices, exchange(): return lax.ppermute(value, RANK, [(at, at ^ mask) for at in range(count)])  17.9 us
    ppermute x14, waiting for transfers between devices, exchange(): return lax.ppermute(value, RANK, [(at, at ^ mask) for at in range(count)])  13.1 us
    dot_general x1, matrix products, body(): jnp.dot(hidden, expert_down[own], preferred_element_type=jnp.float32)  4.46 us
    all_to_all x1, starting transfers between devices, body(): lax.all_to_all(picked_pages.reshape(peers, capp, page_len, width_lat), 'd...  3.59 us
    dot_general x1, matrix products, body(): up = jnp.dot(every, expert_up[own], preferred_element_type=jnp.float32)  2.68 us
    all_to_all x1, waiting for transfers between devices, body(): lax.all_to_all(picked_pages.reshape(peers, capp, page_len, width_lat), 'd...  2.55 us
    dot_general x1, matrix products, attend(): jnp.einsum('rshl,rkl->rshk', queries, keys, preferred_element_type=jnp.fl...  1.74 us
    gather x1, local copies, waits for them, and re-layouts, body(): picked_pages = pages[jnp.maximum(outgoing_slots, 0)]  1.47 us
  transfers between devices with their start and end apart: 15, of which 9 were waited for; matrix products, arithmetic and copies ran while one was open for 25% of the time, Pallas kernels for 0%

profile of v6, /device:TPU:0, one launch (start us, length us, event | category | flops | bytes accessed | tf_op | source)
XLA Modules:
  0.0 54.5 jit_solution(16813193067551090373)
XLA Ops:
  0.6 0.8 %select_reduce_fusion = f32[4,16]{1,0:T(4,128)S(1)} fusion(f32[4,8]{1,0:T(4,128)} %bitcast.58, s32[4,8]{1,0:T(4,128)} %bitcast.59), kind=kLoop, calls=%fused_computation.46 | loop fusion | flops 1472 | bytes 512 | tf_op jit(solution)/shard_map/reduce_sum | solution.py:90
  1.6 0.8 %maximum_bitcast_fusion = bf16[1,4,3712]{2,1,0:T(4,128)(2,1)S(1)} fusion(bf16[4,128]{1,0:T(4,128)(2,1)S(1)} %fusion.31, bf16[4,3584]{1,0:T(4,128)(2,1)} %bitcast.57), kind=kLoop, calls=%fused_computation.44 | loop fusion | flops 59392 | bytes 59392 | tf_op jit(solution)/shard_map/broadcast_in_dim | solution.py:97
  2.4 3.1 %collective-permute-start = (bf16[1,4,3712]{2,1,0:T(4,128)(2,1)S(1)}, bf16[1,4,3712]{2,1,0:T(4,128)(2,1)S(1)}, u32[]{:S(2)}, u32[]{:S(2)}) collective-permute-start(bf16[1,4,3712]{2,1,0:T(4,128)(2,1)S(1)} %maximum_bitcast_fusion), channel_id=1, source_target_pairs={{0,8},{1,9},{2,10},{3,11},{4,12},{5,13},{6,14},{7,15},{8,0},{9,1},... | collective-permute-start | bytes 89096 | tf_op jit(solution)/shard_map/ppermute | solution.py:32
  5.4 2.6 %collective-permute-start.1 = (bf16[1,4,3712]{2,1,0:T(4,128)(2,1)S(1)}, bf16[1,4,3712]{2,1,0:T(4,128)(2,1)S(1)}, u32[]{:S(2)}, u32[]{:S(2)}) collective-permute-start(bf16[1,4,3712]{2,1,0:T(4,128)(2,1)S(1)} %maximum_bitcast_fusion), channel_id=1, source_target_pairs={{0,16},{1,17},{2,18},{3,19},{4,20},{5,21},{6,22},{7,23},{8,24},{9,... | collective-permute-start | bytes 89096 | tf_op jit(solution)/shard_map/ppermute | solution.py:32
  8.0 2.7 %collective-permute-done.1 = bf16[1,4,3712]{2,1,0:T(4,128)(2,1)S(1)} collective-permute-done((bf16[1,4,3712]{2,1,0:T(4,128)(2,1)S(1)}, bf16[1,4,3712]{2,1,0:T(4,128)(2,1)S(1)}, u32[]{:S(2)}, u32[]{:S(2)}) %collective-permute-start.1) | collective-permute-done | bytes 29728 | tf_op jit(solution)/shard_map/ppermute | solution.py:32
  10.7 3.0 %collective-permute-done.2 = bf16[1,4,3712]{2,1,0:T(4,128)(2,1)S(1)} collective-permute-done((bf16[1,4,3712]{2,1,0:T(4,128)(2,1)S(1)}, bf16[1,4,3712]{2,1,0:T(4,128)(2,1)S(1)}, u32[]{:S(2)}, u32[]{:S(2)}) %collective-permute-start.2) | collective-permute-done | bytes 29728 | tf_op jit(solution)/shard_map/ppermute | solution.py:32
  13.9 1.6 %collective-permute-start.3 = (bf16[16,3712]{1,0:T(8,128)(2,1)S(1)}, bf16[16,3712]{1,0:T(8,128)(2,1)S(1)}, u32[]{:S(2)}, u32[]{:S(2)}) collective-permute-start(bf16[16,3712]{1,0:T(8,128)(2,1)S(1)} %reshape.112), channel_id=1, source_target_pairs={{0,1},{1,0},{2,3},{3,2},{4,5},{5,4},{6,7},{7,6},{8,9},{9,8},{10,11... | collective-permute-start | bytes 356360 | tf_op jit(solution)/shard_map/ppermute | solution.py:32
  15.4 1.5 %collective-permute-start.4 = (bf16[16,3712]{1,0:T(8,128)(2,1)S(1)}, bf16[16,3712]{1,0:T(8,128)(2,1)S(1)}, u32[]{:S(2)}, u32[]{:S(2)}) collective-permute-start(bf16[16,3712]{1,0:T(8,128)(2,1)S(1)} %reshape.112), channel_id=1, source_target_pairs={{0,4},{1,5},{2,6},{3,7},{4,0},{5,1},{6,2},{7,3},{8,12},{9,13},{10,... | collective-permute-start | bytes 356360 | tf_op jit(solution)/shard_map/ppermute | solution.py:32
  17.0 0.5 collective-permute-start.5
  17.4 0.7 %maximum_bitcast_fusion.1 = s32[32]{0:T(128)S(1)} fusion(s32[1,32]{1,0:T(1,128)} %param.13), kind=kLoop, calls=%fused_computation.62 | loop fusion | flops 32 | bytes 256 | tf_op jit(solution)/shard_map/max | solution.py:75
  18.1 1.5 %gather_fusion = bf16[32,16,576]{2,1,0:T(8,128)(2,1)} fusion(bf16[32,16,576]{2,1,0:T(8,128)(2,1)S(1)} %bitcast.53, s32[1024]{0:T(1024)S(1)} %pad_clamp_fusion.1), kind=kCustom, calls=%fused_computation | custom fusion | bytes 1179776 | tf_op jit(solution)/shard_map/gather | solution.py:75
  19.6 3.6 %all-to-all-start = ((bf16[16,2,16,576]{3,2,1,0:T(8,128)(2,1)}), bf16[16,2,16,576]{3,2,1,0:T(8,128)(2,1)S(1)}, u32[]{:S(2)}, u32[]{:S(2)}) async-start(bf16[16,2,16,576]{3,2,1,0:T(8,128)(2,1)} %bitcast.3), calls=%async_computation | async-start | bytes 1310720 | tf_op jit(solution)/shard_map/all_to_all | solution.py:76
  23.2 0.4 collective-permute-start.6
  23.8 1.4 %collective-permute-done.6 = bf16[64,3712]{1,0:T(8,128)(2,1)S(1)} collective-permute-done((bf16[64,3712]{1,0:T(8,128)(2,1)S(1)}, bf16[64,3712]{1,0:T(8,128)(2,1)S(1)}, u32[]{:S(2)}, u32[]{:S(2)}) %collective-permute-start.6) | collective-permute-done | bytes 475168 | tf_op jit(solution)/shard_map/ppermute | solution.py:32
  25.2 2.7 %fusion.2 = f32[128,512]{1,0:T(8,128)S(1)} fusion(bf16[1,3584,512]{2,1,0:T(8,128)(2,1)} %param.22, bf16[64,3712]{1,0:T(8,128)(2,1)S(1)} %pad_maximum_fusion.1, bf16[64,3712]{1,0:T(8,128)(2,1)S(1)} %collective-permute-done.6), kind=kOutput, calls=%fused_computation.5 | convolution fusion | flops 471597056 | bytes 4882432 | tf_op jit(solution)/shard_map/dot_general | solution.py:115
  28.0 4.5 %fusion = bf16[128,3584]{1,0:T(8,128)(2,1)S(1)} fusion(bf16[1,512,3584]{2,1,0:T(8,128)(2,1)} %param.23, f32[128]{0:T(128)S(1)} %add_reduce_fusion, f32[128,512]{1,0:T(8,128)S(1)} %fusion.2, bf16[1,3584,512]{2,1,0:T(8,128)(2,1)} %param.21, bf16[64,3712]{1,0:T(8,128)(2,1)S(1)} %pad_maximum_fusion.1, bf16[64,3712]{1,0:T(8,128)(2,1)S(1)} %collective-permute-done.6), kind=kOutput, calls=%fused_computation.3 | convolution fusion | flops 942669824 | bytes 9470464 | tf_op jit(solution)/shard_map/dot_general | solution.py:117
  32.5 0.4 collective-permute-start.7
  32.9 1.5 %collective-permute-done.7 = bf16[64,3584]{1,0:T(8,128)(2,1)S(1)} collective-permute-done((bf16[64,3584]{1,0:T(8,128)(2,1)S(1)}, bf16[64,3584]{1,0:T(8,128)(2,1)S(1)}, u32[]{:S(2)}, u32[]{:S(2)}) %collective-permute-start.7) | collective-permute-done | bytes 458784 | tf_op jit(solution)/shard_map/ppermute | solution.py:32
  34.6 2.8 %collective-permute-start.10 = (bf16[16,3584]{1,0:T(8,128)(2,1)S(1)}, bf16[16,3584]{1,0:T(8,128)(2,1)S(1)}, u32[]{:S(2)}, u32[]{:S(2)}) collective-permute-start(bf16[16,3584]{1,0:T(8,128)(2,1)S(1)} %get-tuple-element.9), channel_id=1, source_target_pairs={{0,5},{1,4},{2,7},{3,6},{4,1},{5,0},{6,3},{7,2},{8,13},{9,12},{10,... | collective-permute-start | bytes 344072 | tf_op jit(solution)/shard_map/ppermute | solution.py:32
  37.4 0.5 collective-permute-start.8
  38.1 2.5 %all-to-all-done = bf16[16,2,16,576]{3,2,1,0:T(8,128)(2,1)S(1)} async-done(((bf16[16,2,16,576]{3,2,1,0:T(8,128)(2,1)}), bf16[16,2,16,576]{3,2,1,0:T(8,128)(2,1)S(1)}, u32[]{:S(2)}, u32[]{:S(2)}) %all-to-all-start) | async-done | bytes 589856 | tf_op jit(solution)/shard_map/all_to_all | solution.py:76
  40.7 0.7 %gather_fusion.1 = bf16[32,16,576]{2,1,0:T(8,128)(2,1)S(1)} fusion(bf16[32,16,576]{2,1,0:T(8,128)(2,1)S(1)} %bitcast.54, s32[1024]{0:T(1024)S(1)} %pad_clamp_fusion), kind=kCustom, calls=%fused_computation.1 | custom fusion | bytes 1179776 | tf_op jit(solution)/shard_map/gather | solution.py:131
  41.4 1.7 %fusion.40 = (f32[2,4,64]{2,1,0:T(4,128)S(1)}, f32[2,4,64,260]{3,2,1,0:T(8,128)S(1)}) fusion(bf16[1,2,4,64,576]{4,3,2,1,0:T(8,128)(2,1)} %param.17, bf16[2,4,576]{2,1,0:T(4,128)(2,1)S(1)} %bitcast.61, bf16[2,256,576]{2,1,0:T(8,128)(2,1)S(1)} %bitcast.55, pred[2,4,260]{2,1,0:T(4,128)(4,1)S(1)} %broadcast_or_fusion), kind=kOutput, calls=%fused_computation.68 | convolution fusion | flops 154951168 | bytes 1725472 | tf_op jit(solution)/shard_map/rshl,rkl->rshk/dot_general | solution.py:39
  43.4 0.5 collective-permute-done.8
  43.9 0.6 %collective-permute-done.9 = bf16[16,3584]{1,0:T(8,128)(2,1)S(1)} collective-permute-done((bf16[16,3584]{1,0:T(8,128)(2,1)S(1)}, bf16[16,3584]{1,0:T(8,128)(2,1)S(1)}, u32[]{:S(2)}, u32[]{:S(2)}) %collective-permute-start.9) | collective-permute-done | bytes 114720 | tf_op jit(solution)/shard_map/ppermute | solution.py:32
  44.6 1.5 %collective-permute-start.11 = (bf16[4,3584]{1,0:T(4,128)(2,1)S(1)}, bf16[4,3584]{1,0:T(4,128)(2,1)S(1)}, u32[]{:S(2)}, u32[]{:S(2)}) collective-permute-start(bf16[4,3584]{1,0:T(4,128)(2,1)S(1)} %get-tuple-element.11), channel_id=1, source_target_pairs={{0,8},{1,9},{2,10},{3,11},{4,12},{5,13},{6,14},{7,15},{8,0},{9,1},... | collective-permute-start | bytes 86024 | tf_op jit(solution)/shard_map/ppermute | solution.py:32
  46.1 2.1 %collective-permute-start.12 = (bf16[4,3584]{1,0:T(4,128)(2,1)S(1)}, bf16[4,3584]{1,0:T(4,128)(2,1)S(1)}, u32[]{:S(2)}, u32[]{:S(2)}) collective-permute-start(bf16[4,3584]{1,0:T(4,128)(2,1)S(1)} %get-tuple-element.13), channel_id=1, source_target_pairs={{0,16},{1,17},{2,18},{3,19},{4,20},{5,21},{6,22},{7,23},{8,24},{9,... | collective-permute-start | bytes 86024 | tf_op jit(solution)/shard_map/ppermute | solution.py:32
  48.2 0.9 %collective-permute-start.13 = (bf16[4,3584]{1,0:T(4,128)(2,1)S(1)}, bf16[4,3584]{1,0:T(4,128)(2,1)S(1)}, u32[]{:S(2)}, u32[]{:S(2)}) collective-permute-start(bf16[4,3584]{1,0:T(4,128)(2,1)S(1)} %get-tuple-element.12), channel_id=1, source_target_pairs={{0,24},{1,25},{2,26},{3,27},{4,28},{5,29},{6,30},{7,31},{8,16},{9,... | collective-permute-start | bytes 86024 | tf_op jit(solution)/shard_map/ppermute | solution.py:32
  49.1 1.3 %fusion.8 = bf16[1,2,4,64,512]{4,3,2,1,0:T(8,128)(2,1)} fusion(bf16[2,256,576]{2,1,0:T(8,128)(2,1)S(1)} %bitcast.56, bf16[2,4,576]{2,1,0:T(4,128)(2,1)S(1)} %bitcast.62, f32[2,4,64,260]{3,2,1,0:T(8,128)S(1)} %get-tuple-element.4, f32[2,4,64]{2,1,0:T(4,128)S(1)} %fusion.10, f32[2,4,64]{2,1,0:T(4,128)S(1)} %get-tuple-element.14), kind=kOutput, calls=%fused_computation.13 | convolution fusion | flops 138041344 | bytes 1659904 | tf_op jit(solution)/shard_map/rshk,rkv->rshv/dot_general | solution.py:51
  50.4 1.4 %collective-permute-done.12 = bf16[4,3584]{1,0:T(4,128)(2,1)S(1)} collective-permute-done((bf16[4,3584]{1,0:T(4,128)(2,1)S(1)}, bf16[4,3584]{1,0:T(4,128)(2,1)S(1)}, u32[]{:S(2)}, u32[]{:S(2)}) %collective-permute-start.12) | collective-permute-done | bytes 28704 | tf_op jit(solution)/shard_map/ppermute | solution.py:32
  51.8 2.1 %collective-permute-done.13 = bf16[4,3584]{1,0:T(4,128)(2,1)S(1)} collective-permute-done((bf16[4,3584]{1,0:T(4,128)(2,1)S(1)}, bf16[4,3584]{1,0:T(4,128)(2,1)S(1)}, u32[]{:S(2)}, u32[]{:S(2)}) %collective-permute-start.13) | collective-permute-done | bytes 28704 | tf_op jit(solution)/shard_map/ppermute | solution.py:32
  53.9 0.6 %fusion.27 = bf16[1,4,3584]{2,1,0:T(4,128)(2,1)} fusion(bf16[4,3584]{1,0:T(4,128)(2,1)S(1)} %collective-permute-done.13, bf16[4,3584]{1,0:T(4,128)(2,1)S(1)} %collective-permute-done.12, bf16[4,3584]{1,0:T(4,128)(2,1)S(1)} %collective-permute-done.11, bf16[16,3584]{1,0:T(8,128)(2,1)S(1)} %add_convert_fusion.1), kind=kLoop, calls=%fused_computation.45 | loop fusion | flops 114688 | bytes 143360 | tf_op jit(solution)/shard_map/broadcast_in_dim | solution.py:133
  (37 shorter events, 1.5 us)
Async XLA Ops:
  0.6 17.5 %copy-start = (bf16[1,32,16,576]{3,2,1,0:T(8,128)(2,1)S(1)}, bf16[1,32,16,576]{3,2,1,0:T(8,128)(2,1)}, u32[]{:S(2)}) copy-start(bf16[1,32,16,576]{3,2,1,0:T(8,128)(2,1)} %param.12) | copy-start | bytes 1769476
  2.4 5.7 %collective-permute-start = (bf16[1,4,3712]{2,1,0:T(4,128)(2,1)S(1)}, bf16[1,4,3712]{2,1,0:T(4,128)(2,1)S(1)}, u32[]{:S(2)}, u32[]{:S(2)}) collective-permute-start(bf16[1,4,3712]{2,1,0:T(4,128)(2,1)S(1)} %maximum_bitcast_fusion), channel_id=1, source_target_pairs={{0,8},{1,9},{2,10},{3,11},{4,12},{5,13},{6,14},{7,15},{8,0},{9,1},... | collective-permute-start | bytes 89096 | tf_op jit(solution)/shard_map/ppermute | solution.py:32
  5.4 5.3 %collective-permute-start.1 = (bf16[1,4,3712]{2,1,0:T(4,128)(2,1)S(1)}, bf16[1,4,3712]{2,1,0:T(4,128)(2,1)S(1)}, u32[]{:S(2)}, u32[]{:S(2)}) collective-permute-start(bf16[1,4,3712]{2,1,0:T(4,128)(2,1)S(1)} %maximum_bitcast_fusion), channel_id=1, source_target_pairs={{0,16},{1,17},{2,18},{3,19},{4,20},{5,21},{6,22},{7,23},{8,24},{9,... | collective-permute-start | bytes 89096 | tf_op jit(solution)/shard_map/ppermute | solution.py:32
  8.0 5.7 %collective-permute-start.2 = (bf16[1,4,3712]{2,1,0:T(4,128)(2,1)S(1)}, bf16[1,4,3712]{2,1,0:T(4,128)(2,1)S(1)}, u32[]{:S(2)}, u32[]{:S(2)}) collective-permute-start(bf16[1,4,3712]{2,1,0:T(4,128)(2,1)S(1)} %maximum_bitcast_fusion), channel_id=1, source_target_pairs={{0,24},{1,25},{2,26},{3,27},{4,28},{5,29},{6,30},{7,31},{8,16},{9,... | collective-permute-start | bytes 89096 | tf_op jit(solution)/shard_map/ppermute | solution.py:32
  13.9 9.7 %copy-start.1 = (s32[1,2,16]{2,1,0:T(2,128)S(1)}, s32[1,2,16]{2,1,0:T(2,128)}, u32[]{:S(2)}) copy-start(s32[1,2,16]{2,1,0:T(2,128)} %param.14) | copy-start | bytes 388
  13.9 9.8 %copy-start.2 = (s32[1,2]{1,0:T(1,128)S(1)}, s32[1,2]{1,0:T(1,128)}, u32[]{:S(2)}) copy-start(s32[1,2]{1,0:T(1,128)} %param.15) | copy-start | bytes 28
  13.9 9.3 %collective-permute-start.3 = (bf16[16,3712]{1,0:T(8,128)(2,1)S(1)}, bf16[16,3712]{1,0:T(8,128)(2,1)S(1)}, u32[]{:S(2)}, u32[]{:S(2)}) collective-permute-start(bf16[16,3712]{1,0:T(8,128)(2,1)S(1)} %reshape.112), channel_id=1, source_target_pairs={{0,1},{1,0},{2,3},{3,2},{4,5},{5,4},{6,7},{7,6},{8,9},{9,8},{10,11... | collective-permute-start | bytes 356360 | tf_op jit(solution)/shard_map/ppermute | solution.py:32
  15.4 7.8 %collective-permute-start.4 = (bf16[16,3712]{1,0:T(8,128)(2,1)S(1)}, bf16[16,3712]{1,0:T(8,128)(2,1)S(1)}, u32[]{:S(2)}, u32[]{:S(2)}) collective-permute-start(bf16[16,3712]{1,0:T(8,128)(2,1)S(1)} %reshape.112), channel_id=1, source_target_pairs={{0,4},{1,5},{2,6},{3,7},{4,0},{5,1},{6,2},{7,3},{8,12},{9,13},{10,... | collective-permute-start | bytes 356360 | tf_op jit(solution)/shard_map/ppermute | solution.py:32
  17.0 6.2 %collective-permute-start.5 = (bf16[16,3712]{1,0:T(8,128)(2,1)S(1)}, bf16[16,3712]{1,0:T(8,128)(2,1)S(1)}, u32[]{:S(2)}, u32[]{:S(2)}) collective-permute-start(bf16[16,3712]{1,0:T(8,128)(2,1)S(1)} %reshape.112), channel_id=1, source_target_pairs={{0,5},{1,4},{2,7},{3,6},{4,1},{5,0},{6,3},{7,2},{8,13},{9,12},{10,... | collective-permute-start | bytes 356360 | tf_op jit(solution)/shard_map/ppermute | solution.py:32
  19.6 21.1 %all-to-all-start = ((bf16[16,2,16,576]{3,2,1,0:T(8,128)(2,1)}), bf16[16,2,16,576]{3,2,1,0:T(8,128)(2,1)S(1)}, u32[]{:S(2)}, u32[]{:S(2)}) async-start(bf16[16,2,16,576]{3,2,1,0:T(8,128)(2,1)} %bitcast.3), calls=%async_computation | async-start | bytes 1310720 | tf_op jit(solution)/shard_map/all_to_all | solution.py:76
  23.2 1.9 %collective-permute-start.6 = (bf16[64,3712]{1,0:T(8,128)(2,1)S(1)}, bf16[64,3712]{1,0:T(8,128)(2,1)S(1)}, u32[]{:S(2)}, u32[]{:S(2)}) collective-permute-start(bf16[64,3712]{1,0:T(8,128)(2,1)S(1)} %pad_maximum_fusion.1), channel_id=1, source_target_pairs={{0,2},{1,3},{2,0},{3,1},{4,6},{5,7},{6,4},{7,5},{8,10},{9,11},{10,... | collective-permute-start | bytes 1425416 | tf_op jit(solution)/shard_map/ppermute | solution.py:32
  32.5 8.8 %copy-start.3 = (bf16[1,2,4,576]{3,2,1,0:T(4,128)(2,1)S(1)}, bf16[1,2,4,576]{3,2,1,0:T(4,128)(2,1)}, u32[]{:S(2)}) copy-start(bf16[1,2,4,576]{3,2,1,0:T(4,128)(2,1)} %param.16) | copy-start | bytes 27652
  32.5 1.9 %collective-permute-start.7 = (bf16[64,3584]{1,0:T(8,128)(2,1)S(1)}, bf16[64,3584]{1,0:T(8,128)(2,1)S(1)}, u32[]{:S(2)}, u32[]{:S(2)}) collective-permute-start(bf16[64,3584]{1,0:T(8,128)(2,1)S(1)} %slice.57), channel_id=1, source_target_pairs={{0,2},{1,3},{2,0},{3,1},{4,6},{5,7},{6,4},{7,5},{8,10},{9,11},{10,... | collective-permute-start | bytes 1376264 | tf_op jit(solution)/shard_map/ppermute | solution.py:32
  34.6 8.8 %collective-permute-start.10 = (bf16[16,3584]{1,0:T(8,128)(2,1)S(1)}, bf16[16,3584]{1,0:T(8,128)(2,1)S(1)}, u32[]{:S(2)}, u32[]{:S(2)}) collective-permute-start(bf16[16,3584]{1,0:T(8,128)(2,1)S(1)} %get-tuple-element.9), channel_id=1, source_target_pairs={{0,5},{1,4},{2,7},{3,6},{4,1},{5,0},{6,3},{7,2},{8,13},{9,12},{10,... | collective-permute-start | bytes 344072 | tf_op jit(solution)/shard_map/ppermute | solution.py:32
  37.4 6.5 %collective-permute-start.8 = (bf16[16,3584]{1,0:T(8,128)(2,1)S(1)}, bf16[16,3584]{1,0:T(8,128)(2,1)S(1)}, u32[]{:S(2)}, u32[]{:S(2)}) collective-permute-start(bf16[16,3584]{1,0:T(8,128)(2,1)S(1)} %get-tuple-element.8), channel_id=1, source_target_pairs={{0,1},{1,0},{2,3},{3,2},{4,5},{5,4},{6,7},{7,6},{8,9},{9,8},{10,11... | collective-permute-start | bytes 344072 | tf_op jit(solution)/shard_map/ppermute | solution.py:32
  37.9 6.6 %collective-permute-start.9 = (bf16[16,3584]{1,0:T(8,128)(2,1)S(1)}, bf16[16,3584]{1,0:T(8,128)(2,1)S(1)}, u32[]{:S(2)}, u32[]{:S(2)}) collective-permute-start(bf16[16,3584]{1,0:T(8,128)(2,1)S(1)} %get-tuple-element.10), channel_id=1, source_target_pairs={{0,4},{1,5},{2,6},{3,7},{4,0},{5,1},{6,2},{7,3},{8,12},{9,13},{10,... | collective-permute-start | bytes 344072 | tf_op jit(solution)/shard_map/ppermute | solution.py:32
  44.6 5.8 %collective-permute-start.11 = (bf16[4,3584]{1,0:T(4,128)(2,1)S(1)}, bf16[4,3584]{1,0:T(4,128)(2,1)S(1)}, u32[]{:S(2)}, u32[]{:S(2)}) collective-permute-start(bf16[4,3584]{1,0:T(4,128)(2,1)S(1)} %get-tuple-element.11), channel_id=1, source_target_pairs={{0,8},{1,9},{2,10},{3,11},{4,12},{5,13},{6,14},{7,15},{8,0},{9,1},... | collective-permute-start | bytes 86024 | tf_op jit(solution)/shard_map/ppermute | solution.py:32
  46.1 5.7 %collective-permute-start.12 = (bf16[4,3584]{1,0:T(4,128)(2,1)S(1)}, bf16[4,3584]{1,0:T(4,128)(2,1)S(1)}, u32[]{:S(2)}, u32[]{:S(2)}) collective-permute-start(bf16[4,3584]{1,0:T(4,128)(2,1)S(1)} %get-tuple-element.13), channel_id=1, source_target_pairs={{0,16},{1,17},{2,18},{3,19},{4,20},{5,21},{6,22},{7,23},{8,24},{9,... | collective-permute-start | bytes 86024 | tf_op jit(solution)/shard_map/ppermute | solution.py:32
  48.2 5.7 %collective-permute-start.13 = (bf16[4,3584]{1,0:T(4,128)(2,1)S(1)}, bf16[4,3584]{1,0:T(4,128)(2,1)S(1)}, u32[]{:S(2)}, u32[]{:S(2)}) collective-permute-start(bf16[4,3584]{1,0:T(4,128)(2,1)S(1)} %get-tuple-element.12), channel_id=1, source_target_pairs={{0,24},{1,25},{2,26},{3,27},{4,28},{5,29},{6,30},{7,31},{8,16},{9,... | collective-permute-start | bytes 86024 | tf_op jit(solution)/shard_map/ppermute | solution.py:32

commit v7 on v6

--- a/solution.py
+++ b/solution.py
@@ -72,7 +72,7 @@
     outgoing_slots = send_page[0]
     page_len, width_lat = (pages.shape[1], pages.shape[2])
     capp = outgoing_slots.shape[0] // peers
-    picked_pages = pages[jnp.maximum(outgoing_slots, 0)]
+    picked_pages = pages.at[outgoing_slots].get(mode="clip", wrap_negative_indices=False)
     arrived = lax.all_to_all(
         picked_pages.reshape(peers, capp, page_len, width_lat),
         "dev",
@@ -128,7 +128,7 @@
 
     table = page_table[0]
     requests, most_pages = table.shape
-    cache = arrived[jnp.maximum(table, 0)].reshape(requests, most_pages * page_len, width_lat)
+    cache = arrived.at[table].get(mode="clip", wrap_negative_indices=False).reshape(requests, most_pages * page_len, width_lat)
     attended = attend(queries[0], new_latent[0], cache, context_len[0])
     return (attended[None], mixed[None])
 

time: 54.9 us -> 58.8 us (1.071)
  waiting for transfers between devices: 15.7 us -> 19.7 us
    ppermute x14, waiting for transfers between devices: 13.1 us -> 15.2 us  [exchange(): return lax.ppermute(value, RANK, [(at, at ^ mask) for at in range(count)])]
    all_to_all x1, waiting for transfers between devices: 2.55 us -> 4.55 us  [body(): lax.all_to_all(picked_pages.reshape(peers, capp, page_len, width_lat), 'd...]
    max x2 -> x0, other arithmetic: 0.66 us -> none  [the longest x1 0.66 us: body(): picked_pages = pages[jnp.maximum(outgoing_slots, 0)]]
    gather x2, other arithmetic: 0.01 us -> 0.67 us  [the longest x1 0.66 us: body(): pages.at[outgoing_slots].get(mode='clip', wrap_negative_indices=False)]
  transfers between devices with their start and end apart: 15 -> 15, of which waited for: 9 -> 8; matrix products, arithmetic and copies ran while one was open for 25% -> 24% of each run, Pallas kernels for 0% -> 0%
where the time goes in v7:
time: 58.8 us; the launch traced here: 58.4 us
  starting transfers between devices  21.4 us (36%)
  waiting for transfers between devices  19.7 us (34%)
  matrix products  10.2 us (17%)
  other arithmetic  3.92 us (7%)
  local copies, waits for them, and re-layouts  2.37 us (4%)
  between operations  0.82 us (1%)
    ppermute x14, starting transfers between devices, exchange(): return lax.ppermute(value, RANK, [(at, at ^ mask) for at in range(count)])  17.8 us
    ppermute x14, waiting for transfers between devices, exchange(): return lax.ppermute(value, RANK, [(at, at ^ mask) for at in range(count)])  15.2 us
    all_to_all x1, waiting for transfers between devices, body(): lax.all_to_all(picked_pages.reshape(peers, capp, page_len, width_lat), 'd...  4.55 us
    dot_general x1, matrix products, body(): jnp.dot(hidden, expert_down[own], preferred_element_type=jnp.float32)  4.46 us
    all_to_all x1, starting transfers between devices, body(): lax.all_to_all(picked_pages.reshape(peers, capp, page_len, width_lat), 'd...  3.59 us
    dot_general x1, matrix products, body(): up = jnp.dot(every, expert_up[own], preferred_element_type=jnp.float32)  2.68 us
    dot_general x1, matrix products, attend(): jnp.einsum('rshl,rkl->rshk', queries, keys, preferred_element_type=jnp.fl...  1.74 us
    gather x1, local copies, waits for them, and re-layouts, body(): pages.at[outgoing_slots].get(mode='clip', wrap_negative_indices=False)  1.47 us
  transfers between devices with their start and end apart: 15, of which 8 were waited for; matrix products, arithmetic and copies ran while one was open for 24% of the time, Pallas kernels for 0%

profile of v7, /device:TPU:0, one launch (start us, length us, event | category | flops | bytes accessed | tf_op | source)
XLA Modules:
  0.0 58.4 jit_solution(15324061103554444797)
XLA Ops:
  0.6 0.8 %select_reduce_fusion = f32[4,16]{1,0:T(4,128)S(1)} fusion(f32[4,8]{1,0:T(4,128)} %bitcast.57, s32[4,8]{1,0:T(4,128)} %bitcast.58), kind=kLoop, calls=%fused_computation.46 | loop fusion | flops 1472 | bytes 512 | tf_op jit(solution)/shard_map/reduce_sum | solution.py:90
  1.6 0.8 %maximum_bitcast_fusion = bf16[1,4,3712]{2,1,0:T(4,128)(2,1)S(1)} fusion(bf16[4,128]{1,0:T(4,128)(2,1)S(1)} %fusion.31, bf16[4,3584]{1,0:T(4,128)(2,1)} %bitcast.56), kind=kLoop, calls=%fused_computation.44 | loop fusion | flops 59392 | bytes 59392 | tf_op jit(solution)/shard_map/broadcast_in_dim | solution.py:97
  2.4 3.1 %collective-permute-start = (bf16[1,4,3712]{2,1,0:T(4,128)(2,1)S(1)}, bf16[1,4,3712]{2,1,0:T(4,128)(2,1)S(1)}, u32[]{:S(2)}, u32[]{:S(2)}) collective-permute-start(bf16[1,4,3712]{2,1,0:T(4,128)(2,1)S(1)} %maximum_bitcast_fusion), channel_id=1, source_target_pairs={{0,8},{1,9},{2,10},{3,11},{4,12},{5,13},{6,14},{7,15},{8,0},{9,1},... | collective-permute-start | bytes 89096 | tf_op jit(solution)/shard_map/ppermute | solution.py:32
  5.4 2.6 %collective-permute-start.1 = (bf16[1,4,3712]{2,1,0:T(4,128)(2,1)S(1)}, bf16[1,4,3712]{2,1,0:T(4,128)(2,1)S(1)}, u32[]{:S(2)}, u32[]{:S(2)}) collective-permute-start(bf16[1,4,3712]{2,1,0:T(4,128)(2,1)S(1)} %maximum_bitcast_fusion), channel_id=1, source_target_pairs={{0,16},{1,17},{2,18},{3,19},{4,20},{5,21},{6,22},{7,23},{8,24},{9,... | collective-permute-start | bytes 89096 | tf_op jit(solution)/shard_map/ppermute | solution.py:32
  8.0 2.7 %collective-permute-done.1 = bf16[1,4,3712]{2,1,0:T(4,128)(2,1)S(1)} collective-permute-done((bf16[1,4,3712]{2,1,0:T(4,128)(2,1)S(1)}, bf16[1,4,3712]{2,1,0:T(4,128)(2,1)S(1)}, u32[]{:S(2)}, u32[]{:S(2)}) %collective-permute-start.1) | collective-permute-done | bytes 29728 | tf_op jit(solution)/shard_map/ppermute | solution.py:32
  10.7 3.0 %collective-permute-done.2 = bf16[1,4,3712]{2,1,0:T(4,128)(2,1)S(1)} collective-permute-done((bf16[1,4,3712]{2,1,0:T(4,128)(2,1)S(1)}, bf16[1,4,3712]{2,1,0:T(4,128)(2,1)S(1)}, u32[]{:S(2)}, u32[]{:S(2)}) %collective-permute-start.2) | collective-permute-done | bytes 29728 | tf_op jit(solution)/shard_map/ppermute | solution.py:32
  13.9 1.6 %collective-permute-start.3 = (bf16[16,3712]{1,0:T(8,128)(2,1)S(1)}, bf16[16,3712]{1,0:T(8,128)(2,1)S(1)}, u32[]{:S(2)}, u32[]{:S(2)}) collective-permute-start(bf16[16,3712]{1,0:T(8,128)(2,1)S(1)} %reshape.88), channel_id=1, source_target_pairs={{0,1},{1,0},{2,3},{3,2},{4,5},{5,4},{6,7},{7,6},{8,9},{9,8},{10,11... | collective-permute-start | bytes 356360 | tf_op jit(solution)/shard_map/ppermute | solution.py:32
  15.4 1.5 %collective-permute-start.4 = (bf16[16,3712]{1,0:T(8,128)(2,1)S(1)}, bf16[16,3712]{1,0:T(8,128)(2,1)S(1)}, u32[]{:S(2)}, u32[]{:S(2)}) collective-permute-start(bf16[16,3712]{1,0:T(8,128)(2,1)S(1)} %reshape.88), channel_id=1, source_target_pairs={{0,4},{1,5},{2,6},{3,7},{4,0},{5,1},{6,2},{7,3},{8,12},{9,13},{10,... | collective-permute-start | bytes 356360 | tf_op jit(solution)/shard_map/ppermute | solution.py:32
  17.0 0.5 collective-permute-start.5
  17.4 2.3 %collective-permute-done.3 = bf16[16,3712]{1,0:T(8,128)(2,1)S(1)} collective-permute-done((bf16[16,3712]{1,0:T(8,128)(2,1)S(1)}, bf16[16,3712]{1,0:T(8,128)(2,1)S(1)}, u32[]{:S(2)}, u32[]{:S(2)}) %collective-permute-start.3) | collective-permute-done | bytes 118816 | tf_op jit(solution)/shard_map/ppermute | solution.py:32
  19.7 1.3 %collective-permute-done.4 = bf16[16,3712]{1,0:T(8,128)(2,1)S(1)} collective-permute-done((bf16[16,3712]{1,0:T(8,128)(2,1)S(1)}, bf16[16,3712]{1,0:T(8,128)(2,1)S(1)}, u32[]{:S(2)}, u32[]{:S(2)}) %collective-permute-start.4) | collective-permute-done | bytes 118816 | tf_op jit(solution)/shard_map/ppermute | solution.py:32
  21.0 1.7 %collective-permute-done.5 = bf16[16,3712]{1,0:T(8,128)(2,1)S(1)} collective-permute-done((bf16[16,3712]{1,0:T(8,128)(2,1)S(1)}, bf16[16,3712]{1,0:T(8,128)(2,1)S(1)}, u32[]{:S(2)}, u32[]{:S(2)}) %collective-permute-start.5) | collective-permute-done | bytes 118816 | tf_op jit(solution)/shard_map/ppermute | solution.py:32
  22.8 0.7 %pad_clamp_fusion.1 = s32[1024]{0:T(1024)S(1)} fusion(s32[32]{0:T(128)} %bitcast.59), kind=kLoop, calls=%fused_computation.52 | loop fusion | flops 1024 | bytes 4224 | tf_op jit(solution)/shard_map/gather | solution.py:75
  23.5 1.5 %gather_fusion = bf16[32,16,576]{2,1,0:T(8,128)(2,1)} fusion(bf16[32,16,576]{2,1,0:T(8,128)(2,1)S(1)} %bitcast.52, s32[1024]{0:T(1024)S(1)} %pad_clamp_fusion.1), kind=kCustom, calls=%fused_computation | custom fusion | bytes 1179776 | tf_op jit(solution)/shard_map/gather | solution.py:75
  24.9 3.6 %all-to-all-start = ((bf16[16,2,16,576]{3,2,1,0:T(8,128)(2,1)}), bf16[16,2,16,576]{3,2,1,0:T(8,128)(2,1)S(1)}, u32[]{:S(2)}, u32[]{:S(2)}) async-start(bf16[16,2,16,576]{3,2,1,0:T(8,128)(2,1)} %bitcast.3), calls=%async_computation | async-start | bytes 1310720 | tf_op jit(solution)/shard_map/all_to_all | solution.py:76
  28.7 2.7 %fusion.2 = f32[128,512]{1,0:T(8,128)S(1)} fusion(bf16[1,3584,512]{2,1,0:T(8,128)(2,1)} %param.22, bf16[64,3712]{1,0:T(8,128)(2,1)S(1)} %pad_maximum_fusion.1, bf16[64,3712]{1,0:T(8,128)(2,1)S(1)} %collective-permute-done.6), kind=kOutput, calls=%fused_computation.5 | convolution fusion | flops 471597056 | bytes 4882432 | tf_op jit(solution)/shard_map/dot_general | solution.py:115
  31.6 4.5 %fusion = bf16[128,3584]{1,0:T(8,128)(2,1)S(1)} fusion(bf16[1,512,3584]{2,1,0:T(8,128)(2,1)} %param.23, f32[128]{0:T(128)S(1)} %add_reduce_fusion, f32[128,512]{1,0:T(8,128)S(1)} %fusion.2, bf16[1,3584,512]{2,1,0:T(8,128)(2,1)} %param.21, bf16[64,3712]{1,0:T(8,128)(2,1)S(1)} %pad_maximum_fusion.1, bf16[64,3712]{1,0:T(8,128)(2,1)S(1)} %collective-permute-done.6), kind=kOutput, calls=%fused_computation.3 | convolution fusion | flops 942669824 | bytes 9470464 | tf_op jit(solution)/shard_map/dot_general | solution.py:117
  36.1 0.4 collective-permute-start.7
  36.6 1.4 %collective-permute-done.7 = bf16[64,3584]{1,0:T(8,128)(2,1)S(1)} collective-permute-done((bf16[64,3584]{1,0:T(8,128)(2,1)S(1)}, bf16[64,3584]{1,0:T(8,128)(2,1)S(1)}, u32[]{:S(2)}, u32[]{:S(2)}) %collective-permute-start.7) | collective-permute-done | bytes 458784 | tf_op jit(solution)/shard_map/ppermute | solution.py:32
  38.2 1.8 %collective-permute-start.10 = (bf16[16,3584]{1,0:T(8,128)(2,1)S(1)}, bf16[16,3584]{1,0:T(8,128)(2,1)S(1)}, u32[]{:S(2)}, u32[]{:S(2)}) collective-permute-start(bf16[16,3584]{1,0:T(8,128)(2,1)S(1)} %get-tuple-element.9), channel_id=1, source_target_pairs={{0,5},{1,4},{2,7},{3,6},{4,1},{5,0},{6,3},{7,2},{8,13},{9,12},{10,... | collective-permute-start | bytes 344072 | tf_op jit(solution)/shard_map/ppermute | solution.py:32
  40.0 1.5 %collective-permute-start.8 = (bf16[16,3584]{1,0:T(8,128)(2,1)S(1)}, bf16[16,3584]{1,0:T(8,128)(2,1)S(1)}, u32[]{:S(2)}, u32[]{:S(2)}) collective-permute-start(bf16[16,3584]{1,0:T(8,128)(2,1)S(1)} %get-tuple-element.8), channel_id=1, source_target_pairs={{0,1},{1,0},{2,3},{3,2},{4,5},{5,4},{6,7},{7,6},{8,9},{9,8},{10,11... | collective-permute-start | bytes 344072 | tf_op jit(solution)/shard_map/ppermute | solution.py:32
  41.5 0.3 collective-permute-start.9
  41.7 4.6 %all-to-all-done = bf16[16,2,16,576]{3,2,1,0:T(8,128)(2,1)S(1)} async-done(((bf16[16,2,16,576]{3,2,1,0:T(8,128)(2,1)}), bf16[16,2,16,576]{3,2,1,0:T(8,128)(2,1)S(1)}, u32[]{:S(2)}, u32[]{:S(2)}) %all-to-all-start) | async-done | bytes 589856 | tf_op jit(solution)/shard_map/all_to_all | solution.py:76
  46.3 0.7 %gather_fusion.1 = bf16[32,16,576]{2,1,0:T(8,128)(2,1)S(1)} fusion(bf16[32,16,576]{2,1,0:T(8,128)(2,1)S(1)} %bitcast.53, s32[1024]{0:T(1024)S(1)} %pad_clamp_fusion), kind=kCustom, calls=%fused_computation.1 | custom fusion | bytes 1179776 | tf_op jit(solution)/shard_map/gather | solution.py:131
  47.0 1.7 %fusion.40 = (f32[2,4,64]{2,1,0:T(4,128)S(1)}, f32[2,4,64,260]{3,2,1,0:T(8,128)S(1)}) fusion(bf16[1,2,4,64,576]{4,3,2,1,0:T(8,128)(2,1)} %param.17, bf16[2,4,576]{2,1,0:T(4,128)(2,1)S(1)} %bitcast.61, bf16[2,256,576]{2,1,0:T(8,128)(2,1)S(1)} %bitcast.54, pred[2,4,260]{2,1,0:T(4,128)(4,1)S(1)} %broadcast_or_fusion), kind=kOutput, calls=%fused_computation.66 | convolution fusion | flops 154951168 | bytes 1725472 | tf_op jit(solution)/shard_map/rshl,rkl->rshk/dot_general | solution.py:39
  48.7 0.3 fusion.10
  49.2 0.5 collective-permute-start.11
  49.7 2.4 %collective-permute-start.12 = (bf16[4,3584]{1,0:T(4,128)(2,1)S(1)}, bf16[4,3584]{1,0:T(4,128)(2,1)S(1)}, u32[]{:S(2)}, u32[]{:S(2)}) collective-permute-start(bf16[4,3584]{1,0:T(4,128)(2,1)S(1)} %get-tuple-element.13), channel_id=1, source_target_pairs={{0,16},{1,17},{2,18},{3,19},{4,20},{5,21},{6,22},{7,23},{8,24},{9,... | collective-permute-start | bytes 86024 | tf_op jit(solution)/shard_map/ppermute | solution.py:32
  52.1 1.5 %collective-permute-start.13 = (bf16[4,3584]{1,0:T(4,128)(2,1)S(1)}, bf16[4,3584]{1,0:T(4,128)(2,1)S(1)}, u32[]{:S(2)}, u32[]{:S(2)}) collective-permute-start(bf16[4,3584]{1,0:T(4,128)(2,1)S(1)} %get-tuple-element.12), channel_id=1, source_target_pairs={{0,24},{1,25},{2,26},{3,27},{4,28},{5,29},{6,30},{7,31},{8,16},{9,... | collective-permute-start | bytes 86024 | tf_op jit(solution)/shard_map/ppermute | solution.py:32
  53.6 1.3 %fusion.8 = bf16[1,2,4,64,512]{4,3,2,1,0:T(8,128)(2,1)} fusion(bf16[2,256,576]{2,1,0:T(8,128)(2,1)S(1)} %bitcast.55, bf16[2,4,576]{2,1,0:T(4,128)(2,1)S(1)} %bitcast.62, f32[2,4,64,260]{3,2,1,0:T(8,128)S(1)} %get-tuple-element.4, f32[2,4,64]{2,1,0:T(4,128)S(1)} %fusion.10, f32[2,4,64]{2,1,0:T(4,128)S(1)} %get-tuple-element.14), kind=kOutput, calls=%fused_computation.13 | convolution fusion | flops 138041344 | bytes 1659904 | tf_op jit(solution)/shard_map/rshk,rkv->rshv/dot_general | solution.py:51
  54.9 2.8 %collective-permute-done.13 = bf16[4,3584]{1,0:T(4,128)(2,1)S(1)} collective-permute-done((bf16[4,3584]{1,0:T(4,128)(2,1)S(1)}, bf16[4,3584]{1,0:T(4,128)(2,1)S(1)}, u32[]{:S(2)}, u32[]{:S(2)}) %collective-permute-start.13) | collective-permute-done | bytes 28704 | tf_op jit(solution)/shard_map/ppermute | solution.py:32
  57.7 0.6 %fusion.27 = bf16[1,4,3584]{2,1,0:T(4,128)(2,1)} fusion(bf16[4,3584]{1,0:T(4,128)(2,1)S(1)} %collective-permute-done.13, bf16[4,3584]{1,0:T(4,128)(2,1)S(1)} %collective-permute-done.12, bf16[4,3584]{1,0:T(4,128)(2,1)S(1)} %collective-permute-done.11, bf16[16,3584]{1,0:T(8,128)(2,1)S(1)} %add_convert_fusion.1), kind=kLoop, calls=%fused_computation.45 | loop fusion | flops 114688 | bytes 143360 | tf_op jit(solution)/shard_map/broadcast_in_dim | solution.py:133
  (35 shorter events, 1.0 us)
Async XLA Ops:
  0.6 22.8 %copy-start = (bf16[1,32,16,576]{3,2,1,0:T(8,128)(2,1)S(1)}, bf16[1,32,16,576]{3,2,1,0:T(8,128)(2,1)}, u32[]{:S(2)}) copy-start(bf16[1,32,16,576]{3,2,1,0:T(8,128)(2,1)} %param.12) | copy-start | bytes 1769476
  2.4 5.7 %collective-permute-start = (bf16[1,4,3712]{2,1,0:T(4,128)(2,1)S(1)}, bf16[1,4,3712]{2,1,0:T(4,128)(2,1)S(1)}, u32[]{:S(2)}, u32[]{:S(2)}) collective-permute-start(bf16[1,4,3712]{2,1,0:T(4,128)(2,1)S(1)} %maximum_bitcast_fusion), channel_id=1, source_target_pairs={{0,8},{1,9},{2,10},{3,11},{4,12},{5,13},{6,14},{7,15},{8,0},{9,1},... | collective-permute-start | bytes 89096 | tf_op jit(solution)/shard_map/ppermute | solution.py:32
  5.4 5.3 %collective-permute-start.1 = (bf16[1,4,3712]{2,1,0:T(4,128)(2,1)S(1)}, bf16[1,4,3712]{2,1,0:T(4,128)(2,1)S(1)}, u32[]{:S(2)}, u32[]{:S(2)}) collective-permute-start(bf16[1,4,3712]{2,1,0:T(4,128)(2,1)S(1)} %maximum_bitcast_fusion), channel_id=1, source_target_pairs={{0,16},{1,17},{2,18},{3,19},{4,20},{5,21},{6,22},{7,23},{8,24},{9,... | collective-permute-start | bytes 89096 | tf_op jit(solution)/shard_map/ppermute | solution.py:32
  8.0 5.7 %collective-permute-start.2 = (bf16[1,4,3712]{2,1,0:T(4,128)(2,1)S(1)}, bf16[1,4,3712]{2,1,0:T(4,128)(2,1)S(1)}, u32[]{:S(2)}, u32[]{:S(2)}) collective-permute-start(bf16[1,4,3712]{2,1,0:T(4,128)(2,1)S(1)} %maximum_bitcast_fusion), channel_id=1, source_target_pairs={{0,24},{1,25},{2,26},{3,27},{4,28},{5,29},{6,30},{7,31},{8,16},{9,... | collective-permute-start | bytes 89096 | tf_op jit(solution)/shard_map/ppermute | solution.py:32
  13.9 14.7 %copy-start.3 = (s32[1,2,16]{2,1,0:T(2,128)S(1)}, s32[1,2,16]{2,1,0:T(2,128)}, u32[]{:S(2)}) copy-start(s32[1,2,16]{2,1,0:T(2,128)} %param.14) | copy-start | bytes 388
  13.9 14.8 %copy-start.1 = (s32[1,2]{1,0:T(1,128)S(1)}, s32[1,2]{1,0:T(1,128)}, u32[]{:S(2)}) copy-start(s32[1,2]{1,0:T(1,128)} %param.15) | copy-start | bytes 28
  13.9 5.8 %collective-permute-start.3 = (bf16[16,3712]{1,0:T(8,128)(2,1)S(1)}, bf16[16,3712]{1,0:T(8,128)(2,1)S(1)}, u32[]{:S(2)}, u32[]{:S(2)}) collective-permute-start(bf16[16,3712]{1,0:T(8,128)(2,1)S(1)} %reshape.88), channel_id=1, source_target_pairs={{0,1},{1,0},{2,3},{3,2},{4,5},{5,4},{6,7},{7,6},{8,9},{9,8},{10,11... | collective-permute-start | bytes 356360 | tf_op jit(solution)/shard_map/ppermute | solution.py:32
  15.4 5.5 %collective-permute-start.4 = (bf16[16,3712]{1,0:T(8,128)(2,1)S(1)}, bf16[16,3712]{1,0:T(8,128)(2,1)S(1)}, u32[]{:S(2)}, u32[]{:S(2)}) collective-permute-start(bf16[16,3712]{1,0:T(8,128)(2,1)S(1)} %reshape.88), channel_id=1, source_target_pairs={{0,4},{1,5},{2,6},{3,7},{4,0},{5,1},{6,2},{7,3},{8,12},{9,13},{10,... | collective-permute-start | bytes 356360 | tf_op jit(solution)/shard_map/ppermute | solution.py:32
  17.0 5.7 %collective-permute-start.5 = (bf16[16,3712]{1,0:T(8,128)(2,1)S(1)}, bf16[16,3712]{1,0:T(8,128)(2,1)S(1)}, u32[]{:S(2)}, u32[]{:S(2)}) collective-permute-start(bf16[16,3712]{1,0:T(8,128)(2,1)S(1)} %reshape.88), channel_id=1, source_target_pairs={{0,5},{1,4},{2,7},{3,6},{4,1},{5,0},{6,3},{7,2},{8,13},{9,12},{10,... | collective-permute-start | bytes 356360 | tf_op jit(solution)/shard_map/ppermute | solution.py:32
  22.7 6.0 %collective-permute-start.6 = (bf16[64,3712]{1,0:T(8,128)(2,1)S(1)}, bf16[64,3712]{1,0:T(8,128)(2,1)S(1)}, u32[]{:S(2)}, u32[]{:S(2)}) collective-permute-start(bf16[64,3712]{1,0:T(8,128)(2,1)S(1)} %pad_maximum_fusion.1), channel_id=1, source_target_pairs={{0,2},{1,3},{2,0},{3,1},{4,6},{5,7},{6,4},{7,5},{8,10},{9,11},{10,... | collective-permute-start | bytes 1425416 | tf_op jit(solution)/shard_map/ppermute | solution.py:32
  24.9 21.3 %all-to-all-start = ((bf16[16,2,16,576]{3,2,1,0:T(8,128)(2,1)}), bf16[16,2,16,576]{3,2,1,0:T(8,128)(2,1)S(1)}, u32[]{:S(2)}, u32[]{:S(2)}) async-start(bf16[16,2,16,576]{3,2,1,0:T(8,128)(2,1)} %bitcast.3), calls=%async_computation | async-start | bytes 1310720 | tf_op jit(solution)/shard_map/all_to_all | solution.py:76
  36.1 10.8 %copy-start.2 = (bf16[1,2,4,576]{3,2,1,0:T(4,128)(2,1)S(1)}, bf16[1,2,4,576]{3,2,1,0:T(4,128)(2,1)}, u32[]{:S(2)}) copy-start(bf16[1,2,4,576]{3,2,1,0:T(4,128)(2,1)} %param.16) | copy-start | bytes 27652
  36.1 1.9 %collective-permute-start.7 = (bf16[64,3584]{1,0:T(8,128)(2,1)S(1)}, bf16[64,3584]{1,0:T(8,128)(2,1)S(1)}, u32[]{:S(2)}, u32[]{:S(2)}) collective-permute-start(bf16[64,3584]{1,0:T(8,128)(2,1)S(1)} %slice.57), channel_id=1, source_target_pairs={{0,2},{1,3},{2,0},{3,1},{4,6},{5,7},{6,4},{7,5},{8,10},{9,11},{10,... | collective-permute-start | bytes 1376264 | tf_op jit(solution)/shard_map/ppermute | solution.py:32
  38.2 10.9 %collective-permute-start.10 = (bf16[16,3584]{1,0:T(8,128)(2,1)S(1)}, bf16[16,3584]{1,0:T(8,128)(2,1)S(1)}, u32[]{:S(2)}, u32[]{:S(2)}) collective-permute-start(bf16[16,3584]{1,0:T(8,128)(2,1)S(1)} %get-tuple-element.9), channel_id=1, source_target_pairs={{0,5},{1,4},{2,7},{3,6},{4,1},{5,0},{6,3},{7,2},{8,13},{9,12},{10,... | collective-permute-start | bytes 344072 | tf_op jit(solution)/shard_map/ppermute | solution.py:32
  40.0 9.0 %collective-permute-start.8 = (bf16[16,3584]{1,0:T(8,128)(2,1)S(1)}, bf16[16,3584]{1,0:T(8,128)(2,1)S(1)}, u32[]{:S(2)}, u32[]{:S(2)}) collective-permute-start(bf16[16,3584]{1,0:T(8,128)(2,1)S(1)} %get-tuple-element.8), channel_id=1, source_target_pairs={{0,1},{1,0},{2,3},{3,2},{4,5},{5,4},{6,7},{7,6},{8,9},{9,8},{10,11... | collective-permute-start | bytes 344072 | tf_op jit(solution)/shard_map/ppermute | solution.py:32
  41.5 7.6 %collective-permute-start.9 = (bf16[16,3584]{1,0:T(8,128)(2,1)S(1)}, bf16[16,3584]{1,0:T(8,128)(2,1)S(1)}, u32[]{:S(2)}, u32[]{:S(2)}) collective-permute-start(bf16[16,3584]{1,0:T(8,128)(2,1)S(1)} %get-tuple-element.10), channel_id=1, source_target_pairs={{0,4},{1,5},{2,6},{3,7},{4,0},{5,1},{6,2},{7,3},{8,12},{9,13},{10,... | collective-permute-start | bytes 344072 | tf_op jit(solution)/shard_map/ppermute | solution.py:32
  49.2 5.7 %collective-permute-start.11 = (bf16[4,3584]{1,0:T(4,128)(2,1)S(1)}, bf16[4,3584]{1,0:T(4,128)(2,1)S(1)}, u32[]{:S(2)}, u32[]{:S(2)}) collective-permute-start(bf16[4,3584]{1,0:T(4,128)(2,1)S(1)} %get-tuple-element.11), channel_id=1, source_target_pairs={{0,8},{1,9},{2,10},{3,11},{4,12},{5,13},{6,14},{7,15},{8,0},{9,1},... | collective-permute-start | bytes 86024 | tf_op jit(solution)/shard_map/ppermute | solution.py:32
  49.7 5.2 %collective-permute-start.12 = (bf16[4,3584]{1,0:T(4,128)(2,1)S(1)}, bf16[4,3584]{1,0:T(4,128)(2,1)S(1)}, u32[]{:S(2)}, u32[]{:S(2)}) collective-permute-start(bf16[4,3584]{1,0:T(4,128)(2,1)S(1)} %get-tuple-element.13), channel_id=1, source_target_pairs={{0,16},{1,17},{2,18},{3,19},{4,20},{5,21},{6,22},{7,23},{8,24},{9,... | collective-permute-start | bytes 86024 | tf_op jit(solution)/shard_map/ppermute | solution.py:32
  52.1 5.7 %collective-permute-start.13 = (bf16[4,3584]{1,0:T(4,128)(2,1)S(1)}, bf16[4,3584]{1,0:T(4,128)(2,1)S(1)}, u32[]{:S(2)}, u32[]{:S(2)}) collective-permute-start(bf16[4,3584]{1,0:T(4,128)(2,1)S(1)} %get-tuple-element.12), channel_id=1, source_target_pairs={{0,24},{1,25},{2,26},{3,27},{4,28},{5,29},{6,30},{7,31},{8,16},{9,... | collective-permute-start | bytes 86024 | tf_op jit(solution)/shard_map/ppermute | solution.py:32
